TPU v7x, 32 devices: a whole 2x2x4 slice. The times are simulated.
32 devices in a mesh: dp: 16 (over z, y, x), tp: 2 (over core).
Axes of the slice: x: 2, y: 2, z: 4, core: 2. Of those that a mesh axis runs over, the one named last changes fastest.
Arguments:
- inputs: bfloat16 [16384, 768], P('dp'), may hold values from -6 to 6
- cotangent: bfloat16 [16384, 768], P(('dp', 'tp')), may hold values from -6 to 6
- seq_lengths: int32 [16, 2], P('dp'), may hold values from 0 to 1024, as said below
- timesteps: int32 [16, 2], P('dp'), may hold values from 0 to 1999
- time_w1: float32 [128, 768], P(None, ('dp', 'tp')), may hold values from -0.5 to 0.5
- time_b1: float32 [768], P(('dp', 'tp')), may hold values from -3 to 3
- time_w2: float32 [768, 768], P(('dp', 'tp')), may hold values from -0.21875 to 0.21875
- time_b2: float32 [768], P(('dp', 'tp')), may hold values from -3 to 3
- w_query: float32 [768, 768], P('dp', 'tp'), may hold values from -0.21875 to 0.21875
- b_query: float32 [768], P('tp'), may hold values from -3 to 3
- w_key: float32 [768, 768], P('dp', 'tp'), may hold values from -0.21875 to 0.21875
- w_value: float32 [768, 768], P('dp', 'tp'), may hold values from -0.21875 to 0.21875
- b_value: float32 [768], P('tp'), may hold values from -3 to 3
- w_out: float32 [768, 768], P('tp', 'dp'), may hold values from -2.5 to 2.5
- b_out: float32 [768], P(('dp', 'tp')), may hold values from -3 to 3
- norm1_gain: float32 [768], P(('dp', 'tp')), may hold values from 0.5 to 1.5
- norm1_bias: float32 [768], P(('dp', 'tp')), may hold values from -3 to 3
- w_up: float32 [768, 3072], P('dp', 'tp'), may hold values from -0.21875 to 0.21875
- b_up: float32 [3072], P('tp'), may hold values from -3 to 3
- w_down: float32 [3072, 768], P('tp', 'dp'), may hold values from -0.109375 to 0.109375
- b_down: float32 [768], P(('dp', 'tp')), may hold values from -3 to 3
- norm2_gain: float32 [768], P(('dp', 'tp')), may hold values from 0.5 to 1.5
- norm2_bias: float32 [768], P(('dp', 'tp')), may hold values from -3 to 3
Outputs:
- outputs: bfloat16 [16384, 768], P(('dp', 'tp'))
- input_grad: float32 [16384, 768], P('dp')
- grad_time_w1: float32 [128, 768], P(None, ('dp', 'tp'))
- grad_time_b1: float32 [768], P(('dp', 'tp'))
- grad_time_w2: float32 [768, 768], P(('dp', 'tp'))
- grad_time_b2: float32 [768], P(('dp', 'tp'))
- grad_w_query: float32 [768, 768], P('dp', 'tp')
- grad_b_query: float32 [768], P('tp')
- grad_w_key: float32 [768, 768], P('dp', 'tp')
- grad_w_value: float32 [768, 768], P('dp', 'tp')
- grad_b_value: float32 [768], P('tp')
- grad_w_out: float32 [768, 768], P('tp', 'dp')
- grad_b_out: float32 [768], P(('dp', 'tp'))
- grad_norm1_gain: float32 [768], P(('dp', 'tp'))
- grad_norm1_bias: float32 [768], P(('dp', 'tp'))
- grad_w_up: float32 [768, 3072], P('dp', 'tp')
- grad_b_up: float32 [3072], P('tp')
- grad_w_down: float32 [3072, 768], P('tp', 'dp')
- grad_b_down: float32 [768], P(('dp', 'tp'))
- grad_norm2_gain: float32 [768], P(('dp', 'tp'))
- grad_norm2_bias: float32 [768], P(('dp', 'tp'))
Inputs may be any that keep to these rules, and one draw needn't show every extreme that they name: Group g's first sequence fills rows 0 to seq_lengths[g,0] - 1 and its second the next seq_lengths[g,1] rows; the remaining rows of the group are padding. Either the second length is 0 and the first exceeds 1024 / 2, or both lie between 256 and 512 with a sum over 512. Some group holds one sequence of exactly 1024.
All inputs are finite; a program needn't handle non-finite values.
Results may differ from a plain program's by a relative error of at most 0.025.
The roundings to bfloat16 on the way count: a program that leaves them out, or rounds other values in their place, can miss the bound.
Values may be sent and summed in bfloat16 or wider, within the bound.
A program may use at most 128 MiB of HBM per device.

v0:
```python
import math

import jax
import jax.numpy as jnp
from jax import lax
from jax.sharding import PartitionSpec as P

HD = 64
TE = 128


epsilon = 1e-05
highest = lax.Precision.HIGHEST


def time_features(time_steps, feature_width):
    half_width = feature_width // 2
    frequency = jnp.exp(-math.log(10000.0) * jnp.arange(half_width, dtype=jnp.float32) / half_width)
    angles = time_steps.astype(jnp.float32)[:, None] * frequency[None, :]
    return jnp.concatenate([jnp.cos(angles), jnp.sin(angles)], axis=1)


def segment_ids(lengths, row_count):
    row_index = jnp.arange(row_count, dtype=jnp.int32)
    inner = jnp.where(row_index < lengths[0] + lengths[1], 1, 2)
    return jnp.where(row_index < lengths[0], 0, inner).astype(jnp.int32)


def contract_rows(left_side, right_side, precision_mode=None):
    return lax.dot_general(
        left_side,
        right_side,
        (((0,), (0,)), ((), ())),
        precision=precision_mode,
        preferred_element_type=jnp.float32,
    )


def contract_cols(left_side, right_side, precision_mode=None):
    return lax.dot_general(
        left_side,
        right_side,
        (((1,), (1,)), ((), ())),
        precision=precision_mode,
        preferred_element_type=jnp.float32,
    )


def norm_forward(summed, gain_row, shift_row):
    centered = summed - jnp.mean(summed, axis=-1, keepdims=True)
    inv_std = lax.rsqrt(jnp.mean(centered * centered, axis=-1, keepdims=True) + epsilon)
    normed = centered * inv_std
    return (normed * gain_row + shift_row, normed, inv_std)


def norm_backward(grad_rows, normed, inv_std, gain_row):
    scaled = grad_rows * gain_row
    inner = (
        scaled
        - jnp.mean(scaled, axis=-1, keepdims=True)
        - normed * jnp.mean(scaled * normed, axis=-1, keepdims=True)
    )
    return (inner * inv_std, jnp.sum(grad_rows * normed, axis=0), jnp.sum(grad_rows, axis=0))


def block_scores(query_blk, key_heads, seg_blk, segment, factor):
    raw_scores = (
        jnp.einsum("qhd,khd->hqk", query_blk, key_heads, preferred_element_type=jnp.float32)
        * factor
    )
    allowed = seg_blk[:, None] == segment[None, :]
    return jnp.where(allowed[None], raw_scores, -1e30)


def attention_forward(query_rows, key_rows, value_rows, segment, block_rows):
    rows_total = query_rows.shape[0]
    head_count = query_rows.shape[1] // HD
    factor = 1.0 / math.sqrt(HD)
    key_heads = key_rows.reshape(rows_total, head_count, HD)
    value_heads = value_rows.reshape(rows_total, head_count, HD)
    query_blocks = query_rows.reshape(rows_total // block_rows, block_rows, head_count, HD)
    seg_blocks = segment.reshape(rows_total // block_rows, block_rows)

    def one_block(item):
        query_blk, seg_blk = item
        scores = block_scores(query_blk, key_heads, seg_blk, segment, factor)
        row_max = jnp.max(scores, axis=-1, keepdims=True)
        exp_scores = jnp.exp(scores - row_max)
        row_total = jnp.sum(exp_scores, axis=-1, keepdims=True)
        prob_low = (exp_scores / row_total).astype(jnp.bfloat16)
        mixed_blk = jnp.einsum(
            "hqk,khd->qhd", prob_low, value_heads, preferred_element_type=jnp.float32
        )
        log_total = (row_max + jnp.log(row_total))[..., 0]
        return (mixed_blk.reshape(block_rows, head_count * HD).astype(jnp.bfloat16), log_total)

    mixed_blocks, log_totals = lax.map(one_block, (query_blocks, seg_blocks))
    return (mixed_blocks.reshape(rows_total, head_count * HD), log_totals)


def attention_backward(
    query_rows, key_rows, value_rows, grad_mixed, log_totals, segment, block_rows
):
    rows_total = query_rows.shape[0]
    head_count = query_rows.shape[1] // HD
    factor = 1.0 / math.sqrt(HD)
    block_count = rows_total // block_rows
    key_heads = key_rows.reshape(rows_total, head_count, HD)
    value_heads = value_rows.reshape(rows_total, head_count, HD)
    query_blocks = query_rows.reshape(block_count, block_rows, head_count, HD)
    grad_blocks = grad_mixed.reshape(block_count, block_rows, head_count, HD)
    seg_blocks = segment.reshape(block_count, block_rows)

    def one_block(carry, item):
        grad_key_acc, grad_value_acc = carry
        query_blk, grad_blk, seg_blk, log_blk = item
        scores = block_scores(query_blk, key_heads, seg_blk, segment, factor)
        probs_full = jnp.exp(scores - log_blk[..., None])
        prob_low = probs_full.astype(jnp.bfloat16)
        grad_value_acc = grad_value_acc + jnp.einsum(
            "hqk,qhd->khd", prob_low, grad_blk, preferred_element_type=jnp.float32
        )
        grad_probs = jnp.einsum(
            "qhd,khd->hqk", grad_blk, value_heads, preferred_element_type=jnp.float32
        )
        row_inner = jnp.sum(grad_probs * probs_full, axis=-1, keepdims=True)
        grad_scores = (probs_full * (grad_probs - row_inner)).astype(jnp.bfloat16)
        grad_query_blk = (
            jnp.einsum("hqk,khd->qhd", grad_scores, key_heads, preferred_element_type=jnp.float32)
            * factor
        )
        grad_key_acc = (
            grad_key_acc
            + jnp.einsum("hqk,qhd->khd", grad_scores, query_blk, preferred_element_type=jnp.float32)
            * factor
        )
        return ((grad_key_acc, grad_value_acc), grad_query_blk.reshape(block_rows, head_count * HD))

    zeros_heads = jnp.zeros((rows_total, head_count, HD), jnp.float32)
    (grad_key_acc, grad_value_acc), grad_query_blocks = lax.scan(
        one_block, (zeros_heads, zeros_heads), (query_blocks, grad_blocks, seg_blocks, log_totals)
    )
    return (
        grad_query_blocks.reshape(rows_total, head_count * HD),
        grad_key_acc.reshape(rows_total, head_count * HD),
        grad_value_acc.reshape(rows_total, head_count * HD),
    )


def on_device(
    inputs,
    cotangent,
    seq_lengths,
    timesteps,
    time_w1,
    time_b1,
    time_w2,
    time_b2,
    w_query,
    b_query,
    w_key,
    w_value,
    b_value,
    w_out,
    b_out,
    norm1_gain,
    norm1_bias,
    w_up,
    b_up,
    w_down,
    b_down,
    norm2_gain,
    norm2_bias,
):
    bf_type = jnp.bfloat16
    seq_rows = inputs.shape[0]
    own_rows = seq_rows // lax.axis_size("tp")
    row_start = lax.axis_index("tp") * own_rows
    block_rows = min(512, seq_rows)
    head_width = w_query.shape[1]
    gathered_fwd = (
        lax.all_gather(w_query.astype(bf_type), "dp", axis=0, tiled=True),
        lax.all_gather(w_key.astype(bf_type), "dp", axis=0, tiled=True),
        lax.all_gather(w_value.astype(bf_type), "dp", axis=0, tiled=True),
        lax.all_gather(w_up.astype(bf_type), "dp", axis=0, tiled=True),
        lax.all_gather(w_out.astype(bf_type), "dp", axis=1, tiled=True),
        lax.all_gather(w_down.astype(bf_type), "dp", axis=1, tiled=True),
    )
    wq_full, wk_full, wv_full, wup_full, wout_full, wdown_full = gathered_fwd
    (
        tw1_full,
        tb1_full,
        tw2_full,
        tb2_full,
        bout_full,
        gain_one,
        shift_one,
        bdown_full,
        gain_two,
        shift_two,
    ) = (
        lax.all_gather(time_w1, ("dp", "tp"), axis=1, tiled=True),
        lax.all_gather(time_b1, ("dp", "tp"), axis=0, tiled=True),
        lax.all_gather(time_w2, ("dp", "tp"), axis=0, tiled=True),
        lax.all_gather(time_b2, ("dp", "tp"), axis=0, tiled=True),
        lax.all_gather(b_out, ("dp", "tp"), axis=0, tiled=True),
        lax.all_gather(norm1_gain, ("dp", "tp"), axis=0, tiled=True),
        lax.all_gather(norm1_bias, ("dp", "tp"), axis=0, tiled=True),
        lax.all_gather(b_down, ("dp", "tp"), axis=0, tiled=True),
        lax.all_gather(norm2_gain, ("dp", "tp"), axis=0, tiled=True),
        lax.all_gather(norm2_bias, ("dp", "tp"), axis=0, tiled=True),
    )
    lengths = seq_lengths[0]
    segment = segment_ids(lengths, seq_rows)
    features = time_features(timesteps[0], TE).astype(bf_type)
    tw2_low = tw2_full.astype(bf_type)
    time_pre = (
        jnp.dot(features, tw1_full.astype(bf_type), preferred_element_type=jnp.float32) + tb1_full
    )
    silu_value, silu_pull = jax.vjp(jax.nn.silu, time_pre)
    time_hidden = silu_value.astype(bf_type)
    time_embed = jnp.dot(time_hidden, tw2_low, preferred_element_type=jnp.float32) + tb2_full
    inner_embed = jnp.where((segment == 1)[:, None], time_embed[1][None, :], 0.0)
    added = jnp.where((segment == 0)[:, None], time_embed[0][None, :], inner_embed)
    base_rows = inputs.astype(jnp.float32) + added
    base_low = base_rows.astype(bf_type)
    qkv_weight = jnp.concatenate([wq_full, wk_full, wv_full], axis=1)
    projected = jnp.dot(base_low, qkv_weight, preferred_element_type=jnp.float32)
    query_rows = (projected[:, :head_width] + b_query).astype(bf_type)
    key_rows = projected[:, head_width : 2 * head_width].astype(bf_type)
    value_rows = (projected[:, 2 * head_width :] + b_value).astype(bf_type)
    mixed_low, log_totals = attention_forward(query_rows, key_rows, value_rows, segment, block_rows)
    rows_in = mixed_low
    attn_own = (
        lax.psum_scatter(
            jnp.dot(rows_in, wout_full, preferred_element_type=jnp.float32).astype(jnp.bfloat16),
            "tp",
            scatter_dimension=0,
            tiled=True,
        ).astype(jnp.float32)
        + bout_full
    )
    base_own = lax.dynamic_slice_in_dim(base_rows, row_start, own_rows, 0)
    first_out, normed_one, inv_one = norm_forward(base_own + attn_own, gain_one, shift_one)
    first_all = lax.all_gather(first_out.astype(bf_type), "tp", axis=0, tiled=True)
    up_pre = jnp.dot(first_all, wup_full, preferred_element_type=jnp.float32) + b_up
    gelu_value, gelu_pull = jax.vjp(jax.nn.gelu, up_pre)
    up_act = gelu_value.astype(bf_type)
    rows_in = up_act
    ffn_own = (
        lax.psum_scatter(
            jnp.dot(rows_in, wdown_full, preferred_element_type=jnp.float32).astype(jnp.bfloat16),
            "tp",
            scatter_dimension=0,
            tiled=True,
        ).astype(jnp.float32)
        + bdown_full
    )
    outputs_own, normed_two, inv_two = norm_forward(first_out + ffn_own, gain_two, shift_two)
    seg_own = lax.dynamic_slice_in_dim(segment, row_start, own_rows, 0)
    valid_own = (seg_own < 2).astype(jnp.float32)
    grad_y = cotangent.astype(jnp.float32) * valid_own[:, None]
    grad_second, grad_gain_two, grad_shift_two = norm_backward(
        grad_y, normed_two, inv_two, gain_two
    )
    grad_b_down = jnp.sum(grad_second, axis=0)
    gathered_back = (
        lax.all_gather(w_query.astype(bf_type), "dp", axis=0, tiled=True),
        lax.all_gather(w_key.astype(bf_type), "dp", axis=0, tiled=True),
        lax.all_gather(w_value.astype(bf_type), "dp", axis=0, tiled=True),
        lax.all_gather(w_up.astype(bf_type), "dp", axis=0, tiled=True),
        lax.all_gather(w_out.astype(bf_type), "dp", axis=1, tiled=True),
        lax.all_gather(w_down.astype(bf_type), "dp", axis=1, tiled=True),
    )
    wq_back, wk_back, wv_back, wup_back, wout_back, wdown_back = gathered_back
    grad_down_all = lax.all_gather(grad_second.astype(bf_type), "tp", axis=0, tiled=True)
    grad_w_down = contract_rows(up_act, grad_down_all)
    grad_act = contract_cols(grad_down_all, wdown_back)
    grad_up_pre = gelu_pull(grad_act)[0]
    grad_b_up = jnp.sum(grad_up_pre, axis=0)
    grad_up_low = grad_up_pre.astype(bf_type)
    grad_w_up = contract_rows(first_all, grad_up_low)
    rows_in = grad_up_low
    grad_first = grad_second + lax.psum_scatter(
        contract_cols(rows_in, wup_back).astype(jnp.bfloat16), "tp", scatter_dimension=0, tiled=True
    ).astype(jnp.float32)
    grad_r1, grad_gain_one, grad_shift_one = norm_backward(
        grad_first, normed_one, inv_one, gain_one
    )
    grad_b_out = jnp.sum(grad_r1, axis=0)
    grad_attn_all = lax.all_gather(grad_r1.astype(bf_type), "tp", axis=0, tiled=True)
    grad_w_out = contract_rows(mixed_low, grad_attn_all)
    grad_mixed = contract_cols(grad_attn_all, wout_back).astype(bf_type)
    grad_query, grad_keys, grad_values = attention_backward(
        query_rows, key_rows, value_rows, grad_mixed, log_totals, segment, block_rows
    )
    grad_qkv = jnp.concatenate(
        [grad_query.astype(bf_type), grad_keys.astype(bf_type), grad_values.astype(bf_type)], axis=1
    )
    grad_qkv_sums = jnp.sum(grad_qkv.astype(jnp.float32), axis=0)
    grad_b_query = grad_qkv_sums[:head_width]
    grad_b_value = grad_qkv_sums[2 * head_width :]
    grad_qkv_w = contract_rows(base_low, grad_qkv)
    qkv_back = jnp.concatenate([wq_back, wk_back, wv_back], axis=1)
    input_term = contract_cols(grad_qkv, qkv_back)
    own_part = lax.dynamic_slice_in_dim(input_term, row_start, own_rows, 0) + grad_r1
    input_term = lax.dynamic_update_slice_in_dim(input_term, own_part, row_start, 0)
    grad_inputs = lax.psum(input_term.astype(jnp.bfloat16), "tp").astype(jnp.float32)
    grad_own = lax.dynamic_slice_in_dim(grad_inputs, row_start, own_rows, 0)
    picker_own = (seg_own[:, None] == jnp.arange(2, dtype=jnp.int32)[None, :]).astype(jnp.float32)
    grad_embed = contract_rows(picker_own, grad_own, highest)
    grad_tb2 = jnp.sum(grad_embed, axis=0)
    grad_tw2 = contract_rows(time_hidden.astype(jnp.float32), grad_embed, highest)
    tw2_back = lax.optimization_barrier(tw2_low).astype(jnp.float32)
    grad_hidden = contract_cols(grad_embed, tw2_back, highest)
    grad_time_pre = silu_pull(grad_hidden)[0]
    grad_tb1 = jnp.sum(grad_time_pre, axis=0)
    grad_tw1 = contract_rows(features.astype(jnp.float32), grad_time_pre, highest)
    red_wq, red_wk, red_wv, red_wup, red_wout, red_wdown = (
        lax.psum_scatter(grad_qkv_w[:, :head_width], "dp", scatter_dimension=0, tiled=True),
        lax.psum_scatter(
            grad_qkv_w[:, head_width : 2 * head_width], "dp", scatter_dimension=0, tiled=True
        ),
        lax.psum_scatter(grad_qkv_w[:, 2 * head_width :], "dp", scatter_dimension=0, tiled=True),
        lax.psum_scatter(grad_w_up, "dp", scatter_dimension=0, tiled=True),
        lax.psum_scatter(grad_w_out, "dp", scatter_dimension=1, tiled=True),
        lax.psum_scatter(grad_w_down, "dp", scatter_dimension=1, tiled=True),
    )
    (
        red_tw1,
        red_tb1,
        red_tw2,
        red_tb2,
        red_bout,
        red_gain_one,
        red_shift_one,
        red_bdown,
        red_gain_two,
        red_shift_two,
    ) = (
        lax.psum_scatter(grad_tw1, ("dp", "tp"), scatter_dimension=1, tiled=True),
        lax.psum_scatter(grad_tb1, ("dp", "tp"), scatter_dimension=0, tiled=True),
        lax.psum_scatter(grad_tw2, ("dp", "tp"), scatter_dimension=0, tiled=True),
        lax.psum_scatter(grad_tb2, ("dp", "tp"), scatter_dimension=0, tiled=True),
        lax.psum_scatter(grad_b_out, ("dp", "tp"), scatter_dimension=0, tiled=True),
        lax.psum_scatter(grad_gain_one, ("dp", "tp"), scatter_dimension=0, tiled=True),
        lax.psum_scatter(grad_shift_one, ("dp", "tp"), scatter_dimension=0, tiled=True),
        lax.psum_scatter(grad_b_down, ("dp", "tp"), scatter_dimension=0, tiled=True),
        lax.psum_scatter(grad_gain_two, ("dp", "tp"), scatter_dimension=0, tiled=True),
        lax.psum_scatter(grad_shift_two, ("dp", "tp"), scatter_dimension=0, tiled=True),
    )
    red_bq, red_bv, red_bup = lax.psum((grad_b_query, grad_b_value, grad_b_up), "dp")
    return (
        outputs_own.astype(bf_type),
        grad_inputs,
        red_tw1,
        red_tb1,
        red_tw2,
        red_tb2,
        red_wq,
        red_bq,
        red_wk,
        red_wv,
        red_bv,
        red_wout,
        red_bout,
        red_gain_one,
        red_shift_one,
        red_wup,
        red_bup,
        red_wdown,
        red_bdown,
        red_gain_two,
        red_shift_two,
    )


def solution(mesh):
    placed = (
        P("dp", None),
        P(("dp", "tp"), None),
        P("dp", None),
        P("dp", None),
        P(None, ("dp", "tp")),
        P(("dp", "tp")),
        P(("dp", "tp"), None),
        P(("dp", "tp")),
        P("dp", "tp"),
        P("tp"),
        P("dp", "tp"),
        P("dp", "tp"),
        P("tp"),
        P("tp", "dp"),
        P(("dp", "tp")),
        P(("dp", "tp")),
        P(("dp", "tp")),
        P("dp", "tp"),
        P("tp"),
        P("tp", "dp"),
        P(("dp", "tp")),
        P(("dp", "tp")),
        P(("dp", "tp")),
    )
    return jax.shard_map(
        on_device,
        mesh=mesh,
        in_specs=placed,
        out_specs=(
            P(("dp", "tp"), None),
            P("dp", None),
            P(None, ("dp", "tp")),
            P(("dp", "tp")),
            P(("dp", "tp"), None),
            P(("dp", "tp")),
            P("dp", "tp"),
            P("tp"),
            P("dp", "tp"),
            P("dp", "tp"),
            P("tp"),
            P("tp", "dp"),
            P(("dp", "tp")),
            P(("dp", "tp")),
            P(("dp", "tp")),
            P("dp", "tp"),
            P("tp"),
            P("tp", "dp"),
            P(("dp", "tp")),
            P(("dp", "tp")),
            P(("dp", "tp")),
        ),
        check_vma=False,
    )
```

profile of v0, /device:TPU:0, one launch (start us, length us, event | category | flops | bytes accessed | tf_op | source)
XLA Modules:
  0.0 1630.1 jit_solution(4557967913669338525)
XLA Ops:
  13.7 43.9 %all_gather.63 = bf16[128,768]{0,1:T(8,128)(2,1)S(1)} all-gather(bf16[128,24]{0,1:T(8,128)(2,1)S(1)} %convert.21), channel_id=1, replica_groups=mesh['dp'=16,'tp'=2] {'dp','tp'}, dimensions={1}, use_global_device_ids=true | all-gather | bytes 202752 | tf_op jit(solution)/shard_map/all_gather | solution.py:202
  66.9 37.7 %all-reduce.18 = (f32[768]{0:T(1024)S(1)}, f32[768]{0:T(1024)S(1)}, f32[768]{0:T(1024)S(1)}, f32[768]{0:T(1024)S(1)}, f32[768]{0:T(1024)S(1)}, /*index=5*/f32[768]{0:T(1024)}, f32[768]{0:T(1024)}) all-reduce(f32[768]{0:T(1024)S(1)} %dynamic-update-slice.1, f32[768]{0:T(1024)S(1)} %dynamic-update-slice, ...), channel_id=1, replica_groups=mesh['dp'=16,'tp'=2] {'dp','tp'}, use_global_device_ids=true, to_apply=%add.1 | all-reduce | flops 5376 | bytes 43008
  105.3 42.1 %all_gather.67 = bf16[768,384]{1,0:T(8,128)(2,1)S(1)} all-gather(bf16[48,384]{1,0:T(8,128)(2,1)S(1)} %convert_element_type.165), channel_id=1, replica_groups=mesh['dp'=16,'tp'=2] {'dp'}, dimensions={0}, use_global_device_ids=true | all-gather | bytes 626688 | tf_op jit(solution)/shard_map/all_gather | solution.py:182
  147.5 38.7 %all_gather.68 = bf16[768,384]{1,0:T(8,128)(2,1)S(1)} all-gather(bf16[48,384]{1,0:T(8,128)(2,1)S(1)} %convert_element_type.166), channel_id=1, replica_groups=mesh['dp'=16,'tp'=2] {'dp'}, dimensions={0}, use_global_device_ids=true | all-gather | bytes 626688 | tf_op jit(solution)/shard_map/all_gather | solution.py:183
  186.3 41.0 %all_gather.69 = bf16[768,384]{1,0:T(8,128)(2,1)S(1)} all-gather(bf16[48,384]{1,0:T(8,128)(2,1)S(1)} %convert_element_type.167), channel_id=1, replica_groups=mesh['dp'=16,'tp'=2] {'dp'}, dimensions={0}, use_global_device_ids=true | all-gather | bytes 626688 | tf_op jit(solution)/shard_map/all_gather | solution.py:184
  228.6 41.7 %all_gather.70 = bf16[384,768]{0,1:T(8,128)(2,1)} all-gather(bf16[384,48]{0,1:T(8,128)(2,1)S(1)} %convert_element_type.170), channel_id=1, replica_groups=mesh['dp'=16,'tp'=2] {'dp'}, dimensions={1}, use_global_device_ids=true | all-gather | bytes 626688 | tf_op jit(solution)/shard_map/all_gather | solution.py:186
  281.9 24.9 %while.28 = (s32[]{:T(128)}, bf16[2,512,384]{2,1,0:T(8,128)(2,1)}, f32[2,6,512]{2,1,0:T(8,128)S(1)}, s32[2,512]{1,0:T(2,128)S(1)}, bf16[2,512,6,64]{1,3,2,0:T(8,...) while((s32[]{:T(128)}, bf16[2,512,384]{2,1,0:T(8,128)(2,1)}, ...), condition=%wide.region_3.4_spmd.clone, body=%wide.region_0.3_spmd.clone.sunk | while | flops 843777024 | bytes 43903108 | solution.py:97
  321.8 52.8 %all-gather.11.cloned.1.call-done = bf16[768,1536]{1,0:T(8,128)(2,1)} async-done(((bf16[48,1536]{1,0:T(8,128)(2,1)}), bf16[768,1536]{1,0:T(8,128)(2,1)}) %all-gather.11.cloned.1.call-update) | async-done | bytes 2359312 | tf_op jit(solution)/shard_map/all_gather | solution.py:185
  374.6 10.0 all-gather.9.cloned.1.call-done
  384.7 9.4 multiply_convert_fusion.1
  394.1 58.0 %all-gather.13.cloned.1.call-done = bf16[1536,768]{0,1:T(8,128)(2,1)} async-done(((bf16[1536,48]{0,1:T(8,128)(2,1)}), bf16[1536,768]{0,1:T(8,128)(2,1)}) %all-gather.13.cloned.1.call-update) | async-done | bytes 2359312 | tf_op jit(solution)/shard_map/all_gather | solution.py:187
  452.0 6.4 convolution_convert_fusion.2
  459.9 6.1 reduce-scatter.16.cloned.1.call-done
  471.7 11.1 all-gather.15.cloned.1.call-done
  482.8 9.5 fusion.70
  497.8 10.3 reduce-scatter.18.cloned.1.call-done
  514.9 10.9 all-gather.17.cloned.1.call-done
  530.1 57.5 %while.29 = (s32[]{:T(128)}, f32[1024,6,64]{0,2,1:T(8,128)}, f32[1024,6,64]{0,2,1:T(8,128)}, bf16[2,512,384]{2,1,0:T(8,128)(2,1)}, bf16[2,512,6,64]{1,3,2,0:T(8,...) while((s32[]{:T(128)}, f32[1024,6,64]{0,2,1:T(8,128)}, ...), condition=%wide.region_17.18_spmd.clone, body=%wide.region_15.17_spmd.clone.sunk | while | flops 2063336448 | bytes 140216608 | solution.py:140
  533.1 5.5 bitcast_add_fusion.5
  560.7 6.1 bitcast_add_fusion.5
  597.1 21.3 %all-reduce.22.cloned.1.call-done = bf16[1024,768]{1,0:T(8,128)(2,1)} async-done(((bf16[1024,768]{1,0:T(8,128)(2,1)}), bf16[1024,768]{1,0:T(8,128)(2,1)}) %all-reduce.22.cloned.1.call-update) | async-done | bytes 1572880 | tf_op jit(solution)/shard_map/psum | solution.py:308
  633.3 6.2 fusion.83
  640.9 6.2 fusion.44
  651.8 77.1 %all-reduce.19 = (f32[384]{0:T(512)}, f32[384]{0:T(512)}, f32[1536]{0:T(1024)}) all-reduce(f32[384]{0:T(512)S(1)} %get-tuple-element.373, f32[384]{0:T(512)S(1)} %get-tuple-element.372, f32[1536]{0:T(1024)S(1)} %copy-done.41), channel_id=1, replica_groups=mesh['dp'=16,'tp'=2] {'dp'}, use_global_device_ids=true, to_apply=%region_27.28 | all-reduce | flops 2304 | bytes 18432 | tf_op jit(solution)/shard_map/psum | solution.py:352
  729.0 37.8 %all-reduce.17 = (f32[768]{0:T(1024)S(1)}, f32[768]{0:T(1024)S(1)}, f32[768]{0:T(1024)S(1)}, f32[768]{0:T(1024)S(1)}, f32[768]{0:T(1024)S(1)}, /*index=5*/f32[76...) all-reduce(f32[768]{0:T(1024)S(1)} %dynamic-update-slice.7, ...), channel_id=1, replica_groups=mesh['dp'=16,'tp'=2] {'dp','tp'}, use_global_device_ids=true, to_apply=%add.7 | all-reduce | flops 6912 | bytes 55296
  774.6 72.7 %reduce-scatter.28.cloned.1.call-done = f32[384,48]{0,1:T(8,128)} async-done(((f32[384,768]{0,1:T(8,128)}), f32[384,48]{0,1:T(8,128)}) %reduce-scatter.28.cloned.1.call-update) | async-done | bytes 73744 | tf_op jit(solution)/shard_map/reduce_scatter | solution.py:326
  847.4 128.7 %reduce-scatter.26.cloned.1.call-done = f32[48,384]{1,0:T(8,128)} async-done(((f32[768,384]{1,0:T(8,128)}), f32[48,384]{1,0:T(8,128)}) %reduce-scatter.26.cloned.1.call-update) | async-done | bytes 73744 | tf_op jit(solution)/shard_map/reduce_scatter | solution.py:324
  976.1 128.7 %reduce-scatter.24.cloned.1.call-done = f32[48,384]{1,0:T(8,128)} async-done(((f32[768,384]{1,0:T(8,128)}), f32[48,384]{1,0:T(8,128)}) %reduce-scatter.24.cloned.1.call-update) | async-done | bytes 73744 | tf_op jit(solution)/shard_map/reduce_scatter | solution.py:321
  1104.8 128.6 %reduce-scatter.22.cloned.1.call-done = f32[48,384]{1,0:T(8,128)} async-done(((f32[768,384]{1,0:T(8,128)}), f32[48,384]{1,0:T(8,128)}) %reduce-scatter.22.cloned.1.call-update) | async-done | bytes 73744 | tf_op jit(solution)/shard_map/reduce_scatter | solution.py:320
  1233.3 142.6 %reduce-scatter.32.cloned.1.call-done = f32[1536,48]{0,1:T(8,128)} async-done(((f32[1536,768]{0,1:T(8,128)}), f32[1536,48]{0,1:T(8,128)}) %reduce-scatter.32.cloned.1.call-update) | async-done | bytes 294928 | tf_op jit(solution)/shard_map/reduce_scatter | solution.py:327
  1375.9 141.8 %reduce-scatter.30.cloned.1.call-done = f32[48,1536]{1,0:T(8,128)} async-done(((f32[768,1536]{1,0:T(8,128)}), f32[48,1536]{1,0:T(8,128)}) %reduce-scatter.30.cloned.1.call-update) | async-done | bytes 294928 | tf_op jit(solution)/shard_map/reduce_scatter | solution.py:325
  1517.6 104.9 %reduce-scatter.20.cloned.1.call-done = f32[24,768]{1,0:T(8,128)} async-done(((f32[768,768]{1,0:T(8,128)}), f32[24,768]{1,0:T(8,128)}) %reduce-scatter.20.cloned.1.call-update) | async-done | bytes 73744 | tf_op jit(solution)/shard_map/reduce_scatter | solution.py:343
  (303 shorter events, 173.6 us)
Async XLA Ops:
  8.0 262.3 %all-gather.7.cloned.1.call-start = ((), (), s32[]{:S(2)}) async-start(), calls=%async_computation.11 | async-start | bytes 1216512 | tf_op jit(solution)/shard_map/all_gather | solution.py:204
  9.6 307.5 %reduce-scatter.14.cloned.1.call-start = ((), (), s32[]{:S(2)}) async-start(), calls=%async_computation.12 | async-start | bytes 2359296 | tf_op jit(solution)/shard_map/reduce_scatter | solution.py:235
  12.9 298.5 %copy-start.47 = (pred[1024]{0:T(1024)(128)(4,1)}, pred[1024]{0:T(1024)(128)(4,1)S(1)}, u32[]{:S(2)}) copy-start(pred[1024]{0:T(1024)(128)(4,1)S(1)} %get-tuple-element.382) | copy-start | bytes 3076
  12.9 298.5 %copy-start.49 = (pred[1024]{0:T(1024)(128)(4,1)}, pred[1024]{0:T(1024)(128)(4,1)S(1)}, u32[]{:S(2)}) copy-start(pred[1024]{0:T(1024)(128)(4,1)S(1)} %get-tuple-element.383) | copy-start | bytes 3076
  147.4 80.0 %copy-start.56 = (s32[1,2]{1,0:T(1,128)S(1)}, s32[1,2]{1,0:T(1,128)}, u32[]{:S(2)}) copy-start(s32[1,2]{1,0:T(1,128)} %param.30) | copy-start | bytes 28
  186.2 85.7 %copy-start.13 = (bf16[1024,768]{1,0:T(8,128)(2,1)S(1)}, bf16[1024,768]{1,0:T(8,128)(2,1)}, u32[]{:S(2)}) copy-start(bf16[1024,768]{1,0:T(8,128)(2,1)} %param.27) | copy-start | bytes 4718596
  227.5 42.7 %copy-start.42 = (bf16[2,64]{1,0:T(2,128)(2,1)}, bf16[2,64]{1,0:T(2,128)(2,1)S(1)}, u32[]{:S(2)}) copy-start(bf16[2,64]{1,0:T(2,128)(2,1)S(1)} %get-tuple-element.374) | copy-start | bytes 772
  228.6 47.3 %copy-start.22 = (f32[2,768]{1,0:T(2,128)}, f32[2,768]{1,0:T(2,128)S(1)}, u32[]{:S(2)}) copy-start(f32[2,768]{1,0:T(2,128)S(1)} %convolution_add_fusion.1) | copy-start | bytes 18436
  310.6 64.0 %all-gather.11.cloned.1.call-start = ((), (), s32[]{:S(2)}) async-start(), calls=%async_computation.14 | async-start | bytes 2506752 | tf_op jit(solution)/shard_map/all_gather | solution.py:185
  311.4 73.3 %all-gather.9.cloned.1.call-start = ((), (), s32[]{:S(2)}) async-start(), calls=%async_computation.13 | async-start | bytes 2359296 | tf_op jit(solution)/shard_map/all_gather | solution.py:245
  319.0 65.6 %copy-start.55 = (f32[1536]{0:T(1024)S(1)}, f32[1536]{0:T(1024)}, u32[]{:S(2)}) copy-start(f32[1536]{0:T(1024)} %param.45) | copy-start | bytes 18436
  320.6 131.5 %all-gather.13.cloned.1.call-start = ((), (), s32[]{:S(2)}) async-start(), calls=%async_computation.15 | async-start | bytes 2506752 | tf_op jit(solution)/shard_map/all_gather | solution.py:187
  321.4 144.6 %reduce-scatter.16.cloned.1.call-start = ((), (), s32[]{:S(2)}) async-start(), calls=%async_computation.16 | async-start | bytes 2359296 | tf_op jit(solution)/shard_map/reduce_scatter | solution.py:251
  458.5 24.3 %all-gather.15.cloned.1.call-start = ((), (), s32[]{:S(2)}) async-start(), calls=%async_computation.17 | async-start | bytes 2359296 | tf_op jit(solution)/shard_map/all_gather | solution.py:276
  471.6 36.5 %reduce-scatter.18.cloned.1.call-start = ((), (), s32[]{:S(2)}) async-start(), calls=%async_computation.18 | async-start | bytes 2359296 | tf_op jit(solution)/shard_map/reduce_scatter | solution.py:284
  497.7 28.1 %all-gather.17.cloned.1.call-start = ((), (), s32[]{:S(2)}) async-start(), calls=%async_computation.19 | async-start | bytes 2359296 | tf_op jit(solution)/shard_map/all_gather | solution.py:291
  514.8 103.6 %all-reduce.22.cloned.1.call-start = ((), (), s32[]{:S(2)}) async-start(), calls=%async_computation.20 | async-start | bytes 3145728 | tf_op jit(solution)/shard_map/psum | solution.py:308
  597.0 177.6 %reduce-scatter.34.cloned.1.call-start = ((), (), s32[]{:S(2)}) async-start(), calls=%async_computation.28 | async-start | bytes 405504
  622.3 225.0 %reduce-scatter.28.cloned.1.call-start = ((), (), s32[]{:S(2)}) async-start(), calls=%async_computation.25 | async-start | bytes 1253376 | tf_op jit(solution)/shard_map/reduce_scatter | solution.py:326
  626.2 349.8 %reduce-scatter.26.cloned.1.call-start = ((), (), s32[]{:S(2)}) async-start(), calls=%async_computation.24 | async-start | bytes 1253376 | tf_op jit(solution)/shard_map/reduce_scatter | solution.py:324
  631.9 472.9 %reduce-scatter.24.cloned.1.call-start = ((), (), s32[]{:S(2)}) async-start(), calls=%async_computation.23 | async-start | bytes 1253376 | tf_op jit(solution)/shard_map/reduce_scatter | solution.py:321
  632.6 600.7 %reduce-scatter.22.cloned.1.call-start = ((), (), s32[]{:S(2)}) async-start(), calls=%async_computation.22 | async-start | bytes 1253376 | tf_op jit(solution)/shard_map/reduce_scatter | solution.py:320
  633.2 742.7 %reduce-scatter.32.cloned.1.call-start = ((), (), s32[]{:S(2)}) async-start(), calls=%async_computation.27 | async-start | bytes 5013504 | tf_op jit(solution)/shard_map/reduce_scatter | solution.py:327
  639.5 878.1 %reduce-scatter.30.cloned.1.call-start = ((), (), s32[]{:S(2)}) async-start(), calls=%async_computation.26 | async-start | bytes 5013504 | tf_op jit(solution)/shard_map/reduce_scatter | solution.py:325
  647.2 975.4 %reduce-scatter.20.cloned.1.call-start = ((), (), s32[]{:S(2)}) async-start(), calls=%async_computation.21 | async-start | bytes 2433024 | tf_op jit(solution)/shard_map/reduce_scatter | solution.py:343
  649.8 79.2 %copy-start.30 = (f32[768]{0:T(1024)S(1)}, f32[768]{0:T(1024)}, u32[]{:S(2)}) copy-start(f32[768]{0:T(1024)} %get-tuple-element.279) | copy-start | bytes 9220
  649.8 79.2 %copy-start.31 = (f32[768]{0:T(1024)S(1)}, f32[768]{0:T(1024)}, u32[]{:S(2)}) copy-start(f32[768]{0:T(1024)} %get-tuple-element.285) | copy-start | bytes 9220
  649.8 79.2 %copy-start.36 = (f32[768]{0:T(1024)S(1)}, f32[768]{0:T(1024)}, u32[]{:S(2)}) copy-start(f32[768]{0:T(1024)} %get-tuple-element.277) | copy-start | bytes 9220
  649.8 79.2 %copy-start.37 = (f32[768]{0:T(1024)S(1)}, f32[768]{0:T(1024)}, u32[]{:S(2)}) copy-start(f32[768]{0:T(1024)} %get-tuple-element.282) | copy-start | bytes 9220
  649.8 79.2 %copy-start.38 = (f32[768]{0:T(1024)S(1)}, f32[768]{0:T(1024)}, u32[]{:S(2)}) copy-start(f32[768]{0:T(1024)} %get-tuple-element.283) | copy-start | bytes 9220
  649.8 79.2 %copy-start.39 = (f32[768]{0:T(1024)S(1)}, f32[768]{0:T(1024)}, u32[]{:S(2)}) copy-start(f32[768]{0:T(1024)} %get-tuple-element.351) | copy-start | bytes 9220
  649.8 121.7 %copy-start.8 = (bf16[1024,768]{1,0:T(8,128)(2,1)S(1)}, bf16[1024,768]{1,0:T(8,128)(2,1)}, u32[]{:S(2)}) copy-start(bf16[1024,768]{1,0:T(8,128)(2,1)} %all-reduce.22.cloned.1.call-done) | copy-start | bytes 4718596
  (47 other events, 386.6 us)
Sparse Core Ops, SparseCore 0:
  12.3 56.7 all-gather.6
  310.7 6.3 reduce-scatter.13
  458.6 7.3 reduce-scatter.15
  471.8 11.0 all-gather.14
  497.9 10.2 reduce-scatter.17
  622.4 96.0 reduce-scatter.33
  724.5 122.8 reduce-scatter.27
  853.4 122.6 reduce-scatter.25
  982.1 122.5 reduce-scatter.23
  1110.7 122.6 reduce-scatter.21
  1239.9 135.9 reduce-scatter.31
  1381.5 136.1 reduce-scatter.29
  1524.4 98.1 reduce-scatter.19
Sparse Core Ops, SparseCore 1:
  314.9 59.7 all-gather.10
  376.7 7.9 all-gather.8
  388.3 63.7 all-gather.12
  514.9 10.9 all-gather.16
  597.1 21.2 all-reduce.21
where the time goes:
time: 1630 us
  waiting for transfers between devices  1030 us (63%)
  blocking collectives  360 us (22%)
  matrix products  127 us (8%)
  other arithmetic  60.1 us (4%)
  local copies, waits for them, and re-layouts  31.5 us (2%)
  between operations  18 us (1%)
    reduce_scatter x1, waiting for transfers between devices, on_device(): lax.psum_scatter(grad_w_down, 'dp', scatter_dimension=1, tiled=True)  143 us
    reduce_scatter x1, waiting for transfers between devices, on_device(): lax.psum_scatter(grad_w_up, 'dp', scatter_dimension=0, tiled=True)  142 us
    reduce_scatter x1, waiting for transfers between devices, on_device(): lax.psum_scatter(grad_qkv_w[:, 2 * head_width:], 'dp', scatter_dimension=...  129 us
    reduce_scatter x1, waiting for transfers between devices, on_device(): lax.psum_scatter(grad_qkv_w[:, head_width:2 * head_width], 'dp', scatter_...  129 us
    reduce_scatter x1, waiting for transfers between devices, on_device(): lax.psum_scatter(grad_qkv_w[:, :head_width], 'dp', scatter_dimension=0, t...  129 us
    reduce_scatter x1, waiting for transfers between devices, on_device(): lax.psum_scatter(grad_tw2, ('dp', 'tp'), scatter_dimension=0, tiled=True)  105 us
    psum x1, blocking collectives, on_device(): lax.psum((grad_b_query, grad_b_value, grad_b_up), 'dp')  77.1 us
    unnamed x2, blocking collectives  75.6 us
  transfers between devices with their start and end apart: 18, of which 16 were waited for; matrix products, arithmetic and copies ran while one was open for 4% of the time, Pallas kernels for 0%

commit v1 on v0

v1 whole, which is shorter than its diff:
```python
import functools
import math

import jax
import jax.numpy as jnp
from jax import lax
from jax.experimental import pallas as pl
from jax.experimental.pallas import tpu as pltpu
from jax.sharding import PartitionSpec as P

HD = 64
TE = 128
SUPER = 16

epsilon = 1e-05
highest = lax.Precision.HIGHEST
f32 = jnp.float32
bf16 = jnp.bfloat16


class Place:
    def __init__(self, sub):
        self.sub = sub
        index = lax.axis_index("dp")
        self.low = lax.rem(index, sub)
        self.place = lax.div(index, sub)
        self.z = lax.div(self.place, 4)
        self.p = lax.rem(self.place, 4)
        self.r = self.ring(self.p)

    @staticmethod
    def ring(v):
        half = lax.div(v, 2)
        return 2 * half + lax.rem(lax.rem(v, 2) + half, 2)

    def spot(self, dz, dr):
        z = lax.rem(self.z + dz + 4, 4)
        p = self.ring(lax.rem(self.r + dr + 4, 4))
        return z * 4 + p

    def device(self, dz, dr):
        return {"dp": self.spot(dz, dr) * self.sub + self.low}

    def other(self):
        return {"tp": 1 - lax.axis_index("tp")}

    def rows(self, dz, dr, count):
        return pl.ds(pl.multiple_of(self.spot(dz, dr) * count, 16), count)

    def enter(self):
        barrier = pltpu.get_barrier_semaphore()
        for peer in (
            [self.device(d, 0) for d in (1, 2, 3)]
            + [self.device(0, d) for d in (1, 2, 3)]
            + [self.other()]
        ):
            pl.semaphore_signal(barrier, inc=1, device_id=peer, device_id_type=pl.DeviceIdType.MESH)
        pl.semaphore_wait(barrier, 7)


def remote(src, dst, send, recv, device):
    return pltpu.make_async_remote_copy(
        src_ref=src,
        dst_ref=dst,
        send_sem=send,
        recv_sem=recv,
        device_id=device,
        device_id_type=pl.DeviceIdType.MESH,
    )


class Gather:
    def __init__(self, place, shard, full, send, recv, g):
        rows = shard.shape[0]
        at = lambda dz, dr: full.at[place.rows(dz, dr, rows), :]
        self.place, self.shard, self.full, self.count = place, shard, full, rows
        self.to_planes = [
            remote(shard, at(0, 0), send.at[g, d - 1], recv.at[g, d - 1], place.device(d, 0))
            for d in (1, 2, 3)
        ]
        self.around = []
        self.relay = []
        for d in range(4):
            source = shard if d == 0 else at(-d, 0)
            self.around.append(
                [
                    remote(
                        source,
                        at(-d, 0),
                        send.at[g, 3 + 2 * d + k],
                        recv.at[g, 3 + 2 * d + k],
                        place.device(0, 1 - 2 * k),
                    )
                    for k in (0, 1)
                ]
            )
            k = d // 2
            self.relay.append(
                remote(
                    at(-d, 2 * k - 1),
                    at(-d, 2 * k - 1),
                    send.at[g, 11 + d],
                    recv.at[g, 11 + d],
                    place.device(0, 1 - 2 * k),
                )
            )

    def begin(self):
        for copy in self.to_planes:
            copy.start()
        for copy in self.around[0]:
            copy.start()
        self.full[self.place.rows(0, 0, self.count), :] = self.shard[...]

    def turn(self, d):
        if d:
            self.to_planes[d - 1].wait_recv()
            for copy in self.around[d]:
                copy.start()

    def pass_on(self, d):
        k = d // 2
        self.around[d][k].wait_recv()
        self.relay[d].start()

    def finish(self):
        for d in range(4):
            self.around[d][1 - d // 2].wait_recv()
            self.relay[d].wait_recv()

    def drain(self):
        for copy in self.to_planes + [c for pair in self.around for c in pair] + self.relay:
            copy.wait_send()


class Reduce:
    def __init__(self, place, grads, total, first, second, third, joined, across, send, recv, g):
        rows = total.shape[0]
        at = lambda dz, dr: grads.at[place.rows(dz, dr, rows), :]
        self.place, self.grads, self.total, self.rows = place, grads, total, rows
        self.first, self.second, self.third, self.joined, self.across = first, second, third, joined, across
        self.far, self.near, self.up = [], [], []
        for d in range(4):
            k = d // 2
            self.far.append(
                remote(
                    at(d, 2), first.at[d], send.at[g, d], recv.at[g, d], place.device(0, 1 - 2 * k)
                )
            )
            pair = []
            for j in (0, 1):
                source = joined.at[d] if j == k else at(d, 1 - 2 * j)
                pair.append(
                    remote(
                        source,
                        second.at[j * 4 + d],
                        send.at[g, 4 + 2 * d + j],
                        recv.at[g, 4 + 2 * d + j],
                        place.device(0, 1 - 2 * j),
                    )
                )
            self.near.append(pair)
        for d in (1, 2, 3):
            self.up.append(
                remote(
                    across.at[d - 1],
                    third.at[d - 1],
                    send.at[g, 11 + d],
                    recv.at[g, 11 + d],
                    place.device(d, 0),
                )
            )

    def block(self, dz, dr):
        return self.grads[self.place.rows(dz, dr, self.rows), :].astype(f32)

    def begin(self):
        for d in range(4):
            self.far[d].start()
        for d in range(4):
            self.near[d][1 - d // 2].start()

    def join(self, d):
        k = d // 2
        self.far[d].wait_recv()
        self.joined[d] = (self.first[d].astype(f32) + self.block(d, 1 - 2 * k)).astype(bf16)
        self.near[d][k].start()

    def cross(self, d):
        for j in (0, 1):
            self.near[d][j].wait_recv()
        summed = self.block(d, 0) + self.second[d].astype(f32) + self.second[4 + d].astype(f32)
        if d:
            self.across[d - 1] = summed.astype(bf16)
            self.up[d - 1].start()
        else:
            self.total[...] = summed

    def finish(self):
        for copy in self.up:
            copy.wait_recv()
        self.total[...] += (
            self.third[0].astype(f32) + self.third[1].astype(f32) + self.third[2].astype(f32)
        )

    def drain(self):
        for copy in self.far + [c for pair in self.near for c in pair] + self.up:
            copy.wait_send()


class Spread:
    def __init__(self, place, along, sources, slots, send, recv, base):
        if along == "tp":
            self.copies = [remote(sources[0], slots, send.at[base], recv.at[base], place.other())]
            return
        self.copies = [
            remote(
                sources[d - 1],
                slots.at[d - 1],
                send.at[base + d - 1],
                recv.at[base + d - 1],
                place.device(d, 0) if along == "z" else place.device(0, d),
            )
            for d in (1, 2, 3)
        ]

    def start(self):
        for copy in self.copies:
            copy.start()

    def wait(self):
        for copy in self.copies:
            copy.wait_recv()

    def drain(self):
        for copy in self.copies:
            copy.wait_send()


def gather_kernel(
    sub,
    w0, w1, w2, w3, feats, vectors, tw1, tb1, tw2,
    f0, f1, f2, f3, all_feats, embed, shared,
    feat_z, feat_sum, feat_in, part, part_in, part_sum, part_z, part_zsum, part_tp,
    send, recv, small_send, small_recv,
):
    place = Place(sub)
    place.enter()
    seqs = feats.shape[0]
    spread_z = Spread(place, "z", [feats] * 3, feat_z, small_send, small_recv, 0)
    spread_z.start()
    gathers = [
        Gather(place, shard, full, send, recv, g)
        for g, (shard, full) in enumerate(((w0, f0), (w1, f1), (w2, f2), (w3, f3)))
    ]
    for one in gathers:
        one.begin()
    spread_z.wait()
    feat_sum[...] = feats[...] + feat_z[0] + feat_z[1] + feat_z[2]
    spread_r = Spread(place, "r", [feat_sum] * 3, feat_in, small_send, small_recv, 3)
    spread_r.start()
    all_feats[0] = feat_sum[...]
    spread_r.wait()
    for d in (1, 2, 3):
        all_feats[d] = feat_in[d - 1]
    every = all_feats[...].reshape(4 * seqs, TE)
    before = (
        jnp.dot(every.astype(bf16), tw1[...].astype(bf16), preferred_element_type=f32) + tb1[...]
    )
    hidden = jax.nn.silu(before).astype(bf16)
    share = jnp.dot(hidden, tw2[...].astype(bf16), preferred_element_type=f32)
    for d in range(4):
        part[d, :seqs, :] = share[d * seqs : (d + 1) * seqs, :]
        part[d, seqs:, :] = vectors[...]
    back = Spread(
        place, "r", [part.at[3], part.at[2], part.at[1]], part_in, small_send, small_recv, 6
    )
    back.start()
    back.wait()
    part_sum[...] = part[0] + part_in[0] + part_in[1] + part_in[2]
    over_z = Spread(place, "z", [part_sum] * 3, part_z, small_send, small_recv, 9)
    over_z.start()
    over_z.wait()
    part_zsum[...] = part_sum[...] + part_z[0] + part_z[1] + part_z[2]
    pair = Spread(place, "tp", [part_zsum], part_tp, small_send, small_recv, 12)
    pair.start()
    pair.wait()
    both = part_zsum[...] + part_tp[...]
    shared[...] = both[seqs:]
    embed[...] = both[:seqs] + shared[0:1, :]
    for one in gathers:
        for d in (1, 2, 3):
            one.turn(d)
        for d in range(4):
            one.pass_on(d)
    for one in gathers:
        one.finish()
    for one in gathers:
        one.drain()
    for one in (spread_z, spread_r, back, over_z, pair):
        one.drain()


def reduce_kernel(
    sub,
    g0, g1, g2, g3, sums,
    t0, t1, t2, t3, all_sums, all_embed,
    *rest,
):
    buffers, (pair_in, pair_sum, z_in, z_sum, r_in, send, recv, small_send, small_recv) = rest[:20], rest[20:]
    place = Place(sub)
    place.enter()
    reduces = [
        Reduce(place, grads, total, *buffers[5 * g : 5 * g + 5], send, recv, g)
        for g, (grads, total) in enumerate(((g0, t0), (g1, t1), (g2, t2), (g3, t3)))
    ]
    pair = Spread(place, "tp", [sums], pair_in, small_send, small_recv, 0)
    pair.start()
    for one in reduces:
        one.begin()
    pair.wait()
    other = pair_in[...]
    row = lax.broadcasted_iota(jnp.int32, other.shape, 0)
    pair_sum[...] = sums[...] + jnp.where((row >= 8) & (row < 16), 0.0, other)
    over_z = Spread(place, "z", [pair_sum] * 3, z_in, small_send, small_recv, 1)
    over_z.start()
    over_z.wait()
    z_sum[...] = pair_sum[...] + z_in[0] + z_in[1] + z_in[2]
    over_r = Spread(place, "r", [z_sum] * 3, r_in, small_send, small_recv, 4)
    over_r.start()
    over_r.wait()
    all_sums[...] = z_sum[:16] + r_in[0, :16] + r_in[1, :16] + r_in[2, :16]
    all_embed[0] = z_sum[16:]
    for d in (1, 2, 3):
        all_embed[d] = r_in[d - 1, 16:]
    for one in reduces:
        for d in range(4):
            one.join(d)
    for one in reduces:
        for d in (1, 2, 3, 0):
            one.cross(d)
    for one in reduces:
        one.finish()
    for one in reduces:
        one.drain()
    for one in (pair, over_z, over_r):
        one.drain()


def vmem(count):
    return [pl.BlockSpec(memory_space=pltpu.VMEM)] * count


def call_gather(sub, shards, feats, vectors, tw1, tb1, tw2):
    seqs = feats.shape[0]
    width = vectors.shape[1]
    full = [jax.ShapeDtypeStruct((s.shape[0] * SUPER, s.shape[1]), bf16) for s in shards]
    small = seqs + 8
    return pl.pallas_call(
        functools.partial(gather_kernel, sub),
        out_shape=full
        + [
            jax.ShapeDtypeStruct((4, seqs, TE), f32),
            jax.ShapeDtypeStruct((seqs, width), f32),
            jax.ShapeDtypeStruct((8, width), f32),
        ],
        in_specs=vmem(9),
        out_specs=vmem(7),
        scratch_shapes=[
            pltpu.VMEM((3, seqs, TE), f32),
            pltpu.VMEM((seqs, TE), f32),
            pltpu.VMEM((3, seqs, TE), f32),
            pltpu.VMEM((4, small, width), f32),
            pltpu.VMEM((3, small, width), f32),
            pltpu.VMEM((small, width), f32),
            pltpu.VMEM((3, small, width), f32),
            pltpu.VMEM((small, width), f32),
            pltpu.VMEM((small, width), f32),
            pltpu.SemaphoreType.DMA((4, 15)),
            pltpu.SemaphoreType.DMA((4, 15)),
            pltpu.SemaphoreType.DMA((13,)),
            pltpu.SemaphoreType.DMA((13,)),
        ],
        compiler_params=pltpu.CompilerParams(
            collective_id=0, has_side_effects=True, vmem_limit_bytes=40 * 1024 * 1024
        ),
        name="gather_weights",
    )(*shards, feats, vectors, tw1, tb1, tw2)


def call_reduce(sub, grads, sums):
    rows = grads[0].shape[0] // SUPER
    width = sums.shape[1]
    seqs = sums.shape[0] - 16
    buffers = []
    for one in grads:
        for count in (4, 8, 3, 4, 3):
            buffers.append(pltpu.VMEM((count, rows, one.shape[1]), bf16))
    tall = sums.shape[0]
    return pl.pallas_call(
        functools.partial(reduce_kernel, sub),
        out_shape=[jax.ShapeDtypeStruct((rows, one.shape[1]), f32) for one in grads]
        + [
            jax.ShapeDtypeStruct((16, width), f32),
            jax.ShapeDtypeStruct((4, seqs, width), f32),
        ],
        in_specs=vmem(5),
        out_specs=vmem(6),
        scratch_shapes=buffers
        + [
            pltpu.VMEM((tall, width), f32),
            pltpu.VMEM((tall, width), f32),
            pltpu.VMEM((3, tall, width), f32),
            pltpu.VMEM((tall, width), f32),
            pltpu.VMEM((3, tall, width), f32),
            pltpu.SemaphoreType.DMA((4, 15)),
            pltpu.SemaphoreType.DMA((4, 15)),
            pltpu.SemaphoreType.DMA((7,)),
            pltpu.SemaphoreType.DMA((7,)),
        ],
        compiler_params=pltpu.CompilerParams(
            collective_id=1, has_side_effects=True, vmem_limit_bytes=48 * 1024 * 1024
        ),
        name="reduce_gradients",
    )(*grads, sums)


def time_features(time_steps, feature_width):
    half_width = feature_width // 2
    frequency = jnp.exp(-math.log(10000.0) * jnp.arange(half_width, dtype=f32) / half_width)
    angles = time_steps.astype(f32)[:, None] * frequency[None, :]
    return jnp.concatenate([jnp.cos(angles), jnp.sin(angles)], axis=1)


def segment_ids(lengths, row_count):
    row_index = jnp.arange(row_count, dtype=jnp.int32)
    inner = jnp.where(row_index < lengths[0] + lengths[1], 1, 2)
    return jnp.where(row_index < lengths[0], 0, inner).astype(jnp.int32)


def contract_rows(left_side, right_side, precision_mode=None):
    return lax.dot_general(
        left_side,
        right_side,
        (((0,), (0,)), ((), ())),
        precision=precision_mode,
        preferred_element_type=jnp.float32,
    )


def contract_cols(left_side, right_side, precision_mode=None):
    return lax.dot_general(
        left_side,
        right_side,
        (((1,), (1,)), ((), ())),
        precision=precision_mode,
        preferred_element_type=jnp.float32,
    )


def norm_forward(summed, gain_row, shift_row):
    centered = summed - jnp.mean(summed, axis=-1, keepdims=True)
    inv_std = lax.rsqrt(jnp.mean(centered * centered, axis=-1, keepdims=True) + epsilon)
    normed = centered * inv_std
    return (normed * gain_row + shift_row, normed, inv_std)


def norm_backward(grad_rows, normed, inv_std, gain_row):
    scaled = grad_rows * gain_row
    inner = (
        scaled
        - jnp.mean(scaled, axis=-1, keepdims=True)
        - normed * jnp.mean(scaled * normed, axis=-1, keepdims=True)
    )
    return (inner * inv_std, jnp.sum(grad_rows * normed, axis=0), jnp.sum(grad_rows, axis=0))


def block_scores(query_blk, key_heads, seg_blk, segment, factor):
    raw_scores = (
        jnp.einsum("qhd,khd->hqk", query_blk, key_heads, preferred_element_type=jnp.float32)
        * factor
    )
    allowed = seg_blk[:, None] == segment[None, :]
    return jnp.where(allowed[None], raw_scores, -1e30)


def attention_forward(query_rows, key_rows, value_rows, segment, block_rows):
    rows_total = query_rows.shape[0]
    head_count = query_rows.shape[1] // HD
    factor = 1.0 / math.sqrt(HD)
    key_heads = key_rows.reshape(rows_total, head_count, HD)
    value_heads = value_rows.reshape(rows_total, head_count, HD)
    query_blocks = query_rows.reshape(rows_total // block_rows, block_rows, head_count, HD)
    seg_blocks = segment.reshape(rows_total // block_rows, block_rows)

    def one_block(item):
        query_blk, seg_blk = item
        scores = block_scores(query_blk, key_heads, seg_blk, segment, factor)
        row_max = jnp.max(scores, axis=-1, keepdims=True)
        exp_scores = jnp.exp(scores - row_max)
        row_total = jnp.sum(exp_scores, axis=-1, keepdims=True)
        prob_low = (exp_scores / row_total).astype(jnp.bfloat16)
        mixed_blk = jnp.einsum(
            "hqk,khd->qhd", prob_low, value_heads, preferred_element_type=jnp.float32
        )
        log_total = (row_max + jnp.log(row_total))[..., 0]
        return (mixed_blk.reshape(block_rows, head_count * HD).astype(jnp.bfloat16), log_total)

    mixed_blocks, log_totals = lax.map(one_block, (query_blocks, seg_blocks))
    return (mixed_blocks.reshape(rows_total, head_count * HD), log_totals)


def attention_backward(
    query_rows, key_rows, value_rows, grad_mixed, log_totals, segment, block_rows
):
    rows_total = query_rows.shape[0]
    head_count = query_rows.shape[1] // HD
    factor = 1.0 / math.sqrt(HD)
    block_count = rows_total // block_rows
    key_heads = key_rows.reshape(rows_total, head_count, HD)
    value_heads = value_rows.reshape(rows_total, head_count, HD)
    query_blocks = query_rows.reshape(block_count, block_rows, head_count, HD)
    grad_blocks = grad_mixed.reshape(block_count, block_rows, head_count, HD)
    seg_blocks = segment.reshape(block_count, block_rows)

    def one_block(carry, item):
        grad_key_acc, grad_value_acc = carry
        query_blk, grad_blk, seg_blk, log_blk = item
        scores = block_scores(query_blk, key_heads, seg_blk, segment, factor)
        probs_full = jnp.exp(scores - log_blk[..., None])
        prob_low = probs_full.astype(jnp.bfloat16)
        grad_value_acc = grad_value_acc + jnp.einsum(
            "hqk,qhd->khd", prob_low, grad_blk, preferred_element_type=jnp.float32
        )
        grad_probs = jnp.einsum(
            "qhd,khd->hqk", grad_blk, value_heads, preferred_element_type=jnp.float32
        )
        row_inner = jnp.sum(grad_probs * probs_full, axis=-1, keepdims=True)
        grad_scores = (probs_full * (grad_probs - row_inner)).astype(jnp.bfloat16)
        grad_query_blk = (
            jnp.einsum("hqk,khd->qhd", grad_scores, key_heads, preferred_element_type=jnp.float32)
            * factor
        )
        grad_key_acc = (
            grad_key_acc
            + jnp.einsum("hqk,qhd->khd", grad_scores, query_blk, preferred_element_type=jnp.float32)
            * factor
        )
        return ((grad_key_acc, grad_value_acc), grad_query_blk.reshape(block_rows, head_count * HD))

    zeros_heads = jnp.zeros((rows_total, head_count, HD), jnp.float32)
    (grad_key_acc, grad_value_acc), grad_query_blocks = lax.scan(
        one_block, (zeros_heads, zeros_heads), (query_blocks, grad_blocks, seg_blocks, log_totals)
    )
    return (
        grad_query_blocks.reshape(rows_total, head_count * HD),
        grad_key_acc.reshape(rows_total, head_count * HD),
        grad_value_acc.reshape(rows_total, head_count * HD),
    )


def on_device(
    inputs, cotangent, seq_lengths, timesteps, time_w1, time_b1, time_w2, time_b2,
    w_query, b_query, w_key, w_value, b_value, w_out, b_out, norm1_gain, norm1_bias,
    w_up, b_up, w_down, b_down, norm2_gain, norm2_bias,
):
    dp = lax.axis_size("dp")
    sub = dp // SUPER
    low = [[q * sub + l for l in range(sub)] for q in range(SUPER)]
    dp_index = lax.axis_index("dp")
    tp_index = lax.axis_index("tp")
    seq_rows, width = inputs.shape
    own_rows = seq_rows // lax.axis_size("tp")
    row_start = tp_index * own_rows
    block_rows = min(512, seq_rows)
    head_width = w_query.shape[1]

    def near_gather(value, axis):
        if sub == 1:
            return value
        return lax.all_gather(value, "dp", axis=axis, tiled=True, axis_index_groups=low)

    def near_sum(value):
        if sub == 1:
            return value
        return lax.psum(value, "dp", axis_index_groups=low)

    def near_scatter(value):
        if sub == 1:
            return value
        return lax.psum_scatter(
            value, "dp", scatter_dimension=0, tiled=True, axis_index_groups=low
        )

    z = dp_index // (4 * sub)
    pair_row = (z * sub + dp_index % sub) * 2
    seqs = 8 * sub
    features = time_features(timesteps[0], TE).astype(bf16)
    placed_feats = lax.dynamic_update_slice(
        jnp.zeros((seqs, TE), f32), features.astype(f32), (pair_row, 0)
    )
    own_slice = width // (dp * lax.axis_size("tp"))
    slice_start = (dp_index * lax.axis_size("tp") + tp_index) * own_slice
    stacked = jnp.stack(
        [time_b2, b_out, norm1_gain, norm1_bias, b_down, norm2_gain, norm2_bias, jnp.zeros_like(b_out)]
    )
    vectors = lax.dynamic_update_slice(jnp.zeros((8, width), f32), stacked, (0, slice_start))
    shards = [
        near_gather(one, 0)
        for one in (
            jnp.concatenate([w_query, w_key, w_value], axis=1).astype(bf16),
            w_out.T.astype(bf16),
            w_up.astype(bf16),
            w_down.T.astype(bf16),
        )
    ]
    wqkv, wout_t, wup, wdown_t, all_feats, embed, shared = call_gather(
        sub,
        shards,
        near_sum(placed_feats),
        near_sum(vectors),
        near_gather(time_w1, 1),
        near_gather(time_b1, 0)[None, :],
        near_gather(time_w2, 0),
    )
    bout_full, gain_one, shift_one, bdown_full, gain_two, shift_two = [shared[i] for i in range(1, 7)]
    time_embed = lax.dynamic_slice(embed, (pair_row, 0), (2, width))

    lengths = seq_lengths[0]
    segment = segment_ids(lengths, seq_rows)
    inner_embed = jnp.where((segment == 1)[:, None], time_embed[1][None, :], 0.0)
    added = jnp.where((segment == 0)[:, None], time_embed[0][None, :], inner_embed)
    base_rows = inputs.astype(f32) + added
    base_low = base_rows.astype(bf16)
    projected = jnp.dot(base_low, wqkv, preferred_element_type=f32)
    query_rows = (projected[:, :head_width] + b_query).astype(bf16)
    key_rows = projected[:, head_width : 2 * head_width].astype(bf16)
    value_rows = (projected[:, 2 * head_width :] + b_value).astype(bf16)
    mixed_low, log_totals = attention_forward(query_rows, key_rows, value_rows, segment, block_rows)
    attn_own = (
        lax.psum_scatter(
            contract_cols(mixed_low, wout_t).astype(bf16), "tp", scatter_dimension=0, tiled=True
        ).astype(f32)
        + bout_full
    )
    base_own = lax.dynamic_slice_in_dim(base_rows, row_start, own_rows, 0)
    first_out, normed_one, inv_one = norm_forward(base_own + attn_own, gain_one, shift_one)
    first_all = lax.all_gather(first_out.astype(bf16), "tp", axis=0, tiled=True)
    up_pre = jnp.dot(first_all, wup, preferred_element_type=f32) + b_up
    gelu_value, gelu_pull = jax.vjp(jax.nn.gelu, up_pre)
    up_act = gelu_value.astype(bf16)
    ffn_own = (
        lax.psum_scatter(
            contract_cols(up_act, wdown_t).astype(bf16), "tp", scatter_dimension=0, tiled=True
        ).astype(f32)
        + bdown_full
    )
    outputs_own, normed_two, inv_two = norm_forward(first_out + ffn_own, gain_two, shift_two)
    seg_own = lax.dynamic_slice_in_dim(segment, row_start, own_rows, 0)
    valid_own = (seg_own < 2).astype(f32)
    grad_y = cotangent.astype(f32) * valid_own[:, None]
    grad_second, grad_gain_two, grad_shift_two = norm_backward(grad_y, normed_two, inv_two, gain_two)
    grad_b_down = jnp.sum(grad_second, axis=0)
    grad_down_all = lax.all_gather(grad_second.astype(bf16), "tp", axis=0, tiled=True)
    grad_w_down = contract_rows(grad_down_all, up_act)
    grad_act = jnp.dot(grad_down_all, wdown_t, preferred_element_type=f32)
    grad_up_pre = gelu_pull(grad_act)[0]
    grad_b_up = jnp.sum(grad_up_pre, axis=0)
    grad_up_low = grad_up_pre.astype(bf16)
    grad_w_up = contract_rows(first_all, grad_up_low)
    grad_first = grad_second + lax.psum_scatter(
        contract_cols(grad_up_low, wup).astype(bf16), "tp", scatter_dimension=0, tiled=True
    ).astype(f32)
    grad_r1, grad_gain_one, grad_shift_one = norm_backward(grad_first, normed_one, inv_one, gain_one)
    grad_b_out = jnp.sum(grad_r1, axis=0)
    grad_attn_all = lax.all_gather(grad_r1.astype(bf16), "tp", axis=0, tiled=True)
    grad_w_out = contract_rows(grad_attn_all, mixed_low)
    grad_mixed = jnp.dot(grad_attn_all, wout_t, preferred_element_type=f32).astype(bf16)
    grad_query, grad_keys, grad_values = attention_backward(
        query_rows, key_rows, value_rows, grad_mixed, log_totals, segment, block_rows
    )
    grad_qkv = jnp.concatenate(
        [grad_query.astype(bf16), grad_keys.astype(bf16), grad_values.astype(bf16)], axis=1
    )
    grad_qkv_sums = jnp.sum(grad_qkv.astype(f32), axis=0)
    grad_b_query = grad_qkv_sums[:head_width]
    grad_b_value = grad_qkv_sums[2 * head_width :]
    grad_qkv_w = contract_rows(base_low, grad_qkv)
    input_term = contract_cols(grad_qkv, wqkv)
    own_part = lax.dynamic_slice_in_dim(input_term, row_start, own_rows, 0) + grad_r1
    input_term = lax.dynamic_update_slice_in_dim(input_term, own_part, row_start, 0)
    grad_inputs = lax.psum(input_term.astype(bf16), "tp").astype(f32)
    grad_own = lax.dynamic_slice_in_dim(grad_inputs, row_start, own_rows, 0)
    picker_own = (seg_own[:, None] == jnp.arange(2, dtype=jnp.int32)[None, :]).astype(f32)
    grad_embed = contract_rows(picker_own, grad_own, highest)

    placed_embed = lax.dynamic_update_slice(jnp.zeros((seqs, width), f32), grad_embed, (pair_row, 0))
    zero_row = jnp.zeros((width,), f32)
    sums = jnp.concatenate(
        [
            jnp.stack(
                [grad_b_out, grad_gain_one, grad_shift_one, grad_b_down, grad_gain_two, grad_shift_two]
                + [zero_row] * 2
            ),
            jnp.concatenate([grad_b_query, grad_b_value]).reshape(-1, width),
            grad_b_up.reshape(-1, width),
        ],
        axis=0,
    )
    local_rows = sums.shape[0]
    sums = jnp.concatenate([sums, jnp.zeros((16 - local_rows, width), f32), placed_embed], axis=0)
    red_qkv, red_out, red_up, red_down, all_sums, all_embed = call_reduce(
        sub,
        [grad_qkv_w.astype(bf16), grad_w_out.astype(bf16), grad_w_up.astype(bf16), grad_w_down.astype(bf16)],
        sums,
    )
    all_sums, all_embed = near_sum((all_sums, all_embed))
    red_qkv, red_out, red_up, red_down = [
        near_scatter(one) for one in (red_qkv, red_out, red_up, red_down)
    ]
    own_vectors = lax.dynamic_slice(all_sums, (0, slice_start), (8, own_slice))
    tp_vectors = all_sums[8:16].reshape(-1)
    every_feat = all_feats.reshape(-1, TE)
    every_embed = all_embed.reshape(-1, width)
    time_pre = (
        jnp.dot(every_feat.astype(bf16), time_w1.astype(bf16), preferred_element_type=f32) + time_b1
    )
    silu_value, silu_pull = jax.vjp(jax.nn.silu, time_pre)
    time_hidden = silu_value.astype(bf16).astype(f32)
    red_tw2 = contract_rows(time_hidden, every_embed, highest)
    grad_hidden = contract_cols(every_embed, time_w2.astype(bf16).astype(f32), highest)
    grad_time_pre = silu_pull(grad_hidden)[0]
    red_tb1 = jnp.sum(grad_time_pre, axis=0)
    red_tw1 = contract_rows(every_feat, grad_time_pre, highest)
    red_tb2 = lax.dynamic_slice(jnp.sum(every_embed, axis=0), (slice_start,), (own_slice,))
    hidden_width = b_up.shape[0]
    return (
        outputs_own.astype(bf16),
        grad_inputs,
        red_tw1,
        red_tb1,
        red_tw2,
        red_tb2,
        red_qkv[:, :head_width],
        tp_vectors[:head_width],
        red_qkv[:, head_width : 2 * head_width],
        red_qkv[:, 2 * head_width :],
        tp_vectors[head_width : 2 * head_width],
        red_out.T,
        own_vectors[0],
        own_vectors[1],
        own_vectors[2],
        red_up,
        tp_vectors[2 * head_width : 2 * head_width + hidden_width],
        red_down.T,
        own_vectors[3],
        own_vectors[4],
        own_vectors[5],
    )


def solution(mesh):
    placed = (
        P("dp", None),
        P(("dp", "tp"), None),
        P("dp", None),
        P("dp", None),
        P(None, ("dp", "tp")),
        P(("dp", "tp")),
        P(("dp", "tp"), None),
        P(("dp", "tp")),
        P("dp", "tp"),
        P("tp"),
        P("dp", "tp"),
        P("dp", "tp"),
        P("tp"),
        P("tp", "dp"),
        P(("dp", "tp")),
        P(("dp", "tp")),
        P(("dp", "tp")),
        P("dp", "tp"),
        P("tp"),
        P("tp", "dp"),
        P(("dp", "tp")),
        P(("dp", "tp")),
        P(("dp", "tp")),
    )
    return jax.shard_map(
        on_device,
        mesh=mesh,
        in_specs=placed,
        out_specs=(
            P(("dp", "tp"), None),
            P("dp", None),
            P(None, ("dp", "tp")),
            P(("dp", "tp")),
            P(("dp", "tp"), None),
            P(("dp", "tp")),
            P("dp", "tp"),
            P("tp"),
            P("dp", "tp"),
            P("dp", "tp"),
            P("tp"),
            P("tp", "dp"),
            P(("dp", "tp")),
            P(("dp", "tp")),
            P(("dp", "tp")),
            P("dp", "tp"),
            P("tp"),
            P("tp", "dp"),
            P(("dp", "tp")),
            P(("dp", "tp")),
            P(("dp", "tp")),
        ),
        check_vma=False,
    )
```

time: 1630 us -> 511 us (0.31)
  waiting for transfers between devices: 1030 us -> 56.5 us
  blocking collectives: 360 us -> 0 us
  Pallas kernels: 0 us -> 194 us
    reduce_scatter x10 -> x3, waiting for transfers between devices: 866 us -> 23.7 us  [the longest x1 10.3 us: on_device(): lax.psum_scatter(contract_cols(grad_up_low, wup).astype(bf16), 'tp', scat...]
    all_gather x5 -> x0, blocking collectives: 207 us -> none  [the longest x1 43.9 us: on_device(): lax.all_gather(time_w1, ('dp', 'tp'), axis=1, tiled=True)]
    pallas_call x0 -> x2, Pallas kernels: none -> 194 us  [the longest x1 102 us: call_gather(): pl.pallas_call(functools.partial(gather_kernel, sub), out_shape=full + [j...]
    all_gather x6 -> x3, waiting for transfers between devices: 143 us -> 24.2 us  [the longest x1 11.1 us: on_device(): lax.all_gather(grad_second.astype(bf16), 'tp', axis=0, tiled=True)]
    psum x1 -> x0, blocking collectives: 77.1 us -> none  [on_device(): lax.psum((grad_b_query, grad_b_value, grad_b_up), 'dp')]
    unnamed x2 -> x0, blocking collectives: 75.6 us -> none
  transfers between devices with their start and end apart: 18 -> 7, of which waited for: 16 -> 7; matrix products, arithmetic and copies ran while one was open for 4% -> 5% of each run, Pallas kernels for 0% -> 0%
where the time goes in v1:
time: 511 us; the launch traced here: 501 us
  Pallas kernels  194 us (38%)
  matrix products  117 us (23%)
  other arithmetic  61.3 us (12%)
  waiting for transfers between devices  56.5 us (11%)
  local copies, waits for them, and re-layouts  44.4 us (9%)
  between operations  16.7 us (3%)
  loops' own time  9.63 us (2%)
    pallas_call x1, Pallas kernels, call_gather(): pl.pallas_call(functools.partial(gather_kernel, sub), out_shape=full + [j...  102 us
    pallas_call x1, Pallas kernels, call_reduce(): pl.pallas_call(functools.partial(reduce_kernel, sub), out_shape=[jax.Shap...  92.9 us
    dot_general x7, matrix products, contract_rows(): lax.dot_general(left_side, right_side, (((0,), (0,)), ((), ())), precisio...  20 us
    unnamed x114, local copies, waits for them, and re-layouts  17.4 us
    dot_general x5, matrix products, contract_cols(): lax.dot_general(left_side, right_side, (((1,), (1,)), ((), ())), precisio...  16.5 us
    dot_general x2, matrix products, one_block(): jnp.einsum('hqk,qhd->khd', prob_low, grad_blk, preferred_element_type=jnp...  11.6 us
    all_gather x1, waiting for transfers between devices, on_device(): lax.all_gather(grad_second.astype(bf16), 'tp', axis=0, tiled=True)  11.1 us
    all_gather x1, waiting for transfers between devices, on_device(): first_all = lax.all_gather(first_out.astype(bf16), 'tp', axis=0, tiled=True)  11.1 us
  transfers between devices with their start and end apart: 7, of which 7 were waited for; matrix products, arithmetic and copies ran while one was open for 5% of the time, Pallas kernels for 0%

profile of v1, /device:TPU:0, one launch (start us, length us, event | category | flops | bytes accessed | tf_op | source)
XLA Modules:
  0.0 500.9 jit_solution(14663076924929147386)
XLA Ops:
  21.1 101.6 %gather_weights.1 = (bf16[768,1152]{1,0:T(8,128)(2,1)S(1)}, bf16[768,384]{1,0:T(8,128)(2,1)S(1)}, bf16[768,1536]{1,0:T(8,128)(2,1)S(1)}, bf16[768,1536]{1,0:T(8,...) custom-call(bf16[48,1152]{1,0:T(8,128)(2,1)S(1)} %pad_maximum_fusion.1.w0, ...), custom_call_target="tpu_custom_call" | custom-call | tf_op jit(solution)/shard_map/gather_weights/pallas_call | solution.py:359
  122.8 4.6 fusion.52
  142.0 30.6 %while.28 = (s32[]{:T(128)}, bf16[2,512,384]{2,1,0:T(8,128)(2,1)}, f32[2,6,512]{2,1,0:T(8,128)S(1)}, s32[2,512]{1,0:T(2,128)S(1)}, bf16[2,512,6,64]{1,3,2,0:T(8,...) while((s32[]{:T(128)}, bf16[2,512,384]{2,1,0:T(8,128)(2,1)}, ...), condition=%wide.region_3.4_spmd.clone, body=%wide.region_0.3_spmd.clone.sunk | while | flops 843777024 | bytes 47048864 | solution.py:509
  143.0 3.6 fusion.138
  150.3 5.0 fusion.140
  165.7 5.0 fusion.140
  176.4 3.7 select_add_fusion
  180.1 4.3 reduce-scatter.4.cloned.1.call-done
  188.8 11.1 %all-gather.4.cloned.1.call-done = bf16[1024,768]{1,0:T(8,128)(2,1)} async-done(((bf16[512,768]{1,0:T(8,128)(2,1)}), bf16[1024,768]{1,0:T(8,128)(2,1)}) %all-gather.4.cloned.1.call-update) | async-done | bytes 1572880 | tf_op jit(solution)/shard_map/all_gather | solution.py:648
  199.9 4.2 fusion.92
  206.8 5.0 %convolution_convert_fusion.5 = bf16[1024,768]{1,0:T(8,128)(2,1)} fusion(bf16[768,1536]{1,0:T(8,128)(2,1)S(1)} %copy-done.10, f32[1024,1536]{1,0:T(8,128)S(1)} %fusion.92, f32[1536]{0:T(1024)S(1)} %copy-done.55), kind=kOutput, calls=%fused_computation.71 | convolution fusion | flops 2432434176 | bytes 10229760 | tf_op jit(solution)/shard_map/dot_general | solution.py:452
  213.2 9.0 %reduce-scatter.6.cloned.1.call-done = bf16[512,768]{1,0:T(8,128)(2,1)} async-done(((bf16[1024,768]{1,0:T(8,128)(2,1)}), bf16[512,768]{1,0:T(8,128)(2,1)}) %reduce-scatter.6.cloned.1.call-update) | async-done | bytes 786448 | tf_op jit(solution)/shard_map/reduce_scatter | solution.py:653
  228.2 11.1 %all-gather.6.cloned.1.call-done = bf16[1024,768]{1,0:T(8,128)(2,1)} async-done(((bf16[512,768]{1,0:T(8,128)(2,1)}), bf16[1024,768]{1,0:T(8,128)(2,1)}) %all-gather.6.cloned.1.call-update) | async-done | bytes 1572880 | tf_op jit(solution)/shard_map/all_gather | solution.py:664
  239.3 9.3 %fusion.79 = (f32[1536]{0:T(1024)}, bf16[1024,1536]{1,0:T(8,128)(2,1)S(1)}) fusion(f32[1024,1536]{1,0:T(8,128)} %copy-done.57, f32[1536]{0:T(1024)S(1)} %copy-done.55, bf16[1024,768]{1,0:T(8,128)(2,1)} %all-gather.6.cloned.1.call-done, bf16[768,1536]{1,0:T(8,128)(2,1)} %copy-done.9), kind=kOutput, calls=%fused_computation.172 | convolution fusion | flops 2450520576 | bytes 13381632 | tf_op jit(solution)/shard_map/dot_general | solution.py:666
  250.3 3.7 convolution_convert_fusion.4
  254.1 10.3 %reduce-scatter.8.cloned.1.call-done = bf16[512,768]{1,0:T(8,128)(2,1)} async-done(((bf16[1024,768]{1,0:T(8,128)(2,1)}), bf16[512,768]{1,0:T(8,128)(2,1)}) %reduce-scatter.8.cloned.1.call-update) | async-done | bytes 786448 | tf_op jit(solution)/shard_map/reduce_scatter | solution.py:671
  273.0 7.2 %convolution_convert_fusion.g3 = bf16[768,1536]{1,0:T(8,128)(2,1)} fusion(bf16[1024,768]{1,0:T(8,128)(2,1)S(1)} %copy-done.53, f32[1024,1536]{1,0:T(8,128)} %copy-done.57, f32[1536]{0:T(1024)S(1)} %copy-done.55), kind=kOutput, calls=%fused_computation.64 | convolution fusion | flops 2432827392 | bytes 10229760 | tf_op jit(solution)/shard_map/dot_general | solution.py:442
  286.4 66.4 %while.29 = (s32[]{:T(128)}, f32[1024,6,64]{0,2,1:T(8,128)}, f32[1024,6,64]{0,2,1:T(8,128)}, bf16[2,512,384]{2,1,0:T(8,128)(2,1)}, bf16[2,512,6,64]{1,3,2,0:T(8,...) while((s32[]{:T(128)}, f32[1024,6,64]{0,2,1:T(8,128)}, ...), condition=%wide.region_17.18_spmd.clone, body=%wide.region_15.17_spmd.clone.sunk | while | flops 2063336448 | bytes 140216608 | solution.py:552
  298.5 5.5 %bitcast_add_fusion.5 = f32[1024,6,64]{0,2,1:T(8,128)} fusion(f32[1024,6,64]{0,2,1:T(8,128)} %get-tuple-element.565, f32[6,512,1024]{2,1,0:T(8,128)S(1)} %fusion.150, f32[6,512]{1,0:T(8,128)S(1)} %dynamic-slice_bitcast_fusion.2, pred[512,1024]{1,0:T(8,128)(4,1)S(1)} %broadcast_compare_fusion.5, pred[]{:T(512)S(6)} %compare.6, ...), kind=kOutput, calls=%fused_computation.28.clone.1 | convolution fusion | flops 416022528 | bytes 16658437 | tf_op jit(solution)/shard_map/while/body/eval_jaxpr/hqk,qhd->khd/dot_general | solution.py:532
  304.0 5.4 %multiply_reduce_fusion.9 = (f32[6,512]{1,0:T(8,128)S(1)}, f32[6,512,1024]{2,1,0:T(8,128)S(1)}) fusion(f32[6,512,1024]{2,1,0:T(8,128)S(1)} %fusion.150, f32[6,512]{1,0:T(8,128)S(1)} %dynamic-slice_bitcast_fusion.2, pred[512,1024]{1,0:T(8,128)(4,1)S(1)} %broadcast_compare_fusion.5, bf16[1024,6,64]{0,2,1:T(8,128)(2,1)} %get-tuple-element.586, ...), kind=kOutput, calls=%fused_computation.23.clone.1 | convolution fusion | flops 418378752 | bytes 26894340 | tf_op jit(solution)/shard_map/while/body/eval_jaxpr/qhd,khd->hqk/dot_general | solution.py:535
  309.4 5.1 %multiply_convert_fusion.7 = bf16[6,512,1024]{2,1,0:T(8,128)(2,1)} fusion(f32[6,512,1024]{2,1,0:T(8,128)S(1)} %get-tuple-element.517, f32[6,512,1024]{2,1,0:T(8,128)S(1)} %fusion.150, f32[6,512]{1,0:T(8,128)S(1)} %get-tuple-element.518, f32[6,512]{1,0:T(8,128)S(1)} %dynamic-slice_bitcast_fusion.2, pred[512,1024]{1,0:T(8,128)(4,1)S(1)} %broadcast_compare_fusion.5), kind=kLoop, calls=%fused_computation.22.clone.1 | loop fusion | flops 18874368 | bytes 32006144 | tf_op jit(solution)/shard_map/while/body/eval_jaxpr/convert_element_type | solution.py:539
  314.5 5.0 convolution_multiply_fusion.2
  326.0 6.0 %bitcast_add_fusion.5 = f32[1024,6,64]{0,2,1:T(8,128)} fusion(f32[1024,6,64]{0,2,1:T(8,128)} %get-tuple-element.565, f32[6,512,1024]{2,1,0:T(8,128)S(1)} %fusion.150, f32[6,512]{1,0:T(8,128)S(1)} %dynamic-slice_bitcast_fusion.2, pred[512,1024]{1,0:T(8,128)(4,1)S(1)} %broadcast_compare_fusion.5, pred[]{:T(512)S(6)} %compare.6, ...), kind=kOutput, calls=%fused_computation.28.clone.1 | convolution fusion | flops 416022528 | bytes 16658437 | tf_op jit(solution)/shard_map/while/body/eval_jaxpr/hqk,qhd->khd/dot_general | solution.py:532
  332.1 5.4 %multiply_reduce_fusion.9 = (f32[6,512]{1,0:T(8,128)S(1)}, f32[6,512,1024]{2,1,0:T(8,128)S(1)}) fusion(f32[6,512,1024]{2,1,0:T(8,128)S(1)} %fusion.150, f32[6,512]{1,0:T(8,128)S(1)} %dynamic-slice_bitcast_fusion.2, pred[512,1024]{1,0:T(8,128)(4,1)S(1)} %broadcast_compare_fusion.5, bf16[1024,6,64]{0,2,1:T(8,128)(2,1)} %get-tuple-element.586, ...), kind=kOutput, calls=%fused_computation.23.clone.1 | convolution fusion | flops 418378752 | bytes 26894340 | tf_op jit(solution)/shard_map/while/body/eval_jaxpr/qhd,khd->hqk/dot_general | solution.py:535
  337.5 5.1 %multiply_convert_fusion.7 = bf16[6,512,1024]{2,1,0:T(8,128)(2,1)} fusion(f32[6,512,1024]{2,1,0:T(8,128)S(1)} %get-tuple-element.517, f32[6,512,1024]{2,1,0:T(8,128)S(1)} %fusion.150, f32[6,512]{1,0:T(8,128)S(1)} %get-tuple-element.518, f32[6,512]{1,0:T(8,128)S(1)} %dynamic-slice_bitcast_fusion.2, pred[512,1024]{1,0:T(8,128)(4,1)S(1)} %broadcast_compare_fusion.5), kind=kLoop, calls=%fused_computation.22.clone.1 | loop fusion | flops 18874368 | bytes 32006144 | tf_op jit(solution)/shard_map/while/body/eval_jaxpr/convert_element_type | solution.py:539
  342.5 5.0 convolution_multiply_fusion.2
  347.5 3.9 bitcast_add_fusion.4
  359.0 3.7 fusion.77
  364.4 5.0 %convolution_convert_fusion.1.g2 = bf16[768,1536]{1,0:T(8,128)(2,1)S(1)} fusion(bf16[1024,768]{1,0:T(8,128)(2,1)} %all-gather.4.cloned.1.call-done, bf16[1024,1536]{1,0:T(8,128)(2,1)} %copy-done.56), kind=kOutput, calls=%fused_computation.65 | convolution fusion | flops 2417098752 | bytes 7077888 | tf_op jit(solution)/shard_map/dot_general | solution.py:442
  373.7 3.7 convolution_convert_fusion.2.g0
  377.5 8.6 %all-reduce.2.cloned.1.call-done = bf16[1024,768]{1,0:T(8,128)(2,1)} async-done(((bf16[1024,768]{1,0:T(8,128)(2,1)}), bf16[1024,768]{1,0:T(8,128)(2,1)}) %all-reduce.2.cloned.1.call-update) | async-done | bytes 1572880 | tf_op jit(solution)/shard_map/psum | solution.py:692
  389.1 92.9 %reduce_gradients.1 = (f32[48,1152]{1,0:T(8,128)S(1)}, f32[48,384]{1,0:T(8,128)S(1)}, f32[48,1536]{1,0:T(8,128)S(1)}, f32[48,1536]{1,0:T(8,128)S(1)}, f32[16,768]{1,0:T(8,128)S(1)}, /*index=5*/f32[4,8,768]{2,1,0:T(8,128)S(1)}) custom-call(bf16[768,1152]{1,0:T(8,128)(2,1)S(1)} %copy-done, bf16[768,384]{1,0:T(8,128)(2,1)S(1)} %convolution_convert_fusion.7.g1, ...), custom_call_target="tpu_custom_call" | custom-call | tf_op jit(solution)/shard_map/reduce_gradients/pallas_call | solution.py:400
  (269 shorter events, 115.5 us)
Async XLA Ops:
  7.2 177.2 %reduce-scatter.4.cloned.1.call-start = ((), (), s32[]{:S(2)}) async-start(), calls=%async_computation.3 | async-start | bytes 2359296 | tf_op jit(solution)/shard_map/reduce_scatter | solution.py:641
  10.5 165.8 %copy-start.46 = (pred[1024]{0:T(1024)(128)(4,1)}, pred[1024]{0:T(1024)(128)(4,1)S(1)}, u32[]{:S(2)}) copy-start(pred[1024]{0:T(1024)(128)(4,1)S(1)} %get-tuple-element.379) | copy-start | bytes 3076
  10.5 165.8 %copy-start.48 = (pred[1024]{0:T(1024)(128)(4,1)}, pred[1024]{0:T(1024)(128)(4,1)S(1)}, u32[]{:S(2)}) copy-start(pred[1024]{0:T(1024)(128)(4,1)S(1)} %get-tuple-element.380) | copy-start | bytes 3076
  122.7 4.7 copy-start.9
  122.7 148.4 %copy-start.5 = (f32[4,8,128]{2,1,0:T(8,128)}, f32[4,8,128]{2,1,0:T(8,128)S(1)}, u32[]{:S(2)}) copy-start(f32[4,8,128]{2,1,0:T(8,128)S(1)} %get-tuple-element.147) | copy-start | bytes 49156
  122.7 53.6 %copy-start.37 = (f32[768]{0:T(1024)}, f32[768]{0:T(1024)S(1)}, u32[]{:S(2)}) copy-start(f32[768]{0:T(1024)S(1)} %get-tuple-element.297) | copy-start | bytes 9220
  122.7 53.6 %copy-start.39 = (f32[768]{0:T(1024)}, f32[768]{0:T(1024)S(1)}, u32[]{:S(2)}) copy-start(f32[768]{0:T(1024)S(1)} %get-tuple-element.298) | copy-start | bytes 9220
  122.7 5.6 %copy-start.50 = (f32[384]{0:T(512)S(1)}, f32[384]{0:T(512)}, u32[]{:S(2)}) copy-start(f32[384]{0:T(512)} %param.39) | copy-start | bytes 4612
  122.8 5.6 %copy-start.51 = (f32[384]{0:T(512)S(1)}, f32[384]{0:T(512)}, u32[]{:S(2)}) copy-start(f32[384]{0:T(512)} %param.36) | copy-start | bytes 4612
  176.0 24.0 %all-gather.4.cloned.1.call-start = ((), (), s32[]{:S(2)}) async-start(), calls=%async_computation.4 | async-start | bytes 2359296 | tf_op jit(solution)/shard_map/all_gather | solution.py:648
  188.8 33.4 %reduce-scatter.6.cloned.1.call-start = ((), (), s32[]{:S(2)}) async-start(), calls=%async_computation.5 | async-start | bytes 2359296 | tf_op jit(solution)/shard_map/reduce_scatter | solution.py:653
  199.9 6.8 %copy-start.10 = (bf16[768,1536]{1,0:T(8,128)(2,1)S(1)}, bf16[768,1536]{1,0:T(8,128)(2,1)}, u32[]{:S(2)}) copy-start(bf16[768,1536]{1,0:T(8,128)(2,1)} %copy-done.9) | copy-start | bytes 7077892
  199.9 6.8 %copy-start.55 = (f32[1536]{0:T(1024)S(1)}, f32[1536]{0:T(1024)}, u32[]{:S(2)}) copy-start(f32[1536]{0:T(1024)} %param.45) | copy-start | bytes 18436
  211.8 27.5 %all-gather.6.cloned.1.call-start = ((), (), s32[]{:S(2)}) async-start(), calls=%async_computation.6 | async-start | bytes 2359296 | tf_op jit(solution)/shard_map/all_gather | solution.py:664
  228.2 36.3 %reduce-scatter.8.cloned.1.call-start = ((), (), s32[]{:S(2)}) async-start(), calls=%async_computation.7 | async-start | bytes 2359296 | tf_op jit(solution)/shard_map/reduce_scatter | solution.py:671
  254.0 10.4 %copy-start.17 = (f32[512,768]{1,0:T(8,128)S(1)}, f32[512,768]{1,0:T(8,128)}, u32[]{:S(2)}) copy-start(f32[512,768]{1,0:T(8,128)} %copy-done.16) | copy-start | bytes 4718596
  254.1 28.1 %all-gather.8.cloned.1.call-start = ((), (), s32[]{:S(2)}) async-start(), calls=%async_computation.8 | async-start | bytes 2359296 | tf_op jit(solution)/shard_map/all_gather | solution.py:676
  271.0 115.1 %all-reduce.2.cloned.1.call-start = ((), (), s32[]{:S(2)}) async-start(), calls=%async_computation.9 | async-start | bytes 3145728 | tf_op jit(solution)/shard_map/psum | solution.py:692
  314.5 5.0 copy-start.13
  342.5 5.0 copy-start.13
  354.7 14.8 %copy-start.23 = (bf16[1024,384]{1,0:T(8,128)(2,1)}, bf16[1024,384]{1,0:T(8,128)(2,1)S(1)}, u32[]{:S(2)}) copy-start(bf16[1024,384]{1,0:T(8,128)(2,1)S(1)} %copy.74) | copy-start | bytes 2359300
  364.3 5.1 %copy-start.45 = (f32[1536]{0:T(1024)S(1)}, f32[1536]{0:T(1024)}, u32[]{:S(2)}) copy-start(f32[1536]{0:T(1024)} %get-tuple-element.341) | copy-start | bytes 18436
  364.3 5.1 %copy-start.35 = (f32[768]{0:T(1024)S(1)}, f32[768]{0:T(1024)}, u32[]{:S(2)}) copy-start(f32[768]{0:T(1024)} %get-tuple-element.282) | copy-start | bytes 9220
  364.4 5.1 %copy-start.36 = (f32[768]{0:T(1024)S(1)}, f32[768]{0:T(1024)}, u32[]{:S(2)}) copy-start(f32[768]{0:T(1024)} %get-tuple-element.343) | copy-start | bytes 9220
  364.4 5.1 %copy-start.34 = (f32[768]{0:T(1024)S(1)}, f32[768]{0:T(1024)}, u32[]{:S(2)}) copy-start(f32[768]{0:T(1024)} %get-tuple-element.287) | copy-start | bytes 9220
  364.4 5.1 %copy-start.33 = (f32[768]{0:T(1024)S(1)}, f32[768]{0:T(1024)}, u32[]{:S(2)}) copy-start(f32[768]{0:T(1024)} %get-tuple-element.288) | copy-start | bytes 9220
  373.7 12.3 %copy-start.44 = (s32[512]{0:T(512)S(1)}, s32[512]{0:T(512)}, u32[]{:S(2)}) copy-start(s32[512]{0:T(512)} %get-tuple-element.348) | copy-start | bytes 6148
  373.7 13.8 %copy-start.42 = (f32[1,768]{1,0:T(1,128)S(1)}, f32[1,768]{1,0:T(1,128)}, u32[]{:S(2)}) copy-start(f32[1,768]{1,0:T(1,128)} %stack.57) | copy-start | bytes 9220
  373.7 13.8 %copy-start.43 = (f32[1,768]{1,0:T(1,128)S(1)}, f32[1,768]{1,0:T(1,128)}, u32[]{:S(2)}) copy-start(f32[1,768]{1,0:T(1,128)} %stack.58) | copy-start | bytes 9220
  389.1 93.7 %copy-start.4 = (f32[24,768]{1,0:T(8,128)S(1)}, f32[24,768]{1,0:T(8,128)}, u32[]{:S(2)}) copy-start(f32[24,768]{1,0:T(8,128)} %tw2.1) | copy-start | bytes 221188
  389.1 93.7 %copy-start.32 = (f32[32,24]{0,1:T(8,128)S(1)}, f32[32,24]{0,1:T(8,128)}, u32[]{:S(2)}) copy-start(f32[32,24]{0,1:T(8,128)} %convolution_add_fusion) | copy-start | bytes 9220
  389.1 98.4 %copy-start.6 = (f32[4,8,128]{2,1,0:T(8,128)S(1)}, f32[4,8,128]{2,1,0:T(8,128)}, u32[]{:S(2)}) copy-start(f32[4,8,128]{2,1,0:T(8,128)} %copy-done.5) | copy-start | bytes 49156
  (37 other events, 87.5 us)
Sparse Core Ops, SparseCore 0:
  176.1 8.2 reduce-scatter.3
  188.9 10.9 all-gather.3
  211.9 10.2 reduce-scatter.5
  228.3 11.0 all-gather.5
  254.2 10.2 reduce-scatter.7
  271.1 10.9 all-gather.7
  364.5 21.5 all-reduce.1

commit v2 on v1

v2 whole, which is shorter than its diff:
```python
import functools
import math
import types

import jax
import jax.numpy as jnp
from jax import lax
from jax.experimental import pallas as pl
from jax.experimental.pallas import tpu as pltpu
from jax.sharding import PartitionSpec as P

HD = 64
TE = 128
SUPER = 16

epsilon = 1e-05
highest = lax.Precision.HIGHEST
f32 = jnp.float32
bf16 = jnp.bfloat16


class Place:
    def __init__(self, sub):
        self.sub = sub
        index = lax.axis_index("dp")
        self.low = lax.rem(index, sub)
        self.place = lax.div(index, sub)
        self.z = lax.div(self.place, 4)
        self.p = lax.rem(self.place, 4)
        self.r = self.ring(self.p)

    @staticmethod
    def ring(v):
        half = lax.div(v, 2)
        return 2 * half + lax.rem(lax.rem(v, 2) + half, 2)

    def spot(self, dz, dr):
        z = lax.rem(self.z + dz + 4, 4)
        p = self.ring(lax.rem(self.r + dr + 4, 4))
        return z * 4 + p

    def device(self, dz, dr):
        return {"dp": self.spot(dz, dr) * self.sub + self.low}

    def other(self):
        return {"tp": 1 - lax.axis_index("tp")}

    def rows(self, dz, dr, count):
        return pl.ds(pl.multiple_of(self.spot(dz, dr) * count, 16), count)

    def enter(self):
        barrier = pltpu.get_barrier_semaphore()
        for peer in (
            [self.device(d, 0) for d in (1, 2, 3)]
            + [self.device(0, d) for d in (1, 2, 3)]
            + [self.other()]
        ):
            pl.semaphore_signal(barrier, inc=1, device_id=peer, device_id_type=pl.DeviceIdType.MESH)
        pl.semaphore_wait(barrier, 7)


def remote(src, dst, send, recv, device):
    return pltpu.make_async_remote_copy(
        src_ref=src,
        dst_ref=dst,
        send_sem=send,
        recv_sem=recv,
        device_id=device,
        device_id_type=pl.DeviceIdType.MESH,
    )


def many(k, name, g):
    return getattr(k, name + str(g))


class Gather:
    def __init__(self, place, shard, full, send, recv, g):
        rows = shard.shape[0]
        at = lambda dz, dr: full.at[place.rows(dz, dr, rows), :]
        self.place, self.shard, self.full, self.count = place, shard, full, rows
        self.to_planes = [
            remote(shard, at(0, 0), send.at[g, d - 1], recv.at[g, d - 1], place.device(d, 0))
            for d in (1, 2, 3)
        ]
        self.around = []
        self.relay = []
        for d in range(4):
            source = shard if d == 0 else at(-d, 0)
            self.around.append(
                [
                    remote(
                        source,
                        at(-d, 0),
                        send.at[g, 3 + 2 * d + k],
                        recv.at[g, 3 + 2 * d + k],
                        place.device(0, 1 - 2 * k),
                    )
                    for k in (0, 1)
                ]
            )
            k = d // 2
            self.relay.append(
                remote(
                    at(-d, 2 * k - 1),
                    at(-d, 2 * k - 1),
                    send.at[g, 11 + d],
                    recv.at[g, 11 + d],
                    place.device(0, 1 - 2 * k),
                )
            )

    def begin(self):
        for copy in self.to_planes:
            copy.start()
        for copy in self.around[0]:
            copy.start()
        self.full[self.place.rows(0, 0, self.count), :] = self.shard[...]

    def turn(self):
        for d in (1, 2, 3):
            self.to_planes[d - 1].wait_recv()
            for copy in self.around[d]:
                copy.start()

    def pass_on(self):
        for d in range(4):
            self.around[d][d // 2].wait_recv()
            self.relay[d].start()

    def finish(self):
        for d in range(4):
            self.around[d][1 - d // 2].wait_recv()
            self.relay[d].wait_recv()

    def drain(self):
        for copy in self.to_planes + [c for pair in self.around for c in pair] + self.relay:
            copy.wait_send()


class Reduce:
    def __init__(self, place, grads, total, first, second, third, send, recv, g):
        rows = total.shape[0]
        at = lambda dz, dr: grads.at[place.rows(dz, dr, rows), :]
        self.place, self.grads, self.total, self.rows = place, grads, total, rows
        self.first, self.second, self.third = first, second, third
        self.far, self.near, self.up = [], [], []
        for d in range(4):
            k = d // 2
            self.far.append(
                remote(
                    at(d, 2), first.at[d], send.at[g, d], recv.at[g, d], place.device(0, 1 - 2 * k)
                )
            )
            self.near.append(
                [
                    remote(
                        at(d, 1 - 2 * j),
                        second.at[j * 4 + d],
                        send.at[g, 4 + 2 * d + j],
                        recv.at[g, 4 + 2 * d + j],
                        place.device(0, 1 - 2 * j),
                    )
                    for j in (0, 1)
                ]
            )
        for d in (1, 2, 3):
            self.up.append(
                remote(
                    at(d, 0),
                    third.at[d - 1],
                    send.at[g, 11 + d],
                    recv.at[g, 11 + d],
                    place.device(d, 0),
                )
            )

    def begin(self):
        for d in range(4):
            self.far[d].start()
        for d in range(4):
            self.near[d][1 - d // 2].start()

    def join(self):
        for d in range(4):
            k = d // 2
            self.far[d].wait_recv()
            rows = self.place.rows(d, 1 - 2 * k, self.rows)
            self.grads[rows, :] = (self.grads[rows, :].astype(f32) + self.first[d].astype(f32)).astype(bf16)
            self.near[d][k].start()

    def cross(self):
        for d in (1, 2, 3, 0):
            for j in (0, 1):
                self.near[d][j].wait_recv()
            rows = self.place.rows(d, 0, self.rows)
            summed = (
                self.grads[rows, :].astype(f32)
                + self.second[d].astype(f32)
                + self.second[4 + d].astype(f32)
            )
            if d:
                self.grads[rows, :] = summed.astype(bf16)
                self.up[d - 1].start()
            else:
                self.total[...] = summed

    def finish(self):
        for copy in self.up:
            copy.wait_recv()
        self.total[...] += (
            self.third[0].astype(f32) + self.third[1].astype(f32) + self.third[2].astype(f32)
        )

    def drain(self):
        for copy in self.far + [c for pair in self.near for c in pair] + self.up:
            copy.wait_send()


class Spread:
    def __init__(self, place, along, sources, slots, send, recv, base):
        rows = slice(0, sources[0].shape[0])
        if along == "tp":
            self.copies = [
                remote(sources[0], slots.at[rows], send.at[base], recv.at[base], place.other())
            ]
            return
        self.copies = [
            remote(
                sources[d - 1],
                slots.at[d - 1, rows],
                send.at[base + d - 1],
                recv.at[base + d - 1],
                place.device(d, 0) if along == "z" else place.device(0, d),
            )
            for d in (1, 2, 3)
        ]

    def start(self):
        for copy in self.copies:
            copy.start()

    def wait(self):
        for copy in self.copies:
            copy.wait_recv()

    def drain(self):
        for copy in self.copies:
            copy.wait_send()


def mul(a, b):
    return lax.dot_general(a, b, (((1,), (0,)), ((), ())), preferred_element_type=f32)


def mul_t(a, b):
    return lax.dot_general(a, b, (((1,), (1,)), ((), ())), preferred_element_type=f32)


def fold(x):
    return jnp.sum(x.reshape(x.shape[0] // 8, 8, x.shape[1]), axis=0)


def mean(x):
    return jnp.mean(x, axis=-1, keepdims=True)


PAIR = 2 * HD
TOP = math.sqrt(2.0 / math.pi)


def layer_kernel(sub, names, *refs):
    k = types.SimpleNamespace(**dict(zip(names, refs, strict=True)))
    place = Place(sub)
    side = lax.axis_index("tp")
    x_ref = k.x
    total_rows, width = x_ref.shape
    half = total_rows // 2
    tp_send, tp_recv = k.tp_send, k.tp_recv
    seqs = k.feats.shape[0]
    pairs = k.mixed.shape[1] // PAIR
    hidden_width = k.bup.shape[1]
    own0 = pl.multiple_of(side * half, half)
    far0 = pl.multiple_of((1 - side) * half, half)
    first_len = k.lengths[0, 0]
    both_len = first_len + k.lengths[0, 1]

    def segment(start, count):
        row = lax.broadcasted_iota(jnp.int32, (count, 1), 0) + start
        return jnp.where(row < first_len, 0, jnp.where(row < both_len, 1, 2))

    def swap(n, src, dst):
        return remote(src, dst, tp_send.at[n], tp_recv.at[n], place.other())

    place.enter()
    small_send, small_recv = k.small_send, k.small_recv
    spread_z = Spread(place, "z", [k.feats] * 3, k.feat_z, small_send, small_recv, 0)
    spread_z.start()
    gathers = [
        Gather(place, many(k, "w", g), many(k, "full", g), k.g_send, k.g_recv, g) for g in range(4)
    ]
    gathers[0].begin()
    spread_z.wait()
    k.feat_sum[...] = k.feats[...] + k.feat_z[0] + k.feat_z[1] + k.feat_z[2]
    spread_r = Spread(place, "r", [k.feat_sum] * 3, k.feat_in, small_send, small_recv, 3)
    spread_r.start()
    k.all_feats[0] = k.feat_sum[...]
    spread_r.wait()
    for d in (1, 2, 3):
        k.all_feats[d] = k.feat_in[d - 1]
    every = k.all_feats[...].reshape(4 * seqs, TE)
    before = mul(every.astype(bf16), k.tw1[...].astype(bf16)) + k.tb1[...]
    hidden = jax.nn.silu(before).astype(bf16)
    share = mul(hidden, k.tw2[...].astype(bf16))
    part = k.part
    for d in range(4):
        part[d, :seqs, :] = share[d * seqs : (d + 1) * seqs, :]
        part[d, seqs : seqs + 8, :] = k.vectors[...]
    top = slice(0, seqs + 8)
    back = Spread(
        place, "r", [part.at[n, top] for n in (3, 2, 1)], k.part_in, small_send, small_recv, 6
    )
    back.start()
    back.wait()
    in_plane = k.part_in
    k.part_sum[top] = part[0, top] + in_plane[0, top] + in_plane[1, top] + in_plane[2, top]
    over_z = Spread(place, "z", [k.part_sum.at[top]] * 3, k.part_z, small_send, small_recv, 9)
    over_z.start()
    gathers[0].turn()
    gathers[1].begin()
    gathers[2].begin()
    over_z.wait()
    from_z = k.part_z
    k.part_zsum[top] = k.part_sum[top] + from_z[0, top] + from_z[1, top] + from_z[2, top]
    pair = Spread(place, "tp", [k.part_zsum.at[top]], k.part_tp, small_send, small_recv, 12)
    pair.start()
    pair.wait()
    both = k.part_zsum[top] + k.part_tp[top]
    shared = k.shared
    shared[...] = both[seqs:]
    embed = both[:seqs] + shared[0:1, :]
    at_row = (place.z * sub + place.low) * 2
    seq_row = lax.broadcasted_iota(jnp.int32, (seqs, 1), 0)
    for s in (0, 1):
        k.embed[s : s + 1, :] = jnp.sum(
            jnp.where(seq_row == at_row + s, embed, 0.0), axis=0, keepdims=True
        )

    for one in (spread_z, spread_r, back, over_z, pair):
        one.drain()

    def vector(n):
        return shared[n : n + 1, :]

    def base_of(start, count):
        seg = segment(start, count)
        added = jnp.where(
            seg == 0, k.embed[0:1, :], jnp.where(seg == 1, k.embed[1:2, :], 0.0)
        )
        return x_ref[pl.ds(start, count), :].astype(f32) + added

    @pl.loop(0, total_rows // 128)
    def _(i):
        start = pl.multiple_of(i * 128, 128)
        k.base[pl.ds(start, 128), :] = base_of(start, 128).astype(bf16)
        seg = segment(start, 128)
        lane = lax.rem(lax.broadcasted_iota(jnp.int32, (1, PAIR), 1), HD)
        k.mask_k[pl.ds(start, 128), :] = jnp.where(lane == seg, 1.0, 0.0).astype(bf16)
        k.mask_q[pl.ds(start, 128), :] = jnp.where((lane < 3) & (lane != seg), -1e30, 0.0).astype(
            bf16
        )

    def transpose(source, dest):
        @pl.loop(0, width // 128)
        def _(i):
            cut = pl.ds(pl.multiple_of(i * 128, 128), 128)
            dest[cut, :] = source[:, cut].T

    transpose(k.base, k.base_t)
    gathers[0].pass_on()
    gathers[0].finish()

    lane = lax.broadcasted_iota(jnp.int32, (1, PAIR), 1)
    lower = lane < HD
    scale = jnp.where(lax.broadcasted_iota(jnp.int32, (1, 3 * PAIR), 1) < PAIR, HD**-0.5, 1.0)
    qkv = k.qkv
    rows_at_once = 256

    def cut_of(j, part_index):
        return slice((3 * j + part_index) * PAIR, (3 * j + part_index + 1) * PAIR)

    def projection(j):
        cols = slice(3 * j * PAIR, 3 * (j + 1) * PAIR)

        @pl.loop(0, total_rows // 512)
        def _(i):
            rows = pl.ds(pl.multiple_of(i * 512, 512), 512)
            got = (mul(k.base[rows, :], k.full0[:, cols]) + k.bqkv[:, cols]) * scale
            qkv[rows, cols] = got.astype(bf16)

    def in_head(h):
        return lower if h == 0 else jnp.logical_not(lower)

    def with_mask(value, mask, h):
        return jnp.where(in_head(h), value.astype(f32), mask.astype(f32)).astype(bf16)

    def attend(j):
        for h in (0, 1):
            k.keys[h] = with_mask(qkv[:, cut_of(j, 1)], k.mask_k[...], h)

        @pl.loop(0, total_rows // rows_at_once)
        def _(i):
            rows = pl.ds(pl.multiple_of(i * rows_at_once, rows_at_once), rows_at_once)
            outs, logs = [], []
            for h in (0, 1):
                query = with_mask(qkv[rows, cut_of(j, 0)], k.mask_q[rows, :], h)
                scores = mul_t(query, k.keys[h])
                top = jnp.max(scores, axis=-1, keepdims=True)
                weight = jnp.exp(scores - top)
                total = jnp.sum(weight, axis=-1, keepdims=True)
                outs.append(mul(weight.astype(bf16), qkv[:, cut_of(j, 2)]) / total)
                logs.append(top + jnp.log(total))
            k.mixed[rows, j * PAIR : (j + 1) * PAIR] = jnp.where(lower, outs[0], outs[1]).astype(bf16)
            k.lse[rows, :] = jnp.where(lower, logs[0], logs[1])

        flipped = k.lse[...].T
        k.lse_t[j, 0:1, :] = flipped[0:1, :]
        k.lse_t[j, 1:2, :] = flipped[HD : HD + 1, :]

    projection(0)
    gathers[1].turn()
    gathers[2].turn()
    gathers[3].begin()
    projection(1)
    projection(2)
    attend(0)
    gathers[1].pass_on()
    gathers[2].pass_on()
    attend(1)
    gathers[3].turn()
    attend(2)
    for j in range(3, pairs):
        attend(j)
    gathers[1].finish()
    gathers[3].pass_on()

    block = 256

    @pl.loop(0, half // block)
    def _(i):
        rows = pl.ds(pl.multiple_of(far0 + i * block, block), block)
        k.half_send[pl.ds(pl.multiple_of(i * block, block), block), :] = mul_t(
            k.mixed[rows, :], k.full1[...]
        ).astype(bf16)

    swap_a = swap(0, k.half_send, k.half_recv)
    swap_a.start()
    first_own, normed_one, inv_one = k.first_own, k.normed_one, k.inv_one

    @pl.loop(0, half // block)
    def _(i):
        here = pl.ds(pl.multiple_of(i * block, block), block)
        start = pl.multiple_of(own0 + i * block, block)
        first_own[here, :] = (
            base_of(start, block) + vector(1) + mul_t(k.mixed[pl.ds(start, block), :], k.full1[...])
        )

    swap_a.wait_recv()
    small = 128

    @pl.loop(0, half // small)
    def _(i):
        here = pl.ds(pl.multiple_of(i * small, small), small)
        summed = first_own[here, :] + k.half_recv[here, :].astype(f32)
        centered = summed - mean(summed)
        inv = lax.rsqrt(mean(centered * centered) + epsilon)
        normed = centered * inv
        first = normed * vector(2) + vector(3)
        first_own[here, :] = first
        normed_one[here, :] = normed
        inv_one[here, :] = jnp.broadcast_to(inv, (small, 128))
        k.first[pl.ds(pl.multiple_of(own0 + i * small, small), small), :] = first.astype(bf16)

    own = pl.ds(own0, half)
    far = pl.ds(far0, half)
    swap_b = swap(1, k.first.at[own, :], k.first.at[own, :])
    swap_b.start()
    gathers[2].finish()
    chunk = 512
    blocks = hidden_width // chunk

    def rise(start):
        rows = pl.ds(start, half)

        @pl.loop(0, blocks)
        def _(i):
            cols = pl.ds(pl.multiple_of(i * chunk, chunk), chunk)
            up = mul(k.first[rows, :], k.full2[:, cols]) + k.bup[:, cols]
            square = up * up
            inner = up * (TOP + (TOP * 0.044715) * square)
            gate = 0.5 + 0.5 * jnp.tanh(inner)
            act = up * gate
            slope = gate + act * (1.0 - gate) * (2.0 * TOP + (6.0 * TOP * 0.044715) * square)
            k.act[rows, cols] = act.astype(bf16)
            k.slope[rows, cols] = slope.astype(bf16)

    rise(own0)
    swap_a.wait_send()
    swap_b.wait_recv()
    rise(far0)
    transpose(k.first, k.first_t)
    gathers[3].finish()

    @pl.loop(0, half // block)
    def _(i):
        rows = pl.ds(pl.multiple_of(far0 + i * block, block), block)
        k.half_send[pl.ds(pl.multiple_of(i * block, block), block), :] = mul_t(
            k.act[rows, :], k.full3[...]
        ).astype(bf16)

    swap_c = swap(2, k.half_send, k.half_recv)
    swap_c.start()
    own_sum = first_own

    @pl.loop(0, half // block)
    def _(i):
        here = pl.ds(pl.multiple_of(i * block, block), block)
        rows = pl.ds(pl.multiple_of(own0 + i * block, block), block)
        own_sum[here, :] = mul_t(k.act[rows, :], k.full3[...]) + first_own[here, :] + vector(4)

    swap_c.wait_recv()
    swap_b.wait_send()
    acc = k.acc
    acc[...] = jnp.zeros_like(acc)

    @pl.loop(0, half // small)
    def _(i):
        here = pl.ds(pl.multiple_of(i * small, small), small)
        summed = own_sum[here, :] + k.half_recv[here, :].astype(f32)
        centered = summed - mean(summed)
        inv = lax.rsqrt(mean(centered * centered) + epsilon)
        normed = centered * inv
        k.out[here, :] = (normed * vector(5) + vector(6)).astype(bf16)
        start = pl.multiple_of(own0 + i * small, small)
        grad = jnp.where(segment(start, small) < 2, k.cot[here, :].astype(f32), 0.0)
        scaled = grad * vector(5)
        second = inv * (scaled - mean(scaled) - normed * mean(scaled * normed))
        own_sum[here, :] = second
        k.base[pl.ds(start, small), :] = second.astype(bf16)
        acc[0] += fold(grad * normed)
        acc[1] += fold(grad)
        acc[2] += fold(second)

    swap_d = swap(3, k.base.at[own, :], k.base.at[own, :])
    swap_d.start()
    acc_up = k.acc_up
    acc_up[...] = jnp.zeros_like(acc_up)

    def fall(start):
        rows = pl.ds(start, half)

        @pl.loop(0, blocks)
        def _(i):
            cols = pl.ds(pl.multiple_of(i * chunk, chunk), chunk)
            grad = mul(k.base[rows, :], k.full3[:, cols]) * k.slope[rows, cols].astype(f32)
            k.slope[rows, cols] = grad.astype(bf16)
            acc_up[:, cols] += fold(grad)

    reduces = [
        Reduce(
            place, many(k, "grad", g), many(k, "total", g), many(k, "near", g), many(k, "ring", g), many(k, "high", g),
            k.r_send, k.r_recv, g,
        )
        for g in range(3 + pairs)
    ]

    def weight_grad(g, left_t, right, first_col, count, step):
        @pl.loop(0, count // step)
        def _(i):
            cols = pl.ds(pl.multiple_of(i * step, step), step)
            source = pl.ds(pl.multiple_of(first_col + i * step, 128), step)
            many(k, "grad", g)[:, cols] = mul(left_t[...], right[:, source]).astype(bf16)

    fall(own0)
    swap_c.wait_send()
    swap_d.wait_recv()
    transpose(k.base, k.grad_t)
    weight_grad(0, k.grad_t, k.act, 0, hidden_width, chunk)
    reduces[0].begin()
    fall(far0)

    @pl.loop(0, half // block)
    def _(i):
        rows = pl.ds(pl.multiple_of(far0 + i * block, block), block)
        k.half_send[pl.ds(pl.multiple_of(i * block, block), block), :] = mul_t(
            k.slope[rows, :], k.full2[...]
        ).astype(bf16)

    swap_e = swap(4, k.half_send, k.half_recv)
    swap_e.start()

    @pl.loop(0, half // block)
    def _(i):
        here = pl.ds(pl.multiple_of(i * block, block), block)
        rows = pl.ds(pl.multiple_of(own0 + i * block, block), block)
        own_sum[here, :] += mul_t(k.slope[rows, :], k.full2[...])

    swap_e.wait_recv()

    @pl.loop(0, half // small)
    def _(i):
        here = pl.ds(pl.multiple_of(i * small, small), small)
        grad = own_sum[here, :] + k.half_recv[here, :].astype(f32)
        normed = normed_one[here, :]
        scaled = grad * vector(2)
        r1 = inv_one[here, 0:1] * (scaled - mean(scaled) - normed * mean(scaled * normed))
        k.first[pl.ds(pl.multiple_of(own0 + i * small, small), small), :] = r1.astype(bf16)
        acc[3] += fold(grad * normed)
        acc[4] += fold(grad)
        acc[5] += fold(r1)

    swap_f = swap(5, k.first.at[own, :], k.first.at[own, :])
    swap_f.start()
    weight_grad(1, k.first_t, k.slope, 0, hidden_width, chunk)
    reduces[1].begin()
    reduces[0].join()
    swap_f.wait_recv()

    @pl.loop(0, total_rows // 512)
    def _(i):
        rows = pl.ds(pl.multiple_of(i * 512, 512), 512)
        k.grad_mixed[rows, :] = mul(k.first[rows, :], k.full1[...]).astype(bf16)

    transpose(k.first, k.grad_t)
    weight_grad(2, k.grad_t, k.mixed, 0, pairs * PAIR, pairs * PAIR)
    reduces[2].begin()

    grad_qkv = k.grad_qkv
    acc_qkv = k.acc_qkv

    def attend_back(j):
        mixed_cut = slice(j * PAIR, (j + 1) * PAIR)
        for h in (0, 1):
            k.keys[h] = with_mask(qkv[:, cut_of(j, 0)], k.mask_q[...], h)
        product = k.grad_mixed[:, mixed_cut].astype(f32) * k.mixed[:, mixed_cut].astype(f32)
        flipped = product.T
        k.inner[0:1, :] = jnp.sum(flipped[:HD], axis=0, keepdims=True)
        k.inner[1:2, :] = jnp.sum(flipped[HD:], axis=0, keepdims=True)
        k.keys_t[...] = qkv[:, cut_of(j, 1)].T
        k.query_t[...] = jnp.zeros_like(k.query_t)

        @pl.loop(0, total_rows // rows_at_once)
        def _(i):
            start = pl.multiple_of(i * rows_at_once, rows_at_once)
            rows = pl.ds(start, rows_at_once)
            grads_v, grads_k, query_t = [], [], []
            for h in (0, 1):
                key = with_mask(qkv[rows, cut_of(j, 1)], k.mask_k[rows, :], h)
                prob = jnp.exp(mul_t(key, k.keys[h]) - k.lse_t[j, h : h + 1, :])
                value = jnp.where(in_head(h), qkv[rows, cut_of(j, 2)].astype(f32), 0.0).astype(bf16)
                grad_prob = mul_t(value, k.grad_mixed[:, mixed_cut])
                grad_score = (prob * (grad_prob - k.inner[h : h + 1, :])).astype(bf16)
                grads_v.append(mul(prob.astype(bf16), k.grad_mixed[:, mixed_cut]))
                grads_k.append(mul(grad_score, qkv[:, cut_of(j, 0)]))
                query_t.append(mul(k.keys_t[h * HD : (h + 1) * HD, rows], grad_score))
            grad_k = jnp.where(lower, grads_k[0], grads_k[1]).astype(bf16)
            grad_v = jnp.where(lower, grads_v[0], grads_v[1]).astype(bf16)
            grad_qkv[rows, cut_of(j, 1)] = grad_k
            grad_qkv[rows, cut_of(j, 2)] = grad_v
            k.query_t[...] += jnp.concatenate(query_t, axis=0)

        grad_qkv[:, cut_of(j, 0)] = (k.query_t[...].T * HD**-0.5).astype(bf16)
        cols = slice(3 * j * PAIR, 3 * (j + 1) * PAIR)
        acc_qkv[:, cols] = fold(grad_qkv[:, cols].astype(f32))
        weight_grad(3 + j, k.base_t, grad_qkv, 3 * j * PAIR, 3 * PAIR, 3 * PAIR)
        reduces[3 + j].begin()

    attend_back(0)
    reduces[0].cross()
    reduces[1].join()
    attend_back(1)
    reduces[2].join()
    reduces[1].cross()
    reduces[2].cross()
    for j in range(2, pairs):
        attend_back(j)
        reduces[1 + j].join()

    in_send, in_recv = k.act.at[:, :width], k.act.at[:, width : 2 * width]

    @pl.loop(0, total_rows // block)
    def _(i):
        rows = pl.ds(pl.multiple_of(i * block, block), block)
        in_send[rows, :] = mul_t(grad_qkv[rows, :], k.full0[...]).astype(bf16)

    swap_g = swap(6, in_send, in_recv)
    swap_g.start()
    for g in range(3, 2 + pairs):
        if g > 3:
            reduces[g].join()
    reduces[0].finish()
    reduces[3].cross()
    swap_g.wait_recv()
    ge = k.acc_ge
    ge[...] = jnp.zeros_like(ge)

    @pl.loop(0, total_rows // small)
    def _(i):
        start = pl.multiple_of(i * small, small)
        rows = pl.ds(start, small)
        grad = (in_send[rows, :].astype(f32) + in_recv[rows, :].astype(f32)) + k.first[rows, :].astype(f32)
        k.grad_in[rows, :] = grad
        seg = segment(start, small)
        ge[0] += fold(jnp.where(seg == 0, grad, 0.0))
        ge[1] += fold(jnp.where(seg == 1, grad, 0.0))

    def row_of(x):
        return jnp.sum(x, axis=0, keepdims=True)

    sums = k.part.at[0]
    sums[...] = jnp.zeros_like(sums)
    for row, n in enumerate((5, 3, 4, 2, 0, 1)):
        sums[row : row + 1, :] = row_of(acc[n])
    up_row = row_of(acc_up[...])
    for n in range(hidden_width // width):
        sums[8 + n : 9 + n, :] = up_row[:, n * width : (n + 1) * width]
    qkv_row = row_of(acc_qkv[...])
    at = 8 + hidden_width // width
    sums[at : at + 1, :] = qkv_row[:, :width]
    sums[at + 1 : at + 2, : qkv_row.shape[1] - width] = qkv_row[:, width:]
    sums[16:, :] = jnp.where(
        seq_row == at_row, row_of(ge[0]), jnp.where(seq_row == at_row + 1, row_of(ge[1]), 0.0)
    )
    pair_sums = Spread(place, "tp", [sums], k.part_tp, small_send, small_recv, 13)
    pair_sums.start()
    reduces[2 + pairs].join()
    pair_sums.wait()
    row = lax.broadcasted_iota(jnp.int32, sums.shape, 0)
    k.part_sum[...] = sums[...] + jnp.where(row < 8, k.part_tp[...], 0.0)
    sums_z = Spread(place, "z", [k.part_sum] * 3, k.part_z, small_send, small_recv, 14)
    sums_z.start()
    for g in range(4, 2 + pairs):
        reduces[g].cross()
    sums_z.wait()
    k.part_zsum[...] = k.part_sum[...] + k.part_z[0] + k.part_z[1] + k.part_z[2]
    sums_r = Spread(place, "r", [k.part_zsum] * 3, k.part_in, small_send, small_recv, 17)
    sums_r.start()
    for g in range(1, 3):
        reduces[g].finish()
    sums_r.wait()
    k.all_sums[...] = (
        k.part_zsum[:16] + k.part_in[0, :16] + k.part_in[1, :16] + k.part_in[2, :16]
    )
    k.all_embed[0] = k.part_zsum[16:]
    for d in (1, 2, 3):
        k.all_embed[d] = k.part_in[d - 1, 16:]
    reduces[2 + pairs].cross()
    for g in range(3, 3 + pairs):
        reduces[g].finish()
    for one in (
        gathers
        + reduces
        + [pair_sums, sums_z, sums_r]
    ):
        one.drain()
    for copy in (swap_d, swap_e, swap_f, swap_g):
        copy.wait_send()


def call_layer(sub, operands):
    rows, width = operands["x"].shape
    half = rows // 2
    heads = operands["w1"].shape[1]
    hidden = operands["bup"].shape[1]
    pairs = heads // PAIR
    seqs = operands["feats"].shape[0]
    mine = operands["w0"].shape[0]
    tall = seqs + 16
    columns = [hidden, hidden, heads] + [3 * PAIR] * pairs
    shape = jax.ShapeDtypeStruct
    results = dict(
        out=shape((half, width), bf16),
        grad_in=shape((rows, width), f32),
        all_feats=shape((4, seqs, TE), f32),
        all_sums=shape((16, width), f32),
        all_embed=shape((4, seqs, width), f32),
    )
    for g, wide in enumerate(columns):
        results["total" + str(g)] = shape((mine, wide), f32)
    vm = pltpu.VMEM
    sem = pltpu.SemaphoreType.DMA
    scratch = dict(
        full0=vm((width, 3 * heads), bf16),
        full1=vm((width, heads), bf16),
        full2=vm((width, hidden), bf16),
        full3=vm((width, hidden), bf16),
        feat_z=vm((3, seqs, TE), f32),
        feat_sum=vm((seqs, TE), f32),
        feat_in=vm((3, seqs, TE), f32),
        part=vm((4, tall, width), f32),
        part_in=vm((3, tall, width), f32),
        part_sum=vm((tall, width), f32),
        part_z=vm((3, tall, width), f32),
        part_zsum=vm((tall, width), f32),
        part_tp=vm((tall, width), f32),
        shared=vm((8, width), f32),
        embed=vm((8, width), f32),
        base=vm((rows, width), bf16),
        base_t=vm((width, rows), bf16),
        mask_q=vm((rows, PAIR), bf16),
        mask_k=vm((rows, PAIR), bf16),
        keys=vm((2, rows, PAIR), bf16),
        qkv=vm((rows, 3 * heads), bf16),
        mixed=vm((rows, heads), bf16),
        lse=vm((rows, PAIR), f32),
        lse_t=vm((pairs, 8, rows), f32),
        half_send=vm((half, width), bf16),
        half_recv=vm((half, width), bf16),
        first_own=vm((half, width), f32),
        normed_one=vm((half, width), f32),
        inv_one=vm((half, 128), f32),
        first=vm((rows, width), bf16),
        first_t=vm((width, rows), bf16),
        act=vm((rows, hidden), bf16),
        slope=vm((rows, hidden), bf16),
        acc=vm((6, 8, width), f32),
        acc_up=vm((8, hidden), f32),
        acc_qkv=vm((8, 3 * heads), f32),
        acc_ge=vm((2, 8, width), f32),
        grad_t=vm((width, rows), bf16),
        grad_mixed=vm((rows, heads), bf16),
        inner=vm((8, rows), f32),
        keys_t=vm((PAIR, rows), bf16),
        query_t=vm((PAIR, rows), f32),
        grad_qkv=vm((rows, 3 * heads), bf16),
        g_send=sem((4, 15)),
        g_recv=sem((4, 15)),
        r_send=sem((3 + pairs, 15)),
        r_recv=sem((3 + pairs, 15)),
        small_send=sem((20,)),
        small_recv=sem((20,)),
        tp_send=sem((7,)),
        tp_recv=sem((7,)),
    )
    for g, wide in enumerate(columns):
        scratch["grad" + str(g)] = vm((width, wide), bf16)
        scratch["near" + str(g)] = vm((4, mine, wide), bf16)
        scratch["ring" + str(g)] = vm((8, mine, wide), bf16)
        scratch["high" + str(g)] = vm((3, mine, wide), bf16)
    names = [*operands, *results, *scratch]
    in_specs = [
        pl.BlockSpec(memory_space=pltpu.SMEM if n == "lengths" else pltpu.VMEM) for n in operands
    ]
    got = pl.pallas_call(
        functools.partial(layer_kernel, sub, names),
        out_shape=list(results.values()),
        in_specs=in_specs,
        out_specs=vmem(len(results)),
        scratch_shapes=list(scratch.values()),
        compiler_params=pltpu.CompilerParams(
            collective_id=0, has_side_effects=True, vmem_limit_bytes=63_000 * 1024
        ),
        name="layer",
    )(*operands.values())
    return types.SimpleNamespace(**dict(zip(results, got, strict=True)))


def vmem(count):
    return [pl.BlockSpec(memory_space=pltpu.VMEM)] * count


def time_features(time_steps, feature_width):
    half_width = feature_width // 2
    frequency = jnp.exp(-math.log(10000.0) * jnp.arange(half_width, dtype=f32) / half_width)
    angles = time_steps.astype(f32)[:, None] * frequency[None, :]
    return jnp.concatenate([jnp.cos(angles), jnp.sin(angles)], axis=1)


def contract_rows(left_side, right_side, precision_mode=None):
    return lax.dot_general(
        left_side,
        right_side,
        (((0,), (0,)), ((), ())),
        precision=precision_mode,
        preferred_element_type=jnp.float32,
    )


def contract_cols(left_side, right_side, precision_mode=None):
    return lax.dot_general(
        left_side,
        right_side,
        (((1,), (1,)), ((), ())),
        precision=precision_mode,
        preferred_element_type=jnp.float32,
    )


def on_device(
    inputs, cotangent, seq_lengths, timesteps, time_w1, time_b1, time_w2, time_b2,
    w_query, b_query, w_key, w_value, b_value, w_out, b_out, norm1_gain, norm1_bias,
    w_up, b_up, w_down, b_down, norm2_gain, norm2_bias,
):
    dp = lax.axis_size("dp")
    sub = dp // SUPER
    low = [[q * sub + l for l in range(sub)] for q in range(SUPER)]
    dp_index = lax.axis_index("dp")
    tp_index = lax.axis_index("tp")
    seq_rows, width = inputs.shape
    head_width = w_query.shape[1]

    def near_gather(value, axis):
        if sub == 1:
            return value
        return lax.all_gather(value, "dp", axis=axis, tiled=True, axis_index_groups=low)

    def near_sum(value):
        if sub == 1:
            return value
        return lax.psum(value, "dp", axis_index_groups=low)

    def near_scatter(value):
        if sub == 1:
            return value
        return lax.psum_scatter(
            value, "dp", scatter_dimension=0, tiled=True, axis_index_groups=low
        )

    z = dp_index // (4 * sub)
    pair_row = (z * sub + dp_index % sub) * 2
    seqs = 8 * sub
    features = time_features(timesteps[0], TE).astype(bf16)
    placed_feats = lax.dynamic_update_slice(
        jnp.zeros((seqs, TE), f32), features.astype(f32), (pair_row, 0)
    )
    own_slice = width // (dp * lax.axis_size("tp"))
    slice_start = (dp_index * lax.axis_size("tp") + tp_index) * own_slice
    stacked = jnp.stack(
        [time_b2, b_out, norm1_gain, norm1_bias, b_down, norm2_gain, norm2_bias, jnp.zeros_like(b_out)]
    )
    vectors = lax.dynamic_update_slice(jnp.zeros((8, width), f32), stacked, (0, slice_start))
    pairs = head_width // PAIR
    hidden_width = b_up.shape[0]

    def by_pairs(parts):
        cut = [part.reshape(-1, pairs, 1, PAIR) for part in parts]
        return jnp.concatenate(cut, axis=2).reshape(-1, 3 * head_width)

    operands = dict(
        lengths=seq_lengths,
        x=inputs,
        cot=cotangent,
        w0=near_gather(by_pairs([w_query, w_key, w_value]).astype(bf16), 0),
        w1=near_gather(w_out.T.astype(bf16), 0),
        w2=near_gather(w_up.astype(bf16), 0),
        w3=near_gather(w_down.T.astype(bf16), 0),
        bqkv=by_pairs([b_query, jnp.zeros_like(b_query), b_value]),
        bup=b_up[None, :],
        feats=near_sum(placed_feats),
        vectors=near_sum(vectors),
        tw1=near_gather(time_w1, 1),
        tb1=near_gather(time_b1, 0)[None, :],
        tw2=near_gather(time_w2, 0),
    )
    got = call_layer(sub, operands)
    all_feats = got.all_feats
    all_sums, all_embed = near_sum((got.all_sums, got.all_embed))
    red_down, red_up, red_out = [near_scatter(many(got, "total", g)) for g in range(3)]
    red_pairs = [near_scatter(many(got, "total", 3 + j)) for j in range(pairs)]

    def of_pairs(part):
        return jnp.concatenate([one[:, part * PAIR : (part + 1) * PAIR] for one in red_pairs], axis=1)

    own_vectors = lax.dynamic_slice(all_sums, (0, slice_start), (8, own_slice))
    tp_vectors = all_sums[8:16].reshape(-1)
    qkv_sums = tp_vectors[hidden_width : hidden_width + 3 * head_width].reshape(pairs, 3, PAIR)
    every_feat = all_feats.reshape(-1, TE)
    every_embed = all_embed.reshape(-1, width)
    time_pre = (
        jnp.dot(every_feat.astype(bf16), time_w1.astype(bf16), preferred_element_type=f32) + time_b1
    )
    silu_value, silu_pull = jax.vjp(jax.nn.silu, time_pre)
    time_hidden = silu_value.astype(bf16).astype(f32)
    red_tw2 = contract_rows(time_hidden, every_embed, highest)
    grad_hidden = contract_cols(every_embed, time_w2.astype(bf16).astype(f32), highest)
    grad_time_pre = silu_pull(grad_hidden)[0]
    red_tb1 = jnp.sum(grad_time_pre, axis=0)
    red_tw1 = contract_rows(every_feat, grad_time_pre, highest)
    red_tb2 = lax.dynamic_slice(jnp.sum(every_embed, axis=0), (slice_start,), (own_slice,))
    return (
        got.out,
        got.grad_in,
        red_tw1,
        red_tb1,
        red_tw2,
        red_tb2,
        of_pairs(0),
        qkv_sums[:, 0].reshape(-1),
        of_pairs(1),
        of_pairs(2),
        qkv_sums[:, 2].reshape(-1),
        red_out.T,
        own_vectors[0],
        own_vectors[1],
        own_vectors[2],
        red_up,
        tp_vectors[:hidden_width],
        red_down.T,
        own_vectors[3],
        own_vectors[4],
        own_vectors[5],
    )


def solution(mesh):
    placed = (
        P("dp", None),
        P(("dp", "tp"), None),
        P("dp", None),
        P("dp", None),
        P(None, ("dp", "tp")),
        P(("dp", "tp")),
        P(("dp", "tp"), None),
        P(("dp", "tp")),
        P("dp", "tp"),
        P("tp"),
        P("dp", "tp"),
        P("dp", "tp"),
        P("tp"),
        P("tp", "dp"),
        P(("dp", "tp")),
        P(("dp", "tp")),
        P(("dp", "tp")),
        P("dp", "tp"),
        P("tp"),
        P("tp", "dp"),
        P(("dp", "tp")),
        P(("dp", "tp")),
        P(("dp", "tp")),
    )
    return jax.shard_map(
        on_device,
        mesh=mesh,
        in_specs=placed,
        out_specs=(
            P(("dp", "tp"), None),
            P("dp", None),
            P(None, ("dp", "tp")),
            P(("dp", "tp")),
            P(("dp", "tp"), None),
            P(("dp", "tp")),
            P("dp", "tp"),
            P("tp"),
            P("dp", "tp"),
            P("dp", "tp"),
            P("tp"),
            P("tp", "dp"),
            P(("dp", "tp")),
            P(("dp", "tp")),
            P(("dp", "tp")),
            P("dp", "tp"),
            P("tp"),
            P("tp", "dp"),
            P(("dp", "tp")),
            P(("dp", "tp")),
            P(("dp", "tp")),
        ),
        check_vma=False,
    )
```

time: 511 us -> 228 us (0.45); the launches traced: 501 us -> 227 us
  matrix products: 117 us -> 5.72 us
  waiting for transfers between devices: 56.5 us -> 0 us
  other arithmetic: 61.3 us -> 11.5 us
  local copies, waits for them, and re-layouts: 44.4 us -> 18.7 us
  between operations: 16.7 us -> 0.8 us
  loops' own time: 9.63 us -> 0 us
    dot_general x18 -> x0, matrix products: 80 us -> none  [the longest x2 11.6 us: one_block(): jnp.einsum('hqk,qhd->khd', prob_low, grad_blk, preferred_element_type=jnp...]
    convert_element_type x11 -> x0, other arithmetic: 25.6 us -> none  [the longest x2 10.1 us: one_block(): grad_scores = (probs_full * (grad_probs - row_inner)).astype(jnp.bfloat16)]
    all_gather x3 -> x0, waiting for transfers between devices: 24.2 us -> none  [the longest x1 11.1 us: on_device(): lax.all_gather(grad_second.astype(bf16), 'tp', axis=0, tiled=True)]
    reduce_scatter x3 -> x0, waiting for transfers between devices: 23.7 us -> none  [the longest x1 10.3 us: on_device(): lax.psum_scatter(contract_cols(grad_up_low, wup).astype(bf16), 'tp', scat...]
    reduce_sum x10 -> x0, other arithmetic: 19.3 us -> none  [the longest x2 7.27 us: one_block(): row_total = jnp.sum(exp_scores, axis=-1, keepdims=True)]
    dot_general x7 -> x2, matrix products: 20 us -> 3.17 us  [contract_rows(): lax.dot_general(left_side, right_side, (((0,), (0,)), ((), ())), precisio...]
    dot_general x5 -> x1, matrix products: 16.5 us -> 1.76 us  [contract_cols(): lax.dot_general(left_side, right_side, (((1,), (1,)), ((), ())), precisio...]
    unnamed x114 -> x24, local copies, waits for them, and re-layouts: 17.4 us -> 7.27 us
  transfers between devices with their start and end apart: 7 -> 0, of which waited for: 7 -> 0; matrix products, arithmetic and copies ran while one was open for 5% -> 0% of each run, Pallas kernels for 0% -> 0%
where the time goes in v2:
time: 228 us; the launch traced here: 227 us
  Pallas kernels  190 us (83%)
  local copies, waits for them, and re-layouts  18.7 us (8%)
  other arithmetic  11.5 us (5%)
  matrix products  5.72 us (3%)
    pallas_call x1, Pallas kernels, call_layer(): pl.pallas_call(functools.partial(layer_kernel, sub, names), out_shape=lis...  190 us
    unnamed x24, local copies, waits for them, and re-layouts  7.27 us

profile of v2, /device:TPU:0, one launch (start us, length us, event | category | flops | bytes accessed | tf_op | source)
XLA Modules:
  0.0 226.6 jit_solution(17986607498241222617)
XLA Ops:
  0.7 0.7 convert_bitcast_fusion.2
  1.6 0.7 reshape.94
  2.3 0.7 reshape.96
  3.7 0.8 stack.31
  4.5 1.3 broadcast_in_dim.15.refs_8_
  6.0 0.9 convert.18
  6.9 0.9 convert.19
  7.8 0.9 convert.20
  9.0 0.7 convert_element_type.44.refs_3_
  9.7 1.5 convert_bitcast_fusion.1.refs_4_
  11.2 1.4 copy.49.refs_11_
  12.7 1.6 convert_element_type.47.refs_5_
  14.3 1.6 convert_bitcast_fusion.refs_6_
  15.9 189.9 %layer.1 = (bf16[512,768]{1,0:T(8,128)(2,1)}, f32[1024,768]{1,0:T(8,128)}, f32[4,8,128]{2,1,0:T(8,128)}, f32[16,768]{1,0:T(8,128)}, f32[4,8,768]{2,1,0:T(8,128)}...) custom-call(s32[1,2]{1,0:T(1,128)} %refs_0_.1, ...), custom_call_target="tpu_custom_call" | custom-call | tf_op jit(solution)/shard_map/layer/pallas_call | solution.py:854
  205.9 1.1 reduce_sum.19
  207.6 0.8 constant_dynamic-slice_fusion
  208.9 0.7 slice.83
  209.6 0.7 slice.70
  211.6 0.8 convolution_add_fusion
  212.4 1.8 fusion.22
  214.1 1.7 fusion
  215.8 1.5 fusion.5
  217.3 0.8 fusion.21
  218.1 0.8 fusion.19
  218.9 0.6 pad_maximum_fusion.3
  219.6 0.6 pad_maximum_fusion.2
  220.2 0.6 pad_maximum_fusion.1
  220.8 2.1 copy.57
  222.9 1.7 copy.58
  224.6 0.6 copy.59
  225.2 0.7 copy.60
  225.9 0.7 copy.61
  (38 shorter events, 3.8 us)
Async XLA Ops:
  0.7 211.7 %copy-start.3 = (f32[24,768]{1,0:T(8,128)S(1)}, f32[24,768]{1,0:T(8,128)}, u32[]{:S(2)}) copy-start(f32[24,768]{1,0:T(8,128)} %refs_13_.1) | copy-start | bytes 221188
  0.7 210.9 %copy-start.8 = (f32[24]{0:T(128)S(1)}, f32[24]{0:T(128)}, u32[]{:S(2)}) copy-start(f32[24]{0:T(128)} %param.28) | copy-start | bytes 292
  0.7 210.9 %copy-start.7 = (f32[128,24]{0,1:T(8,128)S(1)}, f32[128,24]{0,1:T(8,128)}, u32[]{:S(2)}) copy-start(f32[128,24]{0,1:T(8,128)} %param.27) | copy-start | bytes 36868
  4.5 11.4 %copy-start.6 = (f32[8,128]{1,0:T(8,128)}, f32[8,128]{1,0:T(8,128)S(1)}, u32[]{:S(2)}) copy-start(f32[8,128]{1,0:T(8,128)S(1)} %convert_dynamic-update-slice_fusion.refs_9_) | copy-start | bytes 12292
  6.0 10.0 %copy-start.4 = (f32[8,768]{1,0:T(8,128)}, f32[8,768]{1,0:T(8,128)S(1)}, u32[]{:S(2)}) copy-start(f32[8,768]{1,0:T(8,128)S(1)} %dynamic_update_slice.7.refs_10_) | copy-start | bytes 73732
  205.9 17.0 %copy-start = (f32[1024,768]{1,0:T(8,128)S(1)}, f32[1024,768]{1,0:T(8,128)}, u32[]{:S(2)}) copy-start(f32[1024,768]{1,0:T(8,128)} %get-tuple-element.89) | copy-start | bytes 9437188
  222.9 1.7 copy-start.5
  222.9 2.3 %copy-start.2 = (f32[48,1536]{1,0:T(8,128)S(1)}, f32[48,1536]{1,0:T(8,128)}, u32[]{:S(2)}) copy-start(f32[48,1536]{1,0:T(8,128)} %get-tuple-element.103) | copy-start | bytes 884740
  222.9 3.0 %copy-start.1 = (f32[48,1536]{1,0:T(8,128)S(1)}, f32[48,1536]{1,0:T(8,128)}, u32[]{:S(2)}) copy-start(f32[48,1536]{1,0:T(8,128)} %get-tuple-element.42) | copy-start | bytes 884740

commit v3 on v2

--- a/solution.py
+++ b/solution.py
@@ -28,6 +28,8 @@
         self.z = lax.div(self.place, 4)
         self.p = lax.rem(self.place, 4)
         self.r = self.ring(self.p)
+        self.outer = (self.z == 0) | (self.z == 3)
+        self.inner = (self.z == 1) | (self.z == 2)
 
     @staticmethod
     def ring(v):
@@ -41,6 +43,10 @@
 
     def device(self, dz, dr):
         return {"dp": self.spot(dz, dr) * self.sub + self.low}
+
+    def beside(self, step):
+        plane = lax.rem(self.z + step + 4, 4)
+        return {"dp": (plane * 4 + self.p) * self.sub + self.low}
 
     def other(self):
         return {"tp": 1 - lax.axis_index("tp")}
@@ -75,10 +81,12 @@
 
 
 class Gather:
-    def __init__(self, place, shard, full, send, recv, g):
+    def __init__(self, place, shard, full, cols, send, recv, g):
         rows = shard.shape[0]
-        at = lambda dz, dr: full.at[place.rows(dz, dr, rows), :]
+        at = lambda dz, dr: full.at[place.rows(dz, dr, rows), cols]
         self.place, self.shard, self.full, self.count = place, shard, full, rows
+        self.cols = cols
+        shard = shard.at[:, cols]
         self.to_planes = [
             remote(shard, at(0, 0), send.at[g, d - 1], recv.at[g, d - 1], place.device(d, 0))
             for d in (1, 2, 3)
@@ -113,18 +121,20 @@
     def begin(self):
         for copy in self.to_planes:
             copy.start()
+        self.full[self.place.rows(0, 0, self.count), self.cols] = self.shard[:, self.cols]
+
+    def own(self):
         for copy in self.around[0]:
             copy.start()
-        self.full[self.place.rows(0, 0, self.count), :] = self.shard[...]
-
-    def turn(self):
-        for d in (1, 2, 3):
+
+    def turn(self, *which):
+        for d in which or (1, 2, 3):
             self.to_planes[d - 1].wait_recv()
             for copy in self.around[d]:
                 copy.start()
 
-    def pass_on(self):
-        for d in range(4):
+    def pass_on(self, *which):
+        for d in which or (0, 1, 2, 3):
             self.around[d][d // 2].wait_recv()
             self.relay[d].start()
 
@@ -138,11 +148,78 @@
             copy.wait_send()
 
 
+def halves(cols):
+    middle = (cols.start + cols.stop) // 2
+    return slice(cols.start, middle), slice(middle, cols.stop)
+
+
+class Climb:
+    def __init__(self, place, shard, full, cols, send, recv, g):
+        rows = shard.shape[0]
+        self.place, self.shard, self.full, self.count, self.cols = place, shard, full, rows, cols
+        z = place.z
+        at = lambda dr, part: full.at[place.rows(0, dr, rows), part]
+        slab = lambda plane: full.at[pl.ds(pl.multiple_of(plane * 4 * rows, 16), 4 * rows), cols]
+        self.around = [
+            remote(shard.at[:, cols], at(0, cols), send.at[g, n], recv.at[g, n], place.device(0, 1 - 2 * n))
+            for n in (0, 1)
+        ]
+        self.relay = [
+            remote(at(2 * n - 1, part), at(2 * n - 1, part), send.at[g, 2 + n], recv.at[g, 2 + n], place.device(0, 1 - 2 * n))
+            for n, part in enumerate(halves(cols))
+        ]
+        self.up, self.down = [
+            remote(slab(z), slab(z), send.at[g, 4 + n], recv.at[g, 4 + z], place.beside(1 - 2 * n))
+            for n in (0, 1)
+        ]
+        self.heard = []
+        table = [
+            jnp.where(z == 0, 1, z - 1),
+            jnp.where(z == 3, 1, jnp.where(z == 2, 3, 2)),
+            jnp.where(z < 2, 3, 0),
+        ]
+        for n, plane in enumerate(table):
+            self.heard.append(
+                remote(
+                    slab(plane), slab(plane), send.at[g, 6 + n], recv.at[g, 4 + plane],
+                    place.beside(jnp.where(plane < z, 1, -1)),
+                )
+            )
+
+    def begin(self):
+        for copy in self.around:
+            copy.start()
+        self.full[self.place.rows(0, 0, self.count), self.cols] = self.shard[:, self.cols]
+
+    def pass_on(self):
+        for n in (0, 1):
+            self.around[n].wait_recv()
+            self.relay[n].start()
+
+    def rise(self):
+        for n in (0, 1):
+            self.relay[n].wait_recv()
+        pl.when(self.place.z < 3)(self.up.start)
+        pl.when(self.place.z > 0)(self.down.start)
+
+    def hear(self, n):
+        self.heard[n].wait_recv()
+        pl.when(self.place.inner)(self.heard[n].start)
+
+    def drain(self):
+        for copy in self.around + self.relay:
+            copy.wait_send()
+        pl.when(self.place.z < 3)(self.up.wait_send)
+        pl.when(self.place.z > 0)(self.down.wait_send)
+        for copy in self.heard:
+            pl.when(self.place.inner)(copy.wait_send)
+
+
 class Reduce:
-    def __init__(self, place, grads, total, first, second, third, send, recv, g):
+    def __init__(self, place, grads, total, cols, first, second, third, send, recv, g):
         rows = total.shape[0]
-        at = lambda dz, dr: grads.at[place.rows(dz, dr, rows), :]
-        self.place, self.grads, self.total, self.rows = place, grads, total, rows
+        at = lambda dz, dr: grads.at[place.rows(dz, dr, rows), cols]
+        self.place, self.grads, self.total, self.rows, self.cols = place, grads, total, rows, cols
         self.first, self.second, self.third = first, second, third
         self.far, self.near, self.up = [], [], []
         for d in range(4):
@@ -185,36 +262,141 @@
         for d in range(4):
             k = d // 2
             self.far[d].wait_recv()
-            rows = self.place.rows(d, 1 - 2 * k, self.rows)
-            self.grads[rows, :] = (self.grads[rows, :].astype(f32) + self.first[d].astype(f32)).astype(bf16)
+            here = self.place.rows(d, 1 - 2 * k, self.rows), self.cols
+            self.grads[here] = (self.grads[here].astype(f32) + self.first[d].astype(f32)).astype(bf16)
             self.near[d][k].start()
 
     def cross(self):
         for d in (1, 2, 3, 0):
             for j in (0, 1):
                 self.near[d][j].wait_recv()
-            rows = self.place.rows(d, 0, self.rows)
+            here = self.place.rows(d, 0, self.rows), self.cols
             summed = (
-                self.grads[rows, :].astype(f32)
+                self.grads[here].astype(f32)
                 + self.second[d].astype(f32)
                 + self.second[4 + d].astype(f32)
             )
             if d:
-                self.grads[rows, :] = summed.astype(bf16)
+                self.grads[here] = summed.astype(bf16)
                 self.up[d - 1].start()
             else:
-                self.total[...] = summed
+                self.total[:, self.cols] = summed
 
     def finish(self):
         for copy in self.up:
             copy.wait_recv()
-        self.total[...] += (
+        self.total[:, self.cols] += (
             self.third[0].astype(f32) + self.third[1].astype(f32) + self.third[2].astype(f32)
         )
 
     def drain(self):
         for copy in self.far + [c for pair in self.near for c in pair] + self.up:
             copy.wait_send()
+
+
+class Descend:
+    def __init__(self, place, grads, total, cols, deep, far, near, send, recv, g):
+        rows = total.shape[0]
+        self.place, self.grads, self.total, self.rows, self.cols = place, grads, total, rows, cols
+        self.deep, self.far, self.near = deep, far, near
+        lower = place.z < 2
+        inward = jnp.where(lower, 1, -1)
+        plane = lambda c: jnp.where(lower, c, 3 - c)
+        self.slab = lambda c: (pl.ds(pl.multiple_of(plane(c) * 4 * rows, 16), 4 * rows), cols)
+        part = halves(cols)
+        self.part = part
+        self.here = lambda dr, n: (place.rows(0, dr, rows), part[n])
+        self.slot = [slice(p.start - cols.start, p.stop - cols.start) for p in part]
+
+        def copy(source, dest, n, m, to):
+            return remote(grads.at[source], dest, send.at[g, n], recv.at[g, m], to)
+
+        ahead = place.beside(inward)
+        self.enter = [copy(self.slab(3 - n), deep.at[n], n, n, ahead) for n in range(3)]
+        self.between = [copy(self.slab(3 - n), deep.at[3 + n], 3 + n, 3 + n, ahead) for n in (0, 1)]
+        self.leave = copy(self.slab(0), deep.at[0], 5, 5, place.beside(-inward))
+        side = [place.device(0, 1), place.device(0, -1)]
+        self.away = [
+            copy(self.here(2, n), far.at[:, self.slot[n]], 6 + n, 6 + n, side[n]) for n in (0, 1)
+        ]
+        self.plain = [
+            copy(self.here(1 - 2 * n, 1 - n), near.at[n, :, self.slot[1 - n]], 8 + n, 8 + n, side[n])
+            for n in (0, 1)
+        ]
+        self.joined = [
+            copy(self.here(1 - 2 * n, n), near.at[n, :, self.slot[n]], 10 + n, 10 + n, side[n])
+            for n in (0, 1)
+        ]
+
+    def add(self, here, *terms):
+        total = self.grads[here].astype(f32)
+        for term in terms:
+            total += term.astype(f32)
+        self.grads[here] = total.astype(bf16)
+
+    def begin(self):
+        @pl.when(self.place.outer)
+        def _():
+            for copy in self.enter:
+                copy.start()
+
+    def pass_in(self):
+        @pl.when(self.place.inner)
+        def _():
+            for n in (0, 1):
+                self.enter[n].wait_recv()
+                self.add(self.slab(3 - n), self.deep[n])
+                self.between[n].start()
+
+    def pass_out(self):
+        @pl.when(self.place.inner)
+        def _():
+            self.between[0].wait_recv()
+            self.add(self.slab(0), self.deep[3])
+            self.leave.start()
+
+    def arrive(self):
+        @pl.when(self.place.inner)
+        def _():
+            self.enter[2].wait_recv()
+            self.between[1].wait_recv()
+            self.add(self.slab(1), self.deep[2], self.deep[4])
+
+        @pl.when(self.place.outer)
+        def _():
+            self.leave.wait_recv()
+            self.add(self.slab(0), self.deep[0])
+
+        for copy in self.away + self.plain:
+            copy.start()
+
+    def join(self):
+        for n in (0, 1):
+            self.away[n].wait_recv()
+            self.add(self.here(1 - 2 * n, n), self.far[:, self.slot[n]])
+            self.joined[n].start()
+
+    def finish(self):
+        for copy in self.plain + self.joined:
+            copy.wait_recv()
+        own = self.place.rows(0, 0, self.rows), self.cols
+        self.total[:, self.cols] = (
+            self.grads[own].astype(f32) + self.near[0].astype(f32) + self.near[1].astype(f32)
+        )
+
+    def drain(self):
+        for copy in self.away + self.plain + self.joined:
+            copy.wait_send()
+
+        @pl.when(self.place.outer)
+        def _():
+            for copy in self.enter:
+                copy.wait_send()
+
+        @pl.when(self.place.inner)
+        def _():
+            for copy in self.between + [self.leave]:
+                copy.wait_send()
 
 
 class Spread:
@@ -265,6 +447,21 @@
     return jnp.mean(x, axis=-1, keepdims=True)
 
 
+def exact(a, b, i, j):
+    return lax.dot_general(
+        a, b, (((i,), (j,)), ((), ())), precision=highest, preferred_element_type=f32
+    )
+
+
+def chosen(place, count, width):
+    own = count // place.sub
+    entry = lax.broadcasted_iota(jnp.int32, (count, width), 0)
+    column = lax.broadcasted_iota(jnp.int32, (count, width), 1)
+    low = lax.div(entry, own)
+    home = (place.place * place.sub + low) * lax.axis_size("tp") + lax.axis_index("tp")
+    return jnp.where(column == home * own + lax.rem(entry, own), 1.0, 0.0)
+
+
 PAIR = 2 * HD
 TOP = math.sqrt(2.0 / math.pi)
 
@@ -273,10 +470,11 @@
     k = types.SimpleNamespace(**dict(zip(names, refs, strict=True)))
     place = Place(sub)
     side = lax.axis_index("tp")
-    x_ref = k.x
+    x_ref = k.rows_in
     total_rows, width = x_ref.shape
     half = total_rows // 2
     tp_send, tp_recv = k.tp_send, k.tp_recv
+    per = k.steps.shape[1]
     seqs = k.feats.shape[0]
     pairs = k.mixed.shape[1] // PAIR
     hidden_width = k.bup.shape[1]
@@ -292,60 +490,126 @@
     def swap(n, src, dst):
         return remote(src, dst, tp_send.at[n], tp_recv.at[n], place.other())
 
+    def cut_of(j, part_index):
+        return slice((3 * j + part_index) * PAIR, (3 * j + part_index + 1) * PAIR)
+
+    def pair_of(j):
+        return slice(j * PAIR, (j + 1) * PAIR)
+
+    bring_x = pltpu.make_async_copy(k.x, x_ref, k.local.at[0])
+    bring_cot = pltpu.make_async_copy(k.cot, k.cot_in, k.local.at[1])
+    bring_x.start()
+    bring_cot.start()
+    for j in range(pairs):
+        for n, source in enumerate((k.wq, k.wk, k.wv)):
+            k.w0[:, cut_of(j, n)] = source[:, pair_of(j)].astype(bf16)
+        k.bqkv[:, cut_of(j, 0)] = k.bq[pair_of(j)].reshape(1, PAIR)
+        k.bqkv[:, cut_of(j, 1)] = jnp.zeros((1, PAIR), f32)
+        k.bqkv[:, cut_of(j, 2)] = k.bv[pair_of(j)].reshape(1, PAIR)
+    k.bup[...] = k.bu[...].reshape(1, hidden_width)
+    k.w1[...] = k.wo[...].astype(bf16)
+    k.w2[...] = k.wu[...].astype(bf16)
+    k.w3[...] = k.wd[...].astype(bf16)
+    at_row = (place.z * sub + place.low) * 2
+    seq_row = lax.broadcasted_iota(jnp.int32, (seqs, 1), 0)
+    step = jnp.zeros((seqs, 1), f32)
+    for n in range(per):
+        step = jnp.where(seq_row == place.z * per + n, k.steps[0, n].astype(f32), step)
+    column = lax.broadcasted_iota(jnp.int32, (1, TE), 1)
+    number = jnp.where(column < TE // 2, column, column - TE // 2).astype(f32)
+    angle = step * jnp.exp(-math.log(10000.0) * number / (TE // 2))
+    wave = jnp.where(column < TE // 2, jnp.cos(angle), jnp.sin(angle)).astype(bf16).astype(f32)
+    mine = (seq_row >= place.z * per) & (seq_row < (place.z + 1) * per)
+    k.feats[...] = jnp.where(mine, wave, 0.0)
+    given = (k.v0, k.v1, k.v2, k.v3, k.v4, k.v5, k.v6)
+    count = k.v0.shape[1]
+    for n, source in enumerate(given):
+        k.given[n : n + 1, :] = source[...]
+    k.given[7:8, :] = jnp.zeros((1, count), f32)
+    vectors = exact(k.given[...], chosen(place, count, width), 1, 0)
+
     place.enter()
     small_send, small_recv = k.small_send, k.small_recv
     spread_z = Spread(place, "z", [k.feats] * 3, k.feat_z, small_send, small_recv, 0)
     spread_z.start()
-    gathers = [
-        Gather(place, many(k, "w", g), many(k, "full", g), k.g_send, k.g_recv, g) for g in range(4)
+    low_half, high_half = halves(slice(0, hidden_width))
+    gather_a, gather_b, gather_c, gather_d = [
+        Gather(place, shard, full, part, k.g_send, k.g_recv, g)
+        for g, (shard, full, part) in enumerate(
+            (
+                (k.w0, k.full0, slice(0, k.w0.shape[1])),
+                (k.w1, k.full1, slice(0, k.w1.shape[1])),
+                (k.w2, k.full2, slice(0, hidden_width)),
+                (k.w3, k.full3, low_half),
+            )
+        )
     ]
-    gathers[0].begin()
+    climb = Climb(place, k.w3, k.full3, high_half, k.g_send, k.g_recv, 4)
+    gather_a.begin()
+    gather_a.own()
     spread_z.wait()
     k.feat_sum[...] = k.feats[...] + k.feat_z[0] + k.feat_z[1] + k.feat_z[2]
     spread_r = Spread(place, "r", [k.feat_sum] * 3, k.feat_in, small_send, small_recv, 3)
     spread_r.start()
+    climb.begin()
+    gather_b.own()
     k.all_feats[0] = k.feat_sum[...]
+
+    @pl.loop(0, total_rows // 128)
+    def _(i):
+        start = pl.multiple_of(i * 128, 128)
+        seg = segment(start, 128)
+        lane = lax.rem(lax.broadcasted_iota(jnp.int32, (1, PAIR), 1), HD)
+        k.mask_k[pl.ds(start, 128), :] = jnp.where(lane == seg, 1.0, 0.0).astype(bf16)
+        k.mask_q[pl.ds(start, 128), :] = jnp.where((lane < 3) & (lane != seg), -1e30, 0.0).astype(
+            bf16
+        )
+
     spread_r.wait()
     for d in (1, 2, 3):
         k.all_feats[d] = k.feat_in[d - 1]
     every = k.all_feats[...].reshape(4 * seqs, TE)
-    before = mul(every.astype(bf16), k.tw1[...].astype(bf16)) + k.tb1[...]
+    before = mul_t(every.astype(bf16), k.tw1t[...].astype(bf16)) + k.tb1[...]
     hidden = jax.nn.silu(before).astype(bf16)
     share = mul(hidden, k.tw2[...].astype(bf16))
     part = k.part
     for d in range(4):
         part[d, :seqs, :] = share[d * seqs : (d + 1) * seqs, :]
-        part[d, seqs : seqs + 8, :] = k.vectors[...]
+        part[d, seqs : seqs + 8, :] = vectors
     top = slice(0, seqs + 8)
     back = Spread(
         place, "r", [part.at[n, top] for n in (3, 2, 1)], k.part_in, small_send, small_recv, 6
     )
     back.start()
+    gather_c.own()
+    gather_b.begin()
+    gather_a.turn()
     back.wait()
     in_plane = k.part_in
     k.part_sum[top] = part[0, top] + in_plane[0, top] + in_plane[1, top] + in_plane[2, top]
     over_z = Spread(place, "z", [k.part_sum.at[top]] * 3, k.part_z, small_send, small_recv, 9)
     over_z.start()
-    gathers[0].turn()
-    gathers[1].begin()
-    gathers[2].begin()
+    gather_c.begin()
+    gather_d.begin()
+    gather_d.own()
+    climb.pass_on()
+    gather_a.pass_on(0)
+    bring_x.wait()
     over_z.wait()
     from_z = k.part_z
     k.part_zsum[top] = k.part_sum[top] + from_z[0, top] + from_z[1, top] + from_z[2, top]
     pair = Spread(place, "tp", [k.part_zsum.at[top]], k.part_tp, small_send, small_recv, 12)
     pair.start()
+    gather_b.turn()
     pair.wait()
     both = k.part_zsum[top] + k.part_tp[top]
     shared = k.shared
     shared[...] = both[seqs:]
     embed = both[:seqs] + shared[0:1, :]
-    at_row = (place.z * sub + place.low) * 2
-    seq_row = lax.broadcasted_iota(jnp.int32, (seqs, 1), 0)
     for s in (0, 1):
         k.embed[s : s + 1, :] = jnp.sum(
             jnp.where(seq_row == at_row + s, embed, 0.0), axis=0, keepdims=True
         )
-
     for one in (spread_z, spread_r, back, over_z, pair):
         one.drain()
 
@@ -363,12 +627,6 @@
     def _(i):
         start = pl.multiple_of(i * 128, 128)
         k.base[pl.ds(start, 128), :] = base_of(start, 128).astype(bf16)
-        seg = segment(start, 128)
-        lane = lax.rem(lax.broadcasted_iota(jnp.int32, (1, PAIR), 1), HD)
-        k.mask_k[pl.ds(start, 128), :] = jnp.where(lane == seg, 1.0, 0.0).astype(bf16)
-        k.mask_q[pl.ds(start, 128), :] = jnp.where((lane < 3) & (lane != seg), -1e30, 0.0).astype(
-            bf16
-        )
 
     def transpose(source, dest):
         @pl.loop(0, width // 128)
@@ -377,17 +635,15 @@
             dest[cut, :] = source[:, cut].T
 
     transpose(k.base, k.base_t)
-    gathers[0].pass_on()
-    gathers[0].finish()
+    gather_a.pass_on(1, 2, 3)
+    climb.rise()
+    gather_a.finish()
 
     lane = lax.broadcasted_iota(jnp.int32, (1, PAIR), 1)
     lower = lane < HD
     scale = jnp.where(lax.broadcasted_iota(jnp.int32, (1, 3 * PAIR), 1) < PAIR, HD**-0.5, 1.0)
     qkv = k.qkv
     rows_at_once = 256
-
-    def cut_of(j, part_index):
-        return slice((3 * j + part_index) * PAIR, (3 * j + part_index + 1) * PAIR)
 
     def projection(j):
         cols = slice(3 * j * PAIR, 3 * (j + 1) * PAIR)
@@ -428,21 +684,20 @@
         k.lse_t[j, 1:2, :] = flipped[HD : HD + 1, :]
 
     projection(0)
-    gathers[1].turn()
-    gathers[2].turn()
-    gathers[3].begin()
-    projection(1)
-    projection(2)
+    gather_c.turn()
+    gather_b.pass_on()
+    for j in range(1, pairs):
+        projection(j)
     attend(0)
-    gathers[1].pass_on()
-    gathers[2].pass_on()
+    gather_d.turn()
+    gather_c.pass_on(0, 1)
     attend(1)
-    gathers[3].turn()
-    attend(2)
-    for j in range(3, pairs):
+    gather_c.pass_on(2, 3)
+    climb.hear(0)
+    gather_d.pass_on()
+    for j in range(2, pairs):
         attend(j)
-    gathers[1].finish()
-    gathers[3].pass_on()
+    gather_b.finish()
 
     block = 256
 
@@ -465,6 +720,7 @@
             base_of(start, block) + vector(1) + mul_t(k.mixed[pl.ds(start, block), :], k.full1[...])
         )
 
+    climb.hear(1)
     swap_a.wait_recv()
     small = 128
 
@@ -485,7 +741,7 @@
     far = pl.ds(far0, half)
     swap_b = swap(1, k.first.at[own, :], k.first.at[own, :])
     swap_b.start()
-    gathers[2].finish()
+    gather_c.finish()
     chunk = 512
     blocks = hidden_width // chunk
 
@@ -509,7 +765,9 @@
     swap_b.wait_recv()
     rise(far0)
     transpose(k.first, k.first_t)
-    gathers[3].finish()
+    gather_d.finish()
+    climb.hear(2)
+    bring_cot.wait()
 
     @pl.loop(0, half // block)
     def _(i):
@@ -540,9 +798,9 @@
         centered = summed - mean(summed)
         inv = lax.rsqrt(mean(centered * centered) + epsilon)
         normed = centered * inv
-        k.out[here, :] = (normed * vector(5) + vector(6)).astype(bf16)
+        k.out_stage[here, :] = (normed * vector(5) + vector(6)).astype(bf16)
         start = pl.multiple_of(own0 + i * small, small)
-        grad = jnp.where(segment(start, small) < 2, k.cot[here, :].astype(f32), 0.0)
+        grad = jnp.where(segment(start, small) < 2, k.cot_in[here, :].astype(f32), 0.0)
         scaled = grad * vector(5)
         second = inv * (scaled - mean(scaled) - normed * mean(scaled * normed))
         own_sum[here, :] = second
@@ -551,6 +809,8 @@
         acc[1] += fold(grad)
         acc[2] += fold(second)
 
+    send_out = pltpu.make_async_copy(k.out_stage, k.out, k.local.at[2])
+    send_out.start()
     swap_d = swap(3, k.base.at[own, :], k.base.at[own, :])
     swap_d.start()
     acc_up = k.acc_up
@@ -566,27 +826,35 @@
             k.slope[rows, cols] = grad.astype(bf16)
             acc_up[:, cols] += fold(grad)
 
-    reduces = [
+    descend = Descend(
+        place, k.grad0, k.total0, high_half, k.deep, k.deep_far, k.deep_near, k.r_send, k.r_recv, 0
+    )
+    sum_down, sum_up, sum_out, *sum_pairs = [
         Reduce(
-            place, many(k, "grad", g), many(k, "total", g), many(k, "near", g), many(k, "ring", g), many(k, "high", g),
-            k.r_send, k.r_recv, g,
+            place, many(k, "grad", g), many(k, "total", g), part,
+            many(k, "near", g), many(k, "ring", g), many(k, "high", g), k.r_send, k.r_recv, 1 + g,
         )
-        for g in range(3 + pairs)
+        for g, part in enumerate(
+            [low_half, slice(0, hidden_width), slice(0, pairs * PAIR)] + [slice(0, 3 * PAIR)] * pairs
+        )
     ]
 
-    def weight_grad(g, left_t, right, first_col, count, step):
+    def weight_grad(dest, left_t, right, source_col, dest_col, count, step):
         @pl.loop(0, count // step)
         def _(i):
-            cols = pl.ds(pl.multiple_of(i * step, step), step)
-            source = pl.ds(pl.multiple_of(first_col + i * step, 128), step)
-            many(k, "grad", g)[:, cols] = mul(left_t[...], right[:, source]).astype(bf16)
+            to = pl.ds(pl.multiple_of(dest_col + i * step, 128), step)
+            source = pl.ds(pl.multiple_of(source_col + i * step, 128), step)
+            dest[:, to] = mul(left_t[...], right[:, source]).astype(bf16)
 
     fall(own0)
     swap_c.wait_send()
     swap_d.wait_recv()
     transpose(k.base, k.grad_t)
-    weight_grad(0, k.grad_t, k.act, 0, hidden_width, chunk)
-    reduces[0].begin()
+    middle = hidden_width // 2
+    weight_grad(k.grad0, k.grad_t, k.act, middle, middle, middle, 256)
+    descend.begin()
+    weight_grad(k.grad0, k.grad_t, k.act, 0, 0, middle, 256)
+    sum_down.begin()
     fall(far0)
 
     @pl.loop(0, half // block)
@@ -621,9 +889,10 @@
 
     swap_f = swap(5, k.first.at[own, :], k.first.at[own, :])
     swap_f.start()
-    weight_grad(1, k.first_t, k.slope, 0, hidden_width, chunk)
-    reduces[1].begin()
-    reduces[0].join()
+    sum_down.join()
+    weight_grad(k.grad1, k.first_t, k.slope, 0, 0, hidden_width, 512)
+    sum_up.begin()
+    descend.pass_in()
     swap_f.wait_recv()
 
     @pl.loop(0, total_rows // 512)
@@ -632,13 +901,13 @@
         k.grad_mixed[rows, :] = mul(k.first[rows, :], k.full1[...]).astype(bf16)
 
     transpose(k.first, k.grad_t)
-    weight_grad(2, k.grad_t, k.mixed, 0, pairs * PAIR, pairs * PAIR)
-    reduces[2].begin()
+    weight_grad(k.grad2, k.grad_t, k.mixed, 0, 0, pairs * PAIR, pairs * PAIR)
+    sum_out.begin()
 
     grad_qkv = k.grad_qkv
     acc_qkv = k.acc_qkv
 
-    def attend_back(j):
+    def attend_back(j, midway):
         mixed_cut = slice(j * PAIR, (j + 1) * PAIR)
         for h in (0, 1):
             k.keys[h] = with_mask(qkv[:, cut_of(j, 0)], k.mask_q[...], h)
@@ -649,8 +918,9 @@
         k.keys_t[...] = qkv[:, cut_of(j, 1)].T
         k.query_t[...] = jnp.zeros_like(k.query_t)
 
-        @pl.loop(0, total_rows // rows_at_once)
-        def _(i):
+        steps = total_rows // rows_at_once
+
+        def one_block(i):
             start = pl.multiple_of(i * rows_at_once, rows_at_once)
             rows = pl.ds(start, rows_at_once)
             grads_v, grads_k, query_t = [], [], []
@@ -669,22 +939,25 @@
             grad_qkv[rows, cut_of(j, 2)] = grad_v
             k.query_t[...] += jnp.concatenate(query_t, axis=0)
 
+        pl.loop(0, steps // 2)(one_block)
+        midway()
+        pl.loop(steps // 2, steps)(one_block)
         grad_qkv[:, cut_of(j, 0)] = (k.query_t[...].T * HD**-0.5).astype(bf16)
         cols = slice(3 * j * PAIR, 3 * (j + 1) * PAIR)
         acc_qkv[:, cols] = fold(grad_qkv[:, cols].astype(f32))
-        weight_grad(3 + j, k.base_t, grad_qkv, 3 * j * PAIR, 3 * PAIR, 3 * PAIR)
-        reduces[3 + j].begin()
-
-    attend_back(0)
-    reduces[0].cross()
-    reduces[1].join()
-    attend_back(1)
-    reduces[2].join()
-    reduces[1].cross()
-    reduces[2].cross()
+        weight_grad(many(k, "grad", 3 + j), k.base_t, grad_qkv, 3 * j * PAIR, 0, 3 * PAIR, 3 * PAIR)
+        sum_pairs[j].begin()
+
+    attend_back(0, sum_down.cross)
+    sum_up.join()
+    descend.pass_out()
+    attend_back(1, sum_out.join)
+    descend.arrive()
+    sum_up.cross()
     for j in range(2, pairs):
-        attend_back(j)
-        reduces[1 + j].join()
+        attend_back(j, sum_pairs[j - 2].join)
+    descend.join()
+    sum_out.cross()
 
     in_send, in_recv = k.act.at[:, :width], k.act.at[:, width : 2 * width]
 
@@ -695,24 +968,34 @@
 
     swap_g = swap(6, in_send, in_recv)
     swap_g.start()
-    for g in range(3, 2 + pairs):
-        if g > 3:
-            reduces[g].join()
-    reduces[0].finish()
-    reduces[3].cross()
+    for j in range(pairs - 2, pairs - 1):
+        sum_pairs[j].join()
+    sum_down.finish()
+    sum_pairs[0].cross()
     swap_g.wait_recv()
     ge = k.acc_ge
     ge[...] = jnp.zeros_like(ge)
 
-    @pl.loop(0, total_rows // small)
-    def _(i):
-        start = pl.multiple_of(i * small, small)
-        rows = pl.ds(start, small)
-        grad = (in_send[rows, :].astype(f32) + in_recv[rows, :].astype(f32)) + k.first[rows, :].astype(f32)
-        k.grad_in[rows, :] = grad
-        seg = segment(start, small)
-        ge[0] += fold(jnp.where(seg == 0, grad, 0.0))
-        ge[1] += fold(jnp.where(seg == 1, grad, 0.0))
+    def settle(stage, base):
+        @pl.loop(0, half // small)
+        def _(i):
+            start = pl.multiple_of(base + i * small, small)
+            rows = pl.ds(start, small)
+            grad = (in_send[rows, :].astype(f32) + in_recv[rows, :].astype(f32)) + k.first[
+                rows, :
+            ].astype(f32)
+            stage[pl.ds(pl.multiple_of(i * small, small), small), :] = grad
+            seg = segment(start, small)
+            ge[0] += fold(jnp.where(seg == 0, grad, 0.0))
+            ge[1] += fold(jnp.where(seg == 1, grad, 0.0))
+
+    send_in = []
+    for n, stage in enumerate((first_own, normed_one)):
+        settle(stage, n * half)
+        send_in.append(
+            pltpu.make_async_copy(stage, k.grad_in.at[pl.ds(n * half, half), :], k.local.at[3 + n])
+        )
+        send_in[n].start()
 
     def row_of(x):
         return jnp.sum(x, axis=0, keepdims=True)
@@ -733,20 +1016,21 @@
     )
     pair_sums = Spread(place, "tp", [sums], k.part_tp, small_send, small_recv, 13)
     pair_sums.start()
-    reduces[2 + pairs].join()
+    sum_pairs[pairs - 1].join()
     pair_sums.wait()
     row = lax.broadcasted_iota(jnp.int32, sums.shape, 0)
     k.part_sum[...] = sums[...] + jnp.where(row < 8, k.part_tp[...], 0.0)
     sums_z = Spread(place, "z", [k.part_sum] * 3, k.part_z, small_send, small_recv, 14)
     sums_z.start()
-    for g in range(4, 2 + pairs):
-        reduces[g].cross()
+    for j in range(1, pairs - 1):
+        sum_pairs[j].cross()
     sums_z.wait()
     k.part_zsum[...] = k.part_sum[...] + k.part_z[0] + k.part_z[1] + k.part_z[2]
     sums_r = Spread(place, "r", [k.part_zsum] * 3, k.part_in, small_send, small_recv, 17)
     sums_r.start()
-    for g in range(1, 3):
-        reduces[g].finish()
+    descend.finish()
+    sum_up.finish()
+    sum_out.finish()
     sums_r.wait()
     k.all_sums[...] = (
         k.part_zsum[:16] + k.part_in[0, :16] + k.part_in[1, :16] + k.part_in[2, :16]
@@ -754,15 +1038,17 @@
     k.all_embed[0] = k.part_zsum[16:]
     for d in (1, 2, 3):
         k.all_embed[d] = k.part_in[d - 1, 16:]
-    reduces[2 + pairs].cross()
-    for g in range(3, 3 + pairs):
-        reduces[g].finish()
+    sum_pairs[pairs - 1].cross()
+    for one in sum_pairs:
+        one.finish()
     for one in (
-        gathers
-        + reduces
-        + [pair_sums, sums_z, sums_r]
+        gather_a, gather_b, gather_c, gather_d, climb, descend, sum_down, sum_up, sum_out,
+        *sum_pairs, pair_sums, sums_z, sums_r,
     ):
         one.drain()
+    send_out.wait()
+    for copy in send_in:
+        copy.wait()
     for copy in (swap_d, swap_e, swap_f, swap_g):
         copy.wait_send()
 
@@ -770,11 +1056,11 @@
 def call_layer(sub, operands):
     rows, width = operands["x"].shape
     half = rows // 2
-    heads = operands["w1"].shape[1]
-    hidden = operands["bup"].shape[1]
+    mine, heads = operands["wo"].shape
+    hidden = operands["bu"].shape[0]
     pairs = heads // PAIR
-    seqs = operands["feats"].shape[0]
-    mine = operands["w0"].shape[0]
+    seqs = 8 * sub
+    count = operands["v0"].shape[1]
     tall = seqs + 16
     columns = [hidden, hidden, heads] + [3 * PAIR] * pairs
     shape = jax.ShapeDtypeStruct
@@ -790,6 +1076,21 @@
     vm = pltpu.VMEM
     sem = pltpu.SemaphoreType.DMA
     scratch = dict(
+        rows_in=vm((rows, width), bf16),
+        cot_in=vm((half, width), bf16),
+        out_stage=vm((half, width), bf16),
+        w0=vm((mine, 3 * heads), bf16),
+        w1=vm((mine, heads), bf16),
+        w2=vm((mine, hidden), bf16),
+        w3=vm((mine, hidden), bf16),
+        bqkv=vm((1, 3 * heads), f32),
+        bup=vm((1, hidden), f32),
+        feats=vm((seqs, TE), f32),
+        given=vm((8, count), f32),
+        deep=vm((5, 4 * mine, hidden // 2), bf16),
+        deep_far=vm((mine, hidden // 2), bf16),
+        deep_near=vm((2, mine, hidden // 2), bf16),
+        local=sem((5,)),
         full0=vm((width, 3 * heads), bf16),
         full1=vm((width, heads), bf16),
         full2=vm((width, hidden), bf16),
@@ -833,10 +1134,10 @@
         keys_t=vm((PAIR, rows), bf16),
         query_t=vm((PAIR, rows), f32),
         grad_qkv=vm((rows, 3 * heads), bf16),
-        g_send=sem((4, 15)),
-        g_recv=sem((4, 15)),
-        r_send=sem((3 + pairs, 15)),
-        r_recv=sem((3 + pairs, 15)),
+        g_send=sem((5, 15)),
+        g_recv=sem((5, 15)),
+        r_send=sem((4 + pairs, 15)),
+        r_recv=sem((4 + pairs, 15)),
         small_send=sem((20,)),
         small_recv=sem((20,)),
         tp_send=sem((7,)),
@@ -844,18 +1145,18 @@
     )
     for g, wide in enumerate(columns):
         scratch["grad" + str(g)] = vm((width, wide), bf16)
-        scratch["near" + str(g)] = vm((4, mine, wide), bf16)
-        scratch["ring" + str(g)] = vm((8, mine, wide), bf16)
-        scratch["high" + str(g)] = vm((3, mine, wide), bf16)
+        part = wide // 2 if g == 0 else wide
+        scratch["near" + str(g)] = vm((4, mine, part), bf16)
+        scratch["ring" + str(g)] = vm((8, mine, part), bf16)
+        scratch["high" + str(g)] = vm((3, mine, part), bf16)
     names = [*operands, *results, *scratch]
-    in_specs = [
-        pl.BlockSpec(memory_space=pltpu.SMEM if n == "lengths" else pltpu.VMEM) for n in operands
-    ]
+    spaces = dict(lengths=pltpu.SMEM, steps=pltpu.SMEM, x=pl.ANY, cot=pl.ANY, out=pl.ANY, grad_in=pl.ANY)
+    spec = lambda n: pl.BlockSpec(memory_space=spaces.get(n, pltpu.VMEM))
     got = pl.pallas_call(
         functools.partial(layer_kernel, sub, names),
         out_shape=list(results.values()),
-        in_specs=in_specs,
-        out_specs=vmem(len(results)),
+        in_specs=[spec(n) for n in operands],
+        out_specs=[spec(n) for n in results],
         scratch_shapes=list(scratch.values()),
         compiler_params=pltpu.CompilerParams(
             collective_id=0, has_side_effects=True, vmem_limit_bytes=63_000 * 1024
@@ -865,35 +1166,99 @@
     return types.SimpleNamespace(**dict(zip(results, got, strict=True)))
 
 
-def vmem(count):
-    return [pl.BlockSpec(memory_space=pltpu.VMEM)] * count
-
-
-def time_features(time_steps, feature_width):
-    half_width = feature_width // 2
-    frequency = jnp.exp(-math.log(10000.0) * jnp.arange(half_width, dtype=f32) / half_width)
-    angles = time_steps.astype(f32)[:, None] * frequency[None, :]
-    return jnp.concatenate([jnp.cos(angles), jnp.sin(angles)], axis=1)
-
-
-def contract_rows(left_side, right_side, precision_mode=None):
-    return lax.dot_general(
-        left_side,
-        right_side,
-        (((0,), (0,)), ((), ())),
-        precision=precision_mode,
-        preferred_element_type=jnp.float32,
+def finish_kernel(dp_size, names, *refs):
+    k = types.SimpleNamespace(**dict(zip(names, refs, strict=True)))
+    moves = [
+        pltpu.make_async_copy(k.out_from, k.out, k.local.at[0]),
+        pltpu.make_async_copy(k.grad_from, k.grad_in, k.local.at[1]),
+    ]
+    for move in moves:
+        move.start()
+    feats, embeds = k.feats[...], k.embeds[...]
+    before = mul_t(feats.astype(bf16), k.tw1t[...].astype(bf16)) + k.tb1[...]
+    gate = jax.nn.sigmoid(before)
+    hidden = (before * gate).astype(bf16).astype(f32)
+    grad_hidden = exact(embeds, k.tw2[...].astype(bf16).astype(f32), 1, 1)
+    grad_before = grad_hidden * (gate * (1.0 + before * (1.0 - gate)))
+    k.g_tw2[...] = exact(hidden, embeds, 0, 0)
+    k.g_tw1t[...] = exact(grad_before, feats, 0, 0)
+    k.g_tb1[...] = jnp.sum(grad_before, axis=0, keepdims=True)
+    sums = k.sums[...]
+    width = sums.shape[1]
+    row = lax.broadcasted_iota(jnp.int32, (8, 1), 0)
+    vectors = jnp.where(row == 6, jnp.sum(embeds, axis=0, keepdims=True), sums[:8])
+    count = k.tb1.shape[1]
+    start = (lax.axis_index("dp") * lax.axis_size("tp") + lax.axis_index("tp")) * count
+    entry = lax.broadcasted_iota(jnp.int32, (count, width), 0)
+    column = lax.broadcasted_iota(jnp.int32, (count, width), 1)
+    picked = exact(vectors, jnp.where(column == start + entry, 1.0, 0.0), 1, 1)
+    for n, dest in enumerate((k.g_bout, k.g_g1, k.g_s1, k.g_bdown, k.g_g2, k.g_s2, k.g_tb2)):
+        dest[...] = picked[n : n + 1, :]
+    hidden_width = k.g_bup.shape[0]
+    for n in range(hidden_width // width):
+        k.g_bup[n * width : (n + 1) * width] = sums[8 + n, :]
+    at = 8 + hidden_width // width
+    pairs = k.g_bq.shape[0] // PAIR
+    for j in range(pairs):
+        here = slice(j * PAIR, (j + 1) * PAIR)
+        source = many(k, "pair", j)
+        for n, dest in enumerate((k.g_wq, k.g_wk, k.g_wv)):
+            dest[:, here] = source[:, n * PAIR : (n + 1) * PAIR]
+        for n, dest in ((0, k.g_bq), (2, k.g_bv)):
+            first = (3 * j + n) * PAIR
+            dest[here] = sums[at + first // width, first % width : first % width + PAIR]
+    k.g_wo[...] = k.sum_out[...]
+    k.g_wu[...] = k.sum_up[...]
+    k.g_wd[...] = k.sum_down[...]
+    for move in moves:
+        move.wait()
+
+
+def call_finish(dp_size, operands, hidden):
+    shape = jax.ShapeDtypeStruct
+    own = operands["tb1"].shape[1]
+    width = operands["sums"].shape[1]
+    mine, heads = operands["sum_out"].shape
+    line = shape((1, own), f32)
+    matrix = shape((mine, heads), f32)
+    wide = shape((mine, hidden), f32)
+    results = dict(
+        out=shape(operands["out_from"].shape, bf16),
+        grad_in=shape(operands["grad_from"].shape, f32),
+        g_tw1t=shape((own, TE), f32),
+        g_tb1=line,
+        g_tw2=shape((own, width), f32),
+        g_tb2=line,
+        g_wq=matrix,
+        g_bq=shape((heads,), f32),
+        g_wk=matrix,
+        g_wv=matrix,
+        g_bv=shape((heads,), f32),
+        g_wo=matrix,
+        g_bout=line,
+        g_g1=line,
+        g_s1=line,
+        g_wu=wide,
+        g_bup=shape((hidden,), f32),
+        g_wd=wide,
+        g_bdown=line,
+        g_g2=line,
+        g_s2=line,
     )
-
-
-def contract_cols(left_side, right_side, precision_mode=None):
-    return lax.dot_general(
-        left_side,
-        right_side,
-        (((1,), (1,)), ((), ())),
-        precision=precision_mode,
-        preferred_element_type=jnp.float32,
-    )
+    scratch = dict(local=pltpu.SemaphoreType.DMA((2,)))
+    names = [*operands, *results, *scratch]
+    spaces = dict(out_from=pl.ANY, grad_from=pl.ANY, out=pl.ANY, grad_in=pl.ANY)
+    spec = lambda n: pl.BlockSpec(memory_space=spaces.get(n, pltpu.VMEM))
+    got = pl.pallas_call(
+        functools.partial(finish_kernel, dp_size, names),
+        out_shape=list(results.values()),
+        in_specs=[spec(n) for n in operands],
+        out_specs=[spec(n) for n in results],
+        scratch_shapes=list(scratch.values()),
+        compiler_params=pltpu.CompilerParams(vmem_limit_bytes=61_000 * 1024),
+        name="finish",
+    )(*operands.values())
+    return types.SimpleNamespace(**dict(zip(results, got, strict=True)))
 
 
 def on_device(
@@ -904,111 +1269,94 @@
     dp = lax.axis_size("dp")
     sub = dp // SUPER
     low = [[q * sub + l for l in range(sub)] for q in range(SUPER)]
-    dp_index = lax.axis_index("dp")
-    tp_index = lax.axis_index("tp")
-    seq_rows, width = inputs.shape
     head_width = w_query.shape[1]
 
-    def near_gather(value, axis):
+    def near(value, axis=0):
         if sub == 1:
             return value
         return lax.all_gather(value, "dp", axis=axis, tiled=True, axis_index_groups=low)
 
-    def near_sum(value):
-        if sub == 1:
-            return value
-        return lax.psum(value, "dp", axis_index_groups=low)
-
-    def near_scatter(value):
-        if sub == 1:
-            return value
-        return lax.psum_scatter(
-            value, "dp", scatter_dimension=0, tiled=True, axis_index_groups=low
-        )
-
-    z = dp_index // (4 * sub)
-    pair_row = (z * sub + dp_index % sub) * 2
-    seqs = 8 * sub
-    features = time_features(timesteps[0], TE).astype(bf16)
-    placed_feats = lax.dynamic_update_slice(
-        jnp.zeros((seqs, TE), f32), features.astype(f32), (pair_row, 0)
+    def line(value):
+        return near(value)[None, :]
+
+    steps = timesteps
+    if sub > 1:
+        steps = near(timesteps.astype(f32)).astype(jnp.int32).reshape(1, -1)
+    got = call_layer(
+        sub,
+        dict(
+            lengths=seq_lengths,
+            steps=steps,
+            x=inputs,
+            cot=cotangent,
+            wq=near(w_query),
+            wk=near(w_key),
+            wv=near(w_value),
+            wo=near(w_out.T),
+            wu=near(w_up),
+            wd=near(w_down.T),
+            bq=b_query,
+            bv=b_value,
+            bu=b_up,
+            tw1t=near(time_w1.T),
+            tb1=line(time_b1),
+            tw2=near(time_w2),
+            v0=line(time_b2),
+            v1=line(b_out),
+            v2=line(norm1_gain),
+            v3=line(norm1_bias),
+            v4=line(b_down),
+            v5=line(norm2_gain),
+            v6=line(norm2_bias),
+        ),
     )
-    own_slice = width // (dp * lax.axis_size("tp"))
-    slice_start = (dp_index * lax.axis_size("tp") + tp_index) * own_slice
-    stacked = jnp.stack(
-        [time_b2, b_out, norm1_gain, norm1_bias, b_down, norm2_gain, norm2_bias, jnp.zeros_like(b_out)]
+    sums, embeds, feats = got.all_sums, got.all_embed, got.all_feats
+    pairs = head_width // PAIR
+    totals = [many(got, "total", g) for g in range(3 + pairs)]
+    if sub > 1:
+        sums, embeds = lax.psum((sums, embeds), "dp", axis_index_groups=low)
+        totals = [
+            lax.psum_scatter(one, "dp", scatter_dimension=0, tiled=True, axis_index_groups=low)
+            for one in totals
+        ]
+    operands = dict(
+        out_from=got.out,
+        grad_from=got.grad_in,
+        sums=sums,
+        embeds=embeds.reshape(-1, embeds.shape[-1]),
+        feats=feats.reshape(-1, TE),
+        tw1t=time_w1.T,
+        tb1=time_b1[None, :],
+        tw2=time_w2,
+        sum_down=totals[0],
+        sum_up=totals[1],
+        sum_out=totals[2],
     )
-    vectors = lax.dynamic_update_slice(jnp.zeros((8, width), f32), stacked, (0, slice_start))
-    pairs = head_width // PAIR
-    hidden_width = b_up.shape[0]
-
-    def by_pairs(parts):
-        cut = [part.reshape(-1, pairs, 1, PAIR) for part in parts]
-        return jnp.concatenate(cut, axis=2).reshape(-1, 3 * head_width)
-
-    operands = dict(
-        lengths=seq_lengths,
-        x=inputs,
-        cot=cotangent,
-        w0=near_gather(by_pairs([w_query, w_key, w_value]).astype(bf16), 0),
-        w1=near_gather(w_out.T.astype(bf16), 0),
-        w2=near_gather(w_up.astype(bf16), 0),
-        w3=near_gather(w_down.T.astype(bf16), 0),
-        bqkv=by_pairs([b_query, jnp.zeros_like(b_query), b_value]),
-        bup=b_up[None, :],
-        feats=near_sum(placed_feats),
-        vectors=near_sum(vectors),
-        tw1=near_gather(time_w1, 1),
-        tb1=near_gather(time_b1, 0)[None, :],
-        tw2=near_gather(time_w2, 0),
-    )
-    got = call_layer(sub, operands)
-    all_feats = got.all_feats
-    all_sums, all_embed = near_sum((got.all_sums, got.all_embed))
-    red_down, red_up, red_out = [near_scatter(many(got, "total", g)) for g in range(3)]
-    red_pairs = [near_scatter(many(got, "total", 3 + j)) for j in range(pairs)]
-
-    def of_pairs(part):
-        return jnp.concatenate([one[:, part * PAIR : (part + 1) * PAIR] for one in red_pairs], axis=1)
-
-    own_vectors = lax.dynamic_slice(all_sums, (0, slice_start), (8, own_slice))
-    tp_vectors = all_sums[8:16].reshape(-1)
-    qkv_sums = tp_vectors[hidden_width : hidden_width + 3 * head_width].reshape(pairs, 3, PAIR)
-    every_feat = all_feats.reshape(-1, TE)
-    every_embed = all_embed.reshape(-1, width)
-    time_pre = (
-        jnp.dot(every_feat.astype(bf16), time_w1.astype(bf16), preferred_element_type=f32) + time_b1
-    )
-    silu_value, silu_pull = jax.vjp(jax.nn.silu, time_pre)
-    time_hidden = silu_value.astype(bf16).astype(f32)
-    red_tw2 = contract_rows(time_hidden, every_embed, highest)
-    grad_hidden = contract_cols(every_embed, time_w2.astype(bf16).astype(f32), highest)
-    grad_time_pre = silu_pull(grad_hidden)[0]
-    red_tb1 = jnp.sum(grad_time_pre, axis=0)
-    red_tw1 = contract_rows(every_feat, grad_time_pre, highest)
-    red_tb2 = lax.dynamic_slice(jnp.sum(every_embed, axis=0), (slice_start,), (own_slice,))
+    for j in range(pairs):
+        operands["pair" + str(j)] = totals[3 + j]
+    done = call_finish(dp, operands, b_up.shape[0])
     return (
-        got.out,
-        got.grad_in,
-        red_tw1,
-        red_tb1,
-        red_tw2,
-        red_tb2,
-        of_pairs(0),
-        qkv_sums[:, 0].reshape(-1),
-        of_pairs(1),
-        of_pairs(2),
-        qkv_sums[:, 2].reshape(-1),
-        red_out.T,
-        own_vectors[0],
-        own_vectors[1],
-        own_vectors[2],
-        red_up,
-        tp_vectors[:hidden_width],
-        red_down.T,
-        own_vectors[3],
-        own_vectors[4],
-        own_vectors[5],
+        done.out,
+        done.grad_in,
+        done.g_tw1t.T,
+        done.g_tb1[0],
+        done.g_tw2,
+        done.g_tb2[0],
+        done.g_wq,
+        done.g_bq,
+        done.g_wk,
+        done.g_wv,
+        done.g_bv,
+        done.g_wo.T,
+        done.g_bout[0],
+        done.g_g1[0],
+        done.g_s1[0],
+        done.g_wu,
+        done.g_bup,
+        done.g_wd.T,
+        done.g_bdown[0],
+        done.g_g2[0],
+        done.g_s2[0],
     )
 
 

time: 228 us -> 298 us (1.31)
  Pallas kernels: 190 us -> 297 us
  local copies, waits for them, and re-layouts: 18.7 us -> 0 us
  other arithmetic: 11.5 us -> 0 us
  matrix products: 5.72 us -> 0 us
    pallas_call x0 -> x1, Pallas kernels: none -> 123 us  [call_finish(): pl.pallas_call(functools.partial(finish_kernel, dp_size, names), out_shap...]
    pallas_call x1, Pallas kernels: 190 us -> 175 us  [call_layer(): pl.pallas_call(functools.partial(layer_kernel, sub, names), out_shape=lis...]
    unnamed x24 -> x0, local copies, waits for them, and re-layouts: 7.27 us -> none
    dot_general x4 -> x0, matrix products: 5.72 us -> none  [the longest x2 3.17 us: contract_rows(): lax.dot_general(left_side, right_side, (((0,), (0,)), ((), ())), precisio...]
    convert_element_type x4 -> x0, other arithmetic: 5.46 us -> none  [the longest x1 1.64 us: on_device(): w_up.astype(bf16)]
    slice x7 -> x0, local copies, waits for them, and re-layouts: 4.32 us -> none  [the longest x2 1.61 us: of_pairs(): one[:, part * PAIR:(part + 1) * PAIR]]
where the time goes in v3:
time: 298 us
  Pallas kernels  297 us (100%)
    pallas_call x1, Pallas kernels, call_layer(): pl.pallas_call(functools.partial(layer_kernel, sub, names), out_shape=lis...  175 us
    pallas_call x1, Pallas kernels, call_finish(): pl.pallas_call(functools.partial(finish_kernel, dp_size, names), out_shap...  123 us

profile of v3, /device:TPU:0, one launch (start us, length us, event | category | flops | bytes accessed | tf_op | source)
XLA Modules:
  0.0 298.0 jit_solution(12837646843659487138)
XLA Ops:
  0.7 174.6 %layer.1 = (bf16[512,768]{1,0:T(8,128)(2,1)}, f32[1024,768]{1,0:T(8,128)}, f32[4,8,128]{2,1,0:T(8,128)}, f32[16,768]{1,0:T(8,128)}, f32[4,8,768]{2,1,0:T(8,128)}...) custom-call(s32[1,2]{1,0:T(1,128)} %refs_0_.1, ...), custom_call_target="tpu_custom_call" | custom-call | tf_op jit(solution)/shard_map/layer/pallas_call | solution.py:1155
  175.3 122.6 %finish.1 = (bf16[512,768]{1,0:T(8,128)(2,1)}, f32[1024,768]{1,0:T(8,128)}, f32[24,128]{1,0:T(8,128)}, f32[1,24]{1,0:T(1,128)}, f32[24,768]{1,0:T(8,128)}, /*ind...) custom-call(bf16[512,768]{1,0:T(8,128)(2,1)} %get-tuple-element.53.r, ...), custom_call_target="tpu_custom_call" | custom-call | tf_op jit(solution)/shard_map/finish/pallas_call | solution.py:1252

commit v4 on v3

--- a/solution.py
+++ b/solution.py
@@ -1168,17 +1168,23 @@
 
 def finish_kernel(dp_size, names, *refs):
     k = types.SimpleNamespace(**dict(zip(names, refs, strict=True)))
-    moves = [
-        pltpu.make_async_copy(k.out_from, k.out, k.local.at[0]),
-        pltpu.make_async_copy(k.grad_from, k.grad_in, k.local.at[1]),
-    ]
-    for move in moves:
-        move.start()
+    rows = k.grad_from.shape[0] // 4
+    moves = [(k.out_from, k.out_held, k.out)]
+    for n in range(4):
+        here = slice(n * rows, (n + 1) * rows)
+        moves.append((k.grad_from.at[here], k.grad_held.at[here], k.grad_in.at[here]))
+    fetch = [pltpu.make_async_copy(a, b, k.local.at[n]) for n, (a, b, _) in enumerate(moves)]
+    store = [pltpu.make_async_copy(b, c, k.local.at[5 + n]) for n, (_, b, c) in enumerate(moves)]
+    for copy in fetch:
+        copy.start()
     feats, embeds = k.feats[...], k.embeds[...]
     before = mul_t(feats.astype(bf16), k.tw1t[...].astype(bf16)) + k.tb1[...]
     gate = jax.nn.sigmoid(before)
     hidden = (before * gate).astype(bf16).astype(f32)
     grad_hidden = exact(embeds, k.tw2[...].astype(bf16).astype(f32), 1, 1)
+    for first, then in zip(fetch, store, strict=True):
+        first.wait()
+        then.start()
     grad_before = grad_hidden * (gate * (1.0 + before * (1.0 - gate)))
     k.g_tw2[...] = exact(hidden, embeds, 0, 0)
     k.g_tw1t[...] = exact(grad_before, feats, 0, 0)
@@ -1210,8 +1216,8 @@
     k.g_wo[...] = k.sum_out[...]
     k.g_wu[...] = k.sum_up[...]
     k.g_wd[...] = k.sum_down[...]
-    for move in moves:
-        move.wait()
+    for copy in store:
+        copy.wait()
 
 
 def call_finish(dp_size, operands, hidden):
@@ -1245,7 +1251,11 @@
         g_g2=line,
         g_s2=line,
     )
-    scratch = dict(local=pltpu.SemaphoreType.DMA((2,)))
+    scratch = dict(
+        out_held=pltpu.VMEM(operands["out_from"].shape, bf16),
+        grad_held=pltpu.VMEM(operands["grad_from"].shape, f32),
+        local=pltpu.SemaphoreType.DMA((10,)),
+    )
     names = [*operands, *results, *scratch]
     spaces = dict(out_from=pl.ANY, grad_from=pl.ANY, out=pl.ANY, grad_in=pl.ANY)
     spec = lambda n: pl.BlockSpec(memory_space=spaces.get(n, pltpu.VMEM))

time: 298 us -> 181 us (0.61)
  Pallas kernels: 297 us -> 180 us
    pallas_call x1, Pallas kernels: 123 us -> 5.46 us  [call_finish(): pl.pallas_call(functools.partial(finish_kernel, dp_size, names), out_shap...]
where the time goes in v4:
time: 181 us
  Pallas kernels  180 us (99%)
    pallas_call x1, Pallas kernels, call_layer(): pl.pallas_call(functools.partial(layer_kernel, sub, names), out_shape=lis...  175 us
    pallas_call x1, Pallas kernels, call_finish(): pl.pallas_call(functools.partial(finish_kernel, dp_size, names), out_shap...  5.46 us

profile of v4, /device:TPU:0, one launch (start us, length us, event | category | flops | bytes accessed | tf_op | source)
XLA Modules:
  0.0 181.0 jit_solution(15889778797169525081)
XLA Ops:
  0.7 174.6 %layer.1 = (bf16[512,768]{1,0:T(8,128)(2,1)}, f32[1024,768]{1,0:T(8,128)}, f32[4,8,128]{2,1,0:T(8,128)}, f32[16,768]{1,0:T(8,128)}, f32[4,8,768]{2,1,0:T(8,128)}...) custom-call(s32[1,2]{1,0:T(1,128)} %refs_0_.1, ...), custom_call_target="tpu_custom_call" | custom-call | tf_op jit(solution)/shard_map/layer/pallas_call | solution.py:1155
  175.3 5.5 %finish.1 = (bf16[512,768]{1,0:T(8,128)(2,1)}, f32[1024,768]{1,0:T(8,128)}, f32[24,128]{1,0:T(8,128)}, f32[1,24]{1,0:T(1,128)}, f32[24,768]{1,0:T(8,128)}, /*ind...) custom-call(bf16[512,768]{1,0:T(8,128)(2,1)} %get-tuple-element.53.r, ...), custom_call_target="tpu_custom_call" | custom-call | tf_op jit(solution)/shard_map/finish/pallas_call | solution.py:1262
